TPU v7x, 256 devices: a whole 4x4x8 slice. The times are simulated.
256 devices in a mesh: tok: 32 (over x_lo, z, core), voc: 8 (over y, x_hi).
Axes of the slice: x: 4 (x_hi: 2, x_lo: 2; x = x_hi * 2 + x_lo), y: 4, z: 8, core: 2. Of those that a mesh axis runs over, the one named last changes fastest.
Arguments:
- hidden: bfloat16 [4096, 1792], P('tok'), may hold values from -40 to 40
- head_weight: bfloat16 [1792, 131072], P(None, ('voc', 'tok')), may hold values from -0.37796447 to 0.37796447
- teacher_probs: bfloat16 [4096, 131072], P('tok', 'voc'), may hold values from 0 to 1, as said below
- teacher_row: int32 [4096], replicated, may hold values from 0 to 4095, each once
- lengths: int32 [32], replicated, may hold values from 1 to 128, as said below
Outputs:
- head_grad: bfloat16 [1792, 131072], P(None, ('voc', 'tok'))
Inputs may be any that keep to these rules, and one draw needn't show every extreme that they name: `teacher_row`: a permutation of the 4096 token positions. `lengths`: the last sequence is full. `teacher_probs`: each row is a probability distribution over the vocabulary: its entries sum to 1 up to rounding.
All inputs are finite; a program needn't handle non-finite values.
Results may differ from a plain program's by a relative error of at most 0.008.
Values may be sent and summed in bfloat16 or wider, within the bound.
No kernel may reach another device: no remote copies, remote signals or barrier semaphores. Data moves between devices by JAX's collectives and lax.ppermute only.
A program may use at most 128 MiB of HBM per device.

v0:
```python
import functools

import jax
import jax.numpy as jnp
from jax import lax
from jax.experimental import pallas as pl
from jax.experimental.pallas import tpu as pltpu
from jax.sharding import PartitionSpec as P

SEQ_LEN = 128
AXES = ("tok", "voc")

NX, NY, NZ = 4, 4, 8


loss_scale = 1048576.0


def linear(x, y, z, core):
    x, y, z = x % NX, y % NY, z % NZ
    return (((x % 2) * NZ + z) * 2 + core) * (NY * 2) + y * 2 + x // 2


def hop(array, dx=0, dy=0, dz=0, flip=0):
    pairs = [
        (linear(x, y, z, core), linear(x + dx, y + dy, z + dz, core ^ flip))
        for x in range(NX)
        for y in range(NY)
        for z in range(NZ)
        for core in range(2)
    ]
    return lax.ppermute(array, AXES, pairs)


def spread_over_z(hidden):
    rows = hidden.shape[0] // NY
    y = lax.axis_index("voc") // 2
    own = lax.dynamic_slice_in_dim(hidden, y * rows, rows, 0)
    up, down = [own], [own]
    for step in range(1, 4):
        up.append(hop(up[-1], dz=1))
        down.append(hop(down[-1], dz=-1))
    up.append(hop(up[-1], dz=1))
    return jnp.stack([*up, down[3], down[2], down[1]])


def cross(array, near):
    pairs = [
        (linear(x, y, z, core), linear(x + 1 if (x % 2 == 0) == near else x - 1, y, z, core))
        for x in range(NX)
        for y in range(NY)
        for z in range(NZ)
        for core in range(2)
    ]
    return lax.ppermute(array, AXES, pairs)


def tie(*groups):
    return lax.optimization_barrier(groups)


def flip_all(arrays):
    return tuple(hop(array, flip=1) for array in arrays)


def gather_logits(place, here, weight):
    prev, cross_here = hop(here, dy=1), cross(here, near=False)
    next_a, next_b = hop(here[:4], dy=-1), hop(here[4:], dy=-1)

    prev, next_a, next_b, cross_here = tie(prev, next_a, next_b, cross_here)
    cross_prev, cross_next_a = cross(prev, near=False), cross(next_a, near=True)
    far_a, far_b = hop(prev[:4], dy=1), hop(next_b, dy=-1)
    here_flip, prev_flip, cross_here_flip = flip_all((here, prev, cross_here))

    cross_prev, cross_next_a, far_a, far_b, here_flip, prev_flip, cross_here_flip = tie(
        cross_prev, cross_next_a, far_a, far_b, here_flip, prev_flip, cross_here_flip
    )
    cross_far_a, cross_far_b = cross(far_a, near=False), cross(far_b, near=False)
    cross_next_b = cross(next_b, near=True)
    own = (prev, here, next_a, next_b, far_a, far_b)
    own_flip = (prev_flip, here_flip) + flip_all(own[2:])
    done = block_logits(place, own, own_flip, weight, 0, None)

    done, rest = tie(done, (cross_prev, cross_next_a, cross_next_b, cross_far_a, cross_far_b))
    rest_flip = flip_all(rest)
    crossed = (rest[0], cross_here) + rest[1:]
    crossed_flip = (rest_flip[0], cross_here_flip) + rest_flip[1:]
    return block_logits(place, crossed, crossed_flip, weight, 1, done)


def coords():
    tok, voc = lax.axis_index("tok"), lax.axis_index("voc")
    return jnp.stack([tok // (2 * NZ), lax.rem(tok // 2, NZ), lax.rem(tok, 2), voc // 2]).astype(jnp.int32)


def token_block(place, column, k):
    x_lo = jnp.where(column == 0, place[0], 1 - place[0])
    return x_lo * NZ + lax.rem(place[1] + NZ - k, NZ)


def to_local(values, place):
    order = jnp.stack([token_block(place, column, k) for column in range(2) for k in range(NZ)])
    return values.reshape(2 * NZ, -1)[order].reshape(-1)


def from_local(values, place):
    order = jnp.stack([token_block(place, x_lo, z) for x_lo in range(2) for z in range(NZ)])
    return values.reshape(2 * NZ, -1)[order].reshape(-1)


PIECES = ((-1, 0), (0, 0), (1, 0), (1, 4), (2, 0), (2, 4))


def logits_kernel(column, place, *refs):
    count = 2 * len(PIECES)
    pieces = refs[:count]
    weight, peak_before, total_before = refs[count : count + 3]
    hidden, logits, peak, total, slots, load_sem, store_sem = refs[-7:]
    rows = pieces[0].shape[1]
    step, steps = pl.program_id(0), pl.num_programs(0)

    @pl.when(step == 0)
    def _():
        for group in range(2):
            for i, piece in enumerate(pieces):
                turn, first = PIECES[i % len(PIECES)]
                if first <= 4 * group < first + piece.shape[0]:
                    core = place[2] if i < len(PIECES) else 1 - place[2]
                    start = core * (rows * NY) + lax.rem(place[3] + turn + NY, NY) * rows
                    to = slots.at[group, :, pl.ds(pl.multiple_of(start, rows), rows)]
                    source = piece.at[pl.ds(4 * group - first, 4)]
                    pltpu.make_async_copy(source, to, load_sem.at[group]).start()
        peak[...] = peak_before[...]
        total[...] = total_before[...]

    def store(group):
        return pltpu.make_async_copy(slots.at[group], hidden.at[2 * column + group], store_sem.at[group])

    pltpu.make_async_copy(slots.at[step], slots.at[step], load_sem.at[step]).wait()
    store(step).start()
    tokens = slots[step].reshape(logits.shape[0], slots.shape[-1])
    values = jnp.dot(tokens, weight[...], preferred_element_type=jnp.float32)
    logits[...] = values
    row_peak = jnp.max(values, axis=1, keepdims=True)
    row_total = jnp.sum(jnp.exp(values - row_peak), axis=1, keepdims=True)
    wide = (values.shape[0], 128)
    for out, stat in ((peak, row_peak), (total, row_total)):
        line = jnp.broadcast_to(stat, wide).T[:1]
        width = out.shape[-1]
        for part in range(4):
            out[token_block(place, column, step * 4 + part)] = line[:, part * width : (part + 1) * width]

    @pl.when(step + 1 == steps)
    def _():
        for group in range(2):
            store(group).wait()


def block_logits(place, mine, others, weight, column, before):
    pieces = [*mine, *others]
    rows, depth = pieces[0].shape[1:]
    width = weight.shape[1]
    block = 2 * NY * rows
    blocks = 2 * NZ
    stat = jax.ShapeDtypeStruct((blocks, 1, block), jnp.float32)
    stat_spec = pl.BlockSpec((blocks, 1, block), lambda step, place: (0, 0, 0))
    any_spec = pl.BlockSpec(memory_space=pl.ANY)
    if before is None:
        extra = [jnp.zeros(stat.shape, stat.dtype)] * 2
        aliases = {}
    else:
        extra = [before[2], before[3], before[0], before[1]]
        aliases = {len(pieces) + 4: 0, len(pieces) + 5: 1}
    return pl.pallas_call(
        functools.partial(logits_kernel, column),
        grid_spec=pltpu.PrefetchScalarGridSpec(
            num_scalar_prefetch=1,
            grid=(2,),
            in_specs=[any_spec] * len(pieces)
            + [pl.BlockSpec((depth, width), lambda *_: (0, 0)), stat_spec, stat_spec]
            + [any_spec] * (len(extra) - 2),
            out_specs=[
                any_spec,
                pl.BlockSpec((4 * block, width), lambda step, place: (2 * column + step, 0)),
                stat_spec,
                stat_spec,
            ],
            scratch_shapes=[
                pltpu.VMEM((2, 4, block, depth), jnp.bfloat16),
                pltpu.SemaphoreType.DMA((2,)),
                pltpu.SemaphoreType.DMA((2,)),
            ],
        ),
        out_shape=[
            jax.ShapeDtypeStruct((4, 4, block, depth), jnp.bfloat16),
            jax.ShapeDtypeStruct((blocks * block, width), jnp.float32),
            stat,
            stat,
        ],
        input_output_aliases=aliases,
        compiler_params=pltpu.CompilerParams(vmem_limit_bytes=56 * 1024 * 1024),
        cost_estimate=pl.CostEstimate(
            flops=blocks * block * depth * width,
            transcendentals=blocks * block * width // 2,
            bytes_accessed=blocks * block * (2 * depth + 2 * width) + 2 * depth * width,
        ),
    )(place, *pieces, weight, *extra)


def rows_kernel(chosen, teacher, aligned, narrow, wide, sem):
    step = pl.program_id(0)
    count = aligned.shape[0]
    parts = sem.shape[0]
    part = narrow.shape[0] // parts

    @pl.when(step == 0)
    def _():
        def load(i):
            span = pl.ds(i * part, part)
            return pltpu.make_async_copy(teacher.at[span], narrow.at[span], sem.at[i])

        for i in range(parts):
            load(i).start()
        for i in range(parts):
            load(i).wait()
            wide[pl.ds(i * part, part), :] = narrow[pl.ds(i * part, part), :].astype(jnp.float32)

    @pl.loop(0, count // 16, unroll=4)
    def _(group):
        first = step * count + group * 16
        picked = [wide[pl.ds(chosen[first + i], 1), :] for i in range(16)]
        rows = jnp.concatenate(picked, axis=0).astype(jnp.bfloat16)
        aligned[pl.ds(pl.multiple_of(group * 16, 16), 16), :] = rows


def take_rows(teacher, chosen):
    rows, width = teacher.shape
    count = rows // 4
    return pl.pallas_call(
        rows_kernel,
        grid_spec=pltpu.PrefetchScalarGridSpec(
            num_scalar_prefetch=1,
            grid=(4,),
            in_specs=[pl.BlockSpec(memory_space=pl.ANY)],
            out_specs=pl.BlockSpec((count, width), lambda step, chosen: (step, 0)),
            scratch_shapes=[
                pltpu.VMEM((rows, width), jnp.bfloat16),
                pltpu.VMEM((rows, width), jnp.float32),
                pltpu.SemaphoreType.DMA((8,)),
            ],
        ),
        out_shape=jax.ShapeDtypeStruct((rows, width), jnp.bfloat16),
        compiler_params=pltpu.CompilerParams(vmem_limit_bytes=56 * 1024 * 1024),
        cost_estimate=pl.CostEstimate(flops=0, transcendentals=0, bytes_accessed=10 * rows * width * 2),
    )(chosen, teacher)


def members(key):
    groups = {}
    for tok in range(2 * NZ * 2):
        for voc in range(NY * 2):
            groups.setdefault(key(tok // (2 * NZ), tok // 2 % NZ, tok % 2, voc), []).append(tok * NY * 2 + voc)
    return list(groups.values())


def from_members(values, groups):
    copies = jnp.broadcast_to(values[None], (len(groups[0]),) + values.shape)
    return lax.all_to_all(copies, AXES, split_axis=0, concat_axis=0, tiled=True, axis_index_groups=groups)


def merge_totals(peaks, totals):
    peak = jnp.max(peaks, axis=0)
    return jnp.stack([peak, jnp.sum(totals * jnp.exp(peaks - peak[None]), axis=0)])


def merge_two(mine, theirs):
    both = jnp.stack([mine, theirs])
    return merge_totals(both[:, 0], both[:, 1])


def merge_over_plane(stats, teacher):
    stats = merge_two(stats, hop(stats, flip=1))
    stats = merge_two(stats, cross(stats, near=True))
    stats = merge_two(stats, hop(stats, dx=2))
    stats = merge_two(stats, turn_pair(stats))
    stats, teacher = tie(stats, teacher)
    return merge_two(stats, hop(stats, dy=2)), teacher


def turn_pair(array):
    pairs = [
        (linear(x, y, z, core), linear(x, y ^ 1, z, core))
        for x in range(NX)
        for y in range(NY)
        for z in range(NZ)
        for core in range(2)
    ]
    return lax.ppermute(array, AXES, pairs)


def make_per_device(tok, voc):
    def per_device(hidden, head_weight, teacher_probs, teacher_row, lengths):
        rows_all = hidden.shape[0] * tok
        here = spread_over_z(hidden)
        by_owner = teacher_probs.reshape(teacher_probs.shape[0], tok, -1).transpose(1, 0, 2)
        here, by_owner = tie(here, by_owner)
        teacher = lax.all_to_all(by_owner, "tok", split_axis=0, concat_axis=0, tiled=True)
        place = coords()
        gathered, logits, local_peak, local_total = gather_logits(place, here, head_weight)
        gathered = gathered.reshape(rows_all, -1)
        along_z = members(lambda x_lo, z, core, voc: (x_lo, core, voc))
        in_plane = members(lambda x_lo, z, core, voc: (z, core))
        stats = jnp.stack([local_peak.reshape(-1), local_total.reshape(-1)])
        stats, teacher = merge_over_plane(stats, teacher)
        aligned = take_rows(teacher.reshape(rows_all, -1), to_local(teacher_row, place))
        aligned = aligned.astype(jnp.float32)
        stats = from_members(stats, along_z)
        row_peak, row_total = merge_totals(stats[:, 0], stats[:, 1])
        row_peak, row_total = to_local(row_peak, place), to_local(row_total, place)
        log_student = logits - row_peak[:, None] - jnp.log(row_total)[:, None]
        student = jnp.exp(log_student)
        log_mix = jnp.log(0.5 * aligned + 0.5 * student)
        grad_prob = 0.5 * (log_student - log_mix)
        local_centre = jnp.sum(student * grad_prob, axis=1)
        centre = from_local(local_centre, place)
        centre = centre + hop(centre, flip=1)
        centre = jnp.sum(from_members(centre, along_z), axis=0)
        centre = to_local(jnp.sum(from_members(centre, in_plane), axis=0), place)
        positions = jnp.arange(SEQ_LEN, dtype=jnp.int32)
        valid_mask = (positions[None, :] < lengths[:, None]).astype(jnp.float32).reshape(-1)
        valid_mask = to_local(valid_mask, place)
        token_count = jnp.sum(lengths).astype(jnp.float32)
        grad_scale = loss_scale / token_count
        dlogits = ((grad_scale * valid_mask)[:, None] * student * (grad_prob - centre[:, None])).astype(
            jnp.bfloat16
        )
        head_grad = lax.dot_general(
            gathered, dlogits, (((0,), (0,)), ((), ())), preferred_element_type=jnp.float32
        )
        return head_grad.astype(jnp.bfloat16)

    return per_device


def solution(mesh):
    return jax.shard_map(
        make_per_device(mesh.shape["tok"], mesh.shape["voc"]),
        mesh=mesh,
        in_specs=(P("tok", None), P(None, ("voc", "tok")), P("tok", "voc"), P(), P()),
        out_specs=P(None, ("voc", "tok")),
        check_vma=False,
    )
```

profile of v0, /device:TPU:1, one launch (start us, length us, event | category | flops | bytes accessed | tf_op | source)
XLA Modules:
  0.0 236.9 jit_solution(693233452676620940)
XLA Ops:
  0.0 0.9 bitcast_dynamic-update-slice_fusion.7
  0.9 2.5 %collective-permute-start = (bf16[32,1792]{1,0:T(8,128)(2,1)S(1)}, bf16[32,1792]{1,0:T(8,128)(2,1)S(1)}, u32[]{:S(2)}, u32[]{:S(2)}) collective-permute-start(bf16[32,1792]{1,0:T(8,128)(2,1)S(1)} %get-tuple-element.80), channel_id=1, source_target_pairs={{0,16},{8,24},{16,32},{24,40},{32,48},{40,56},{48,64},{56,72},{64,... | collective-permute-start | bytes 344072 | tf_op jit(solution)/shard_map/ppermute | solution.py:32
  3.5 4.0 %collective-permute-start.4 = (bf16[32,1792]{1,0:T(8,128)(2,1)S(1)}, bf16[32,1792]{1,0:T(8,128)(2,1)S(1)}, u32[]{:S(2)}, u32[]{:S(2)}) collective-permute-start(bf16[32,1792]{1,0:T(8,128)(2,1)S(1)} %get-tuple-element.80), channel_id=1, source_target_pairs={{0,112},{8,120},{16,0},{24,8},{32,16},{40,24},{48,32},{56,40},{64,... | collective-permute-start | bytes 344072 | tf_op jit(solution)/shard_map/ppermute | solution.py:32
  7.5 4.8 %copy.79 = bf16[16,32,8,512]{3,2,0,1:T(8,128)(2,1)} copy(bf16[16,32,8,512]{3,2,1,0:T(8,128)(2,1)} %bitcast.167) | data formatting | bytes 8388608 | tf_op jit(solution)/shard_map/reshape | solution.py:305
  12.3 2.7 %collective-permute-start.5 = (bf16[32,1792]{1,0:T(8,128)(2,1)S(1)}, bf16[32,1792]{1,0:T(8,128)(2,1)S(1)}, u32[]{:S(2)}, u32[]{:S(2)}) collective-permute-start(bf16[32,1792]{1,0:T(8,128)(2,1)S(1)} %collective-permute-done.4), channel_id=1, source_target_pairs={{0,112},{8,120},{16,0},{24,8},{32,16},{40,24},{48,32},{56,40},{64,... | collective-permute-start | bytes 344072 | tf_op jit(solution)/shard_map/ppermute | solution.py:32
  15.1 2.1 collective-permute-done.1
  17.2 2.7 %collective-permute-start.6 = (bf16[32,1792]{1,0:T(8,128)(2,1)S(1)}, bf16[32,1792]{1,0:T(8,128)(2,1)S(1)}, u32[]{:S(2)}, u32[]{:S(2)}) collective-permute-start(bf16[32,1792]{1,0:T(8,128)(2,1)S(1)} %collective-permute-done.5), channel_id=1, source_target_pairs={{0,112},{8,120},{16,0},{24,8},{32,16},{40,24},{48,32},{56,40},{64,... | collective-permute-start | bytes 344072 | tf_op jit(solution)/shard_map/ppermute | solution.py:32
  19.9 2.1 collective-permute-done.2
  22.0 4.8 %collective-permute-done.3 = bf16[32,1792]{1,0:T(8,128)(2,1)S(1)} collective-permute-done((bf16[32,1792]{1,0:T(8,128)(2,1)S(1)}, bf16[32,1792]{1,0:T(8,128)(2,1)S(1)}, u32[]{:S(2)}, u32[]{:S(2)}) %collective-permute-start.3) | collective-permute-done | bytes 114720 | tf_op jit(solution)/shard_map/ppermute | solution.py:32
  26.9 11.3 %all-to-all-start = ((bf16[32,128,512]{2,1,0:T(8,128)(2,1)}), bf16[32,128,512]{2,1,0:T(8,128)(2,1)}, u32[]{:S(2)}, u32[]{:S(2)}) async-start(bf16[32,128,512]{2,1,0:T(8,128)(2,1)} %bitcast.165), calls=%async_computation | async-start | bytes 8388608 | tf_op jit(solution)/shard_map/all_to_all | solution.py:307
  38.3 2.7 %collective-permute-start.10 = (bf16[8,32,1792]{2,1,0:T(8,128)(2,1)S(1)}, bf16[8,32,1792]{2,1,0:T(8,128)(2,1)S(1)}, u32[]{:S(2)}, u32[]{:S(2)}) collective-permute-start(bf16[8,32,1792]{2,1,0:T(8,128)(2,1)S(1)} %bitcast_dynamic-update-slice_fusion.refs_1_), channel_id=1, source_target_pairs={{0,129},{8,137},{16,145},{24,153},{32,161},{40,169},{48,177},{56,1... | collective-permute-start | bytes 2752520 | tf_op jit(solution)/shard_map/ppermute | solution.py:55
  41.0 1.3 collective-permute-start.7
  42.4 1.5 collective-permute-start.8
  43.9 1.5 collective-permute-start.9
  45.4 1.5 collective-permute-start.15
  46.8 6.8 %collective-permute-done.8.refs_2_ = bf16[4,32,1792]{2,1,0:T(8,128)(2,1)} collective-permute-done((bf16[4,32,1792]{2,1,0:T(8,128)(2,1)S(1)}, bf16[4,32,1792]{2,1,0:T(8,128)(2,1)}, u32[]{:S(2)}, u32[]{:S(2)}) %collective-permute-start.8) | collective-permute-done | bytes 458784 | tf_op jit(solution)/shard_map/ppermute | solution.py:32
  53.7 9.8 %collective-permute-done.9.refs_3_ = bf16[4,32,1792]{2,1,0:T(8,128)(2,1)} collective-permute-done((bf16[4,32,1792]{2,1,0:T(8,128)(2,1)S(1)}, bf16[4,32,1792]{2,1,0:T(8,128)(2,1)}, u32[]{:S(2)}, u32[]{:S(2)}) %collective-permute-start.9) | collective-permute-done | bytes 458784 | tf_op jit(solution)/shard_map/ppermute | solution.py:32
  63.7 1.2 collective-permute-start.13
  65.3 2.1 collective-permute-start.16
  67.6 7.9 %collective-permute-done.13.refs_4_ = bf16[4,32,1792]{2,1,0:T(8,128)(2,1)} collective-permute-done((bf16[4,32,1792]{2,1,0:T(8,128)(2,1)S(1)}, bf16[4,32,1792]{2,1,0:T(8,128)(2,1)}, u32[]{:S(2)}, u32[]{:S(2)}) %collective-permute-start.13) | collective-permute-done | bytes 458784 | tf_op jit(solution)/shard_map/ppermute | solution.py:32
  75.5 1.2 collective-permute-start.14
  76.7 10.3 %collective-permute-done.12.refs_2_ = bf16[4,32,1792]{2,1,0:T(8,128)(2,1)S(1)} collective-permute-done((bf16[4,32,1792]{2,1,0:T(8,128)(2,1)}, bf16[4,32,1792]{2,1,0:T(8,128)(2,1)S(1)}, u32[]{:S(2)}, u32[]{:S(2)}) %collective-permute-start.12) | collective-permute-done | bytes 458784 | tf_op jit(solution)/shard_map/ppermute | solution.py:55
  87.0 1.8 collective-permute-start.18
  89.0 1.0 copy-done.3
  90.8 2.6 %collective-permute-start.23 = (bf16[4,32,1792]{2,1,0:T(8,128)(2,1)}, bf16[4,32,1792]{2,1,0:T(8,128)(2,1)S(1)}, u32[]{:S(2)}, u32[]{:S(2)}) collective-permute-start(bf16[4,32,1792]{2,1,0:T(8,128)(2,1)} %collective-permute-done.13.refs_4_), channel_id=1, source_target_pairs={{0,129},{8,137},{16,145},{24,153},{32,161},{40,169},{48,177},{56,1... | collective-permute-start | bytes 1376264 | tf_op jit(solution)/shard_map/ppermute | solution.py:55
  93.4 0.6 collective-permute-start.24
  94.0 0.6 pad_add_fusion.place
  94.6 0.6 broadcast_in_dim.8.refs_13_.refs_14_
  95.2 12.6 %shard_map.55 = (bf16[4,4,256,1792]{3,2,1,0:T(8,128)(2,1)}, f32[4096,512]{1,0:T(8,128)}, f32[16,1,256]{2,1,0:T(1,128)}, f32[16,1,256]{2,1,0:T(1,128)}) custom-call(s32[4]{0:T(128)} %pad_add_fusion.place, bf16[8,32,1792]{2,1,0:T(8,128)(2,1)} %copy-done.13, bf16[8,32,1792]{2,1,0:T(8,128)(2,1)} %copy-done, bf16[4,32,1792]{2,1,0:T(8,128)(2,1)} %collective-permute-done.8.refs_2_, ...), custom_call_target="tpu_custom_call" | custom-call | flops 3758096384 | bytes 20709376 | tf_op jit(solution)/shard_map/pallas_call | solution.py:174
  107.8 3.5 %collective-permute-done.22.refs_3_ = bf16[4,32,1792]{2,1,0:T(8,128)(2,1)S(1)} collective-permute-done((bf16[4,32,1792]{2,1,0:T(8,128)(2,1)}, bf16[4,32,1792]{2,1,0:T(8,128)(2,1)S(1)}, u32[]{:S(2)}, u32[]{:S(2)}) %collective-permute-start.22) | collective-permute-done | bytes 458784 | tf_op jit(solution)/shard_map/ppermute | solution.py:55
  111.2 2.4 %collective-permute-done.24.refs_5_ = bf16[4,32,1792]{2,1,0:T(8,128)(2,1)S(1)} collective-permute-done((bf16[4,32,1792]{2,1,0:T(8,128)(2,1)}, bf16[4,32,1792]{2,1,0:T(8,128)(2,1)S(1)}, u32[]{:S(2)}, u32[]{:S(2)}) %collective-permute-start.24) | collective-permute-done | bytes 458784 | tf_op jit(solution)/shard_map/ppermute | solution.py:55
  113.6 1.4 collective-permute-start.25
  116.0 1.7 collective-permute-done.26.refs_8_
  117.7 0.7 collective-permute-done.27.refs_9_
  118.4 0.7 collective-permute-done.28.refs_10_
  119.1 0.7 collective-permute-done.29.refs_11_
  119.8 0.7 copy-done.12
  120.5 0.9 copy-done.4
  121.4 12.6 %shard_map.56 = (bf16[4,4,256,1792]{3,2,1,0:T(8,128)(2,1)}, f32[4096,512]{1,0:T(8,128)}, f32[16,1,256]{2,1,0:T(1,128)}, f32[16,1,256]{2,1,0:T(1,128)}) custom-call(s32[4]{0:T(128)} %pad_add_fusion.place, bf16[8,32,1792]{2,1,0:T(8,128)(2,1)} %copy-done.2, bf16[8,32,1792]{2,1,0:T(8,128)(2,1)} %copy-done.1, ...), custom_call_target="tpu_custom_call", output_to_operand_aliasing={{0}: (16, {}), {1}: (17, {})} | custom-call | flops 3758096384 | bytes 20709376 | tf_op jit(solution)/shard_map/pallas_call | solution.py:174
  134.1 0.8 fusion.38
  135.3 0.9 collective-permute-done.30
  136.4 1.0 collective-permute-start.31
  137.4 2.0 collective-permute-done.31
  139.7 2.6 %collective-permute-start.32 = (f32[2,4096]{1,0:T(2,128)S(1)}, f32[2,4096]{1,0:T(2,128)S(1)}, u32[]{:S(2)}, u32[]{:S(2)}) collective-permute-start(f32[2,4096]{1,0:T(2,128)S(1)} %get-tuple-element.90), channel_id=1, source_target_pairs={{0,1},{8,9},{16,17},{24,25},{32,33},{40,41},{48,49},{56,57},{64,65... | collective-permute-start | bytes 98312 | tf_op jit(solution)/shard_map/ppermute | solution.py:32
  142.3 1.7 collective-permute-done.32
  144.3 1.0 collective-permute-start.33
  145.4 1.8 collective-permute-done.33
  147.4 2.6 %collective-permute-start.34 = (f32[2,4096]{1,0:T(2,128)S(1)}, f32[2,4096]{1,0:T(2,128)S(1)}, u32[]{:S(2)}, u32[]{:S(2)}) collective-permute-start(f32[2,4096]{1,0:T(2,128)S(1)} %pad_maximum_fusion.9), channel_id=1, source_target_pairs={{0,4},{8,12},{16,20},{24,28},{32,36},{40,44},{48,52},{56,60},{64,6... | collective-permute-start | bytes 98312 | tf_op jit(solution)/shard_map/ppermute | solution.py:32
  150.0 1.9 collective-permute-done.34
  152.1 0.8 broadcast_in_dim.9
  152.9 7.6 %all-to-all-start.1 = ((f32[8,2,4096]{2,1,0:T(2,128)}), f32[8,2,4096]{2,1,0:T(2,128)S(1)}, u32[]{:S(2)}, u32[]{:S(2)}) async-start(f32[8,2,4096]{2,1,0:T(2,128)} %broadcast_in_dim.9), calls=%async_computation.1 | async-start | bytes 524288 | tf_op jit(solution)/shard_map/all_to_all | solution.py:268
  161.2 0.6 copy.50
  161.8 12.7 %shard_map.57 = bf16[4096,512]{1,0:T(8,128)(2,1)} custom-call(s32[4096]{0:T(1024)} %bitcast.178, bf16[4096,512]{1,0:T(8,128)(2,1)} %bitcast.60.teacher), custom_call_target="tpu_custom_call" | custom-call | bytes 41943040 | tf_op jit(solution)/shard_map/pallas_call | solution.py:239
  176.2 7.5 %multiply_reduce_fusion = f32[4096]{0:T(1024)S(1)} fusion(f32[4096,512]{1,0:T(8,128)} %get-tuple-element.63, bf16[4096,512]{1,0:T(8,128)(2,1)} %shard_map.57, f32[4096]{0:T(1024)S(1)} %bitcast.176, f32[4096]{0:T(1024)S(1)} %bitcast.174), kind=kLoop, calls=%fused_computation.7 | loop fusion | flops 18870272 | bytes 12632064 | tf_op jit(solution)/shard_map/reduce_sum | solution.py:324
  184.4 5.3 %collective-permute-start.35 = (f32[4096]{0:T(1024)S(1)}, f32[4096]{0:T(1024)S(1)}, u32[]{:S(2)}, u32[]{:S(2)}) collective-permute-start(f32[4096]{0:T(1024)S(1)} %bitcast.179), channel_id=1, source_target_pairs={{0,8},{8,0},{16,24},{24,16},{32,40},{40,32},{48,56},{56,48},{64,72... | collective-permute-start | bytes 49160 | tf_op jit(solution)/shard_map/ppermute | solution.py:32
  189.7 0.8 collective-permute-done.35
  190.5 0.7 broadcast_in_dim.10
  191.2 6.9 %all-to-all-start.2 = ((f32[8,1,4096]{2,1,0:T(1,128)}), f32[8,1,4096]{2,1,0:T(1,128)S(1)}, u32[]{:S(2)}, u32[]{:S(2)}) async-start(f32[8,1,4096]{2,1,0:T(1,128)} %broadcast_in_dim.10), calls=%async_computation.2 | async-start | bytes 262144 | tf_op jit(solution)/shard_map/all_to_all | solution.py:268
  198.3 7.8 %all-to-all-done.2 = f32[8,1,4096]{2,1,0:T(1,128)S(1)} async-done(((f32[8,1,4096]{2,1,0:T(1,128)}), f32[8,1,4096]{2,1,0:T(1,128)S(1)}, u32[]{:S(2)}, u32[]{:S(2)}) %all-to-all-start.2) | async-done | bytes 131104 | tf_op jit(solution)/shard_map/all_to_all | solution.py:268
  206.2 0.9 broadcast_in_dim.11
  207.1 6.0 %all-to-all-start.3 = ((f32[16,1,4096]{2,1,0:T(1,128)}), f32[16,1,4096]{2,1,0:T(1,128)S(1)}, u32[]{:S(2)}, u32[]{:S(2)}) async-start(f32[16,1,4096]{2,1,0:T(1,128)} %broadcast_in_dim.11), calls=%async_computation.3 | async-start | bytes 524288 | tf_op jit(solution)/shard_map/all_to_all | solution.py:268
  213.2 0.6 reduce_sum.90
  215.0 5.6 %all-to-all-done.3 = f32[16,1,4096]{2,1,0:T(1,128)S(1)} async-done(((f32[16,1,4096]{2,1,0:T(1,128)}), f32[16,1,4096]{2,1,0:T(1,128)S(1)}, u32[]{:S(2)}, u32[]{:S(2)}) %all-to-all-start.3) | async-done | bytes 262176 | tf_op jit(solution)/shard_map/all_to_all | solution.py:268
  221.4 15.5 %fusion.2 = bf16[1792,512]{1,0:T(8,128)(2,1)} fusion(bf16[4096,1792]{1,0:T(8,128)(2,1)} %bitcast.166, f32[4096,512]{1,0:T(8,128)} %get-tuple-element.63, bf16[4096,512]{1,0:T(8,128)(2,1)} %shard_map.57, f32[4096]{0:T(1024)S(1)} %bitcast.193, f32[4096]{0:T(1024)S(1)} %bitcast.177, f32[4096]{0:T(1024)S(1)} %bitcast.175, f32[4096]{0:T(1024)S(1)} %bitcast.192), kind=kOutput, calls=%fused_computation.13 | convolution fusion | flops 7540178944 | bytes 29163520 | tf_op jit(solution)/shard_map/dot_general | solution.py:337
  (129 shorter events, 9.3 us)
Async XLA Ops:
  0.9 11.4 %collective-permute-start = (bf16[32,1792]{1,0:T(8,128)(2,1)S(1)}, bf16[32,1792]{1,0:T(8,128)(2,1)S(1)}, u32[]{:S(2)}, u32[]{:S(2)}) collective-permute-start(bf16[32,1792]{1,0:T(8,128)(2,1)S(1)} %get-tuple-element.80), channel_id=1, source_target_pairs={{0,16},{8,24},{16,32},{24,40},{32,48},{40,56},{48,64},{56,72},{64,... | collective-permute-start | bytes 344072 | tf_op jit(solution)/shard_map/ppermute | solution.py:32
  3.5 8.9 %collective-permute-start.4 = (bf16[32,1792]{1,0:T(8,128)(2,1)S(1)}, bf16[32,1792]{1,0:T(8,128)(2,1)S(1)}, u32[]{:S(2)}, u32[]{:S(2)}) collective-permute-start(bf16[32,1792]{1,0:T(8,128)(2,1)S(1)} %get-tuple-element.80), channel_id=1, source_target_pairs={{0,112},{8,120},{16,0},{24,8},{32,16},{40,24},{48,32},{56,40},{64,... | collective-permute-start | bytes 344072 | tf_op jit(solution)/shard_map/ppermute | solution.py:32
  12.3 4.9 %collective-permute-start.1 = (bf16[32,1792]{1,0:T(8,128)(2,1)S(1)}, bf16[32,1792]{1,0:T(8,128)(2,1)S(1)}, u32[]{:S(2)}, u32[]{:S(2)}) collective-permute-start(bf16[32,1792]{1,0:T(8,128)(2,1)S(1)} %collective-permute-done), channel_id=1, source_target_pairs={{0,16},{8,24},{16,32},{24,40},{32,48},{40,56},{48,64},{56,72},{64,... | collective-permute-start | bytes 344072 | tf_op jit(solution)/shard_map/ppermute | solution.py:32
  12.3 4.8 %collective-permute-start.5 = (bf16[32,1792]{1,0:T(8,128)(2,1)S(1)}, bf16[32,1792]{1,0:T(8,128)(2,1)S(1)}, u32[]{:S(2)}, u32[]{:S(2)}) collective-permute-start(bf16[32,1792]{1,0:T(8,128)(2,1)S(1)} %collective-permute-done.4), channel_id=1, source_target_pairs={{0,112},{8,120},{16,0},{24,8},{32,16},{40,24},{48,32},{56,40},{64,... | collective-permute-start | bytes 344072 | tf_op jit(solution)/shard_map/ppermute | solution.py:32
  17.2 4.9 %collective-permute-start.2 = (bf16[32,1792]{1,0:T(8,128)(2,1)S(1)}, bf16[32,1792]{1,0:T(8,128)(2,1)S(1)}, u32[]{:S(2)}, u32[]{:S(2)}) collective-permute-start(bf16[32,1792]{1,0:T(8,128)(2,1)S(1)} %collective-permute-done.1), channel_id=1, source_target_pairs={{0,16},{8,24},{16,32},{24,40},{32,48},{40,56},{48,64},{56,72},{64,... | collective-permute-start | bytes 344072 | tf_op jit(solution)/shard_map/ppermute | solution.py:32
  17.2 9.7 %collective-permute-start.6 = (bf16[32,1792]{1,0:T(8,128)(2,1)S(1)}, bf16[32,1792]{1,0:T(8,128)(2,1)S(1)}, u32[]{:S(2)}, u32[]{:S(2)}) collective-permute-start(bf16[32,1792]{1,0:T(8,128)(2,1)S(1)} %collective-permute-done.5), channel_id=1, source_target_pairs={{0,112},{8,120},{16,0},{24,8},{32,16},{40,24},{48,32},{56,40},{64,... | collective-permute-start | bytes 344072 | tf_op jit(solution)/shard_map/ppermute | solution.py:32
  22.0 4.9 %collective-permute-start.3 = (bf16[32,1792]{1,0:T(8,128)(2,1)S(1)}, bf16[32,1792]{1,0:T(8,128)(2,1)S(1)}, u32[]{:S(2)}, u32[]{:S(2)}) collective-permute-start(bf16[32,1792]{1,0:T(8,128)(2,1)S(1)} %collective-permute-done.2), channel_id=1, source_target_pairs={{0,16},{8,24},{16,32},{24,40},{32,48},{40,56},{48,64},{56,72},{64,... | collective-permute-start | bytes 344072 | tf_op jit(solution)/shard_map/ppermute | solution.py:32
  26.9 68.2 %copy-start = (bf16[8,32,1792]{2,1,0:T(8,128)(2,1)}, bf16[8,32,1792]{2,1,0:T(8,128)(2,1)S(1)}, u32[]{:S(2)}) copy-start(bf16[8,32,1792]{2,1,0:T(8,128)(2,1)S(1)} %bitcast_dynamic-update-slice_fusion.refs_1_) | copy-start | bytes 2752516
  26.9 120.4 %all-to-all-start = ((bf16[32,128,512]{2,1,0:T(8,128)(2,1)}), bf16[32,128,512]{2,1,0:T(8,128)(2,1)}, u32[]{:S(2)}, u32[]{:S(2)}) async-start(bf16[32,128,512]{2,1,0:T(8,128)(2,1)} %bitcast.165), calls=%async_computation | async-start | bytes 8388608 | tf_op jit(solution)/shard_map/all_to_all | solution.py:307
  38.3 25.2 %collective-permute-start.10 = (bf16[8,32,1792]{2,1,0:T(8,128)(2,1)S(1)}, bf16[8,32,1792]{2,1,0:T(8,128)(2,1)S(1)}, u32[]{:S(2)}, u32[]{:S(2)}) collective-permute-start(bf16[8,32,1792]{2,1,0:T(8,128)(2,1)S(1)} %bitcast_dynamic-update-slice_fusion.refs_1_), channel_id=1, source_target_pairs={{0,129},{8,137},{16,145},{24,153},{32,161},{40,169},{48,177},{56,1... | collective-permute-start | bytes 2752520 | tf_op jit(solution)/shard_map/ppermute | solution.py:55
  41.0 22.7 %collective-permute-start.7 = (bf16[8,32,1792]{2,1,0:T(8,128)(2,1)S(1)}, bf16[8,32,1792]{2,1,0:T(8,128)(2,1)S(1)}, u32[]{:S(2)}, u32[]{:S(2)}) collective-permute-start(bf16[8,32,1792]{2,1,0:T(8,128)(2,1)S(1)} %bitcast_dynamic-update-slice_fusion.refs_1_), channel_id=1, source_target_pairs={{0,2},{8,10},{16,18},{24,26},{32,34},{40,42},{48,50},{56,58},{64,6... | collective-permute-start | bytes 2752520 | tf_op jit(solution)/shard_map/ppermute | solution.py:32
  42.4 11.3 %collective-permute-start.8 = (bf16[4,32,1792]{2,1,0:T(8,128)(2,1)S(1)}, bf16[4,32,1792]{2,1,0:T(8,128)(2,1)}, u32[]{:S(2)}, u32[]{:S(2)}) collective-permute-start(bf16[4,32,1792]{2,1,0:T(8,128)(2,1)S(1)} %get-tuple-element.82), channel_id=1, source_target_pairs={{0,6},{8,14},{16,22},{24,30},{32,38},{40,46},{48,54},{56,62},{64,7... | collective-permute-start | bytes 1376264 | tf_op jit(solution)/shard_map/ppermute | solution.py:32
  43.9 19.6 %collective-permute-start.9 = (bf16[4,32,1792]{2,1,0:T(8,128)(2,1)S(1)}, bf16[4,32,1792]{2,1,0:T(8,128)(2,1)}, u32[]{:S(2)}, u32[]{:S(2)}) collective-permute-start(bf16[4,32,1792]{2,1,0:T(8,128)(2,1)S(1)} %get-tuple-element.81), channel_id=1, source_target_pairs={{0,6},{8,14},{16,22},{24,30},{32,38},{40,46},{48,54},{56,62},{64,7... | collective-permute-start | bytes 1376264 | tf_op jit(solution)/shard_map/ppermute | solution.py:32
  45.4 22.1 %collective-permute-start.15 = (bf16[8,32,1792]{2,1,0:T(8,128)(2,1)S(1)}, bf16[8,32,1792]{2,1,0:T(8,128)(2,1)S(1)}, u32[]{:S(2)}, u32[]{:S(2)}) collective-permute-start(bf16[8,32,1792]{2,1,0:T(8,128)(2,1)S(1)} %bitcast_dynamic-update-slice_fusion.refs_1_), channel_id=1, source_target_pairs={{0,8},{8,0},{16,24},{24,16},{32,40},{40,32},{48,56},{56,48},{64,72... | collective-permute-start | bytes 2752520 | tf_op jit(solution)/shard_map/ppermute | solution.py:32
  63.5 56.2 %copy-start.1 = (bf16[8,32,1792]{2,1,0:T(8,128)(2,1)}, bf16[8,32,1792]{2,1,0:T(8,128)(2,1)S(1)}, u32[]{:S(2)}) copy-start(bf16[8,32,1792]{2,1,0:T(8,128)(2,1)S(1)} %collective-permute-done.10.refs_1_) | copy-start | bytes 2752516
  63.7 26.6 %copy-start.13 = (bf16[8,32,1792]{2,1,0:T(8,128)(2,1)}, bf16[8,32,1792]{2,1,0:T(8,128)(2,1)S(1)}, u32[]{:S(2)}) copy-start(bf16[8,32,1792]{2,1,0:T(8,128)(2,1)S(1)} %collective-permute-done.7.refs_0_) | copy-start | bytes 2752516
  63.7 11.8 %collective-permute-start.13 = (bf16[4,32,1792]{2,1,0:T(8,128)(2,1)S(1)}, bf16[4,32,1792]{2,1,0:T(8,128)(2,1)}, u32[]{:S(2)}, u32[]{:S(2)}) collective-permute-start(bf16[4,32,1792]{2,1,0:T(8,128)(2,1)S(1)} %slice.47), channel_id=1, source_target_pairs={{0,2},{8,10},{16,18},{24,26},{32,34},{40,42},{48,50},{56,58},{64,6... | collective-permute-start | bytes 1376264 | tf_op jit(solution)/shard_map/ppermute | solution.py:32
  64.9 24.0 %collective-permute-start.11 = (bf16[8,32,1792]{2,1,0:T(8,128)(2,1)S(1)}, bf16[8,32,1792]{2,1,0:T(8,128)(2,1)S(1)}, u32[]{:S(2)}, u32[]{:S(2)}) collective-permute-start(bf16[8,32,1792]{2,1,0:T(8,128)(2,1)S(1)} %collective-permute-done.7.refs_0_), channel_id=1, source_target_pairs={{0,129},{8,137},{16,145},{24,153},{32,161},{40,169},{48,177},{56,1... | collective-permute-start | bytes 2752520 | tf_op jit(solution)/shard_map/ppermute | solution.py:55
  65.3 23.6 %collective-permute-start.16 = (bf16[8,32,1792]{2,1,0:T(8,128)(2,1)S(1)}, bf16[8,32,1792]{2,1,0:T(8,128)(2,1)S(1)}, u32[]{:S(2)}, u32[]{:S(2)}) collective-permute-start(bf16[8,32,1792]{2,1,0:T(8,128)(2,1)S(1)} %collective-permute-done.7.refs_0_), channel_id=1, source_target_pairs={{0,8},{8,0},{16,24},{24,16},{32,40},{40,32},{48,56},{56,48},{64,72... | collective-permute-start | bytes 2752520 | tf_op jit(solution)/shard_map/ppermute | solution.py:32
  67.4 21.5 %collective-permute-start.17 = (bf16[8,32,1792]{2,1,0:T(8,128)(2,1)S(1)}, bf16[8,32,1792]{2,1,0:T(8,128)(2,1)S(1)}, u32[]{:S(2)}, u32[]{:S(2)}) collective-permute-start(bf16[8,32,1792]{2,1,0:T(8,128)(2,1)S(1)} %collective-permute-done.10.refs_1_), channel_id=1, source_target_pairs={{0,8},{8,0},{16,24},{24,16},{32,40},{40,32},{48,56},{56,48},{64,72... | collective-permute-start | bytes 2752520 | tf_op jit(solution)/shard_map/ppermute | solution.py:32
  67.4 22.9 %copy-start.16 = (bf16[8,32,1792]{2,1,0:T(8,128)(2,1)}, bf16[8,32,1792]{2,1,0:T(8,128)(2,1)S(1)}, u32[]{:S(2)}) copy-start(bf16[8,32,1792]{2,1,0:T(8,128)(2,1)S(1)} %collective-permute-done.15.refs_7_) | copy-start | bytes 2752516
  67.4 19.6 %collective-permute-start.12 = (bf16[4,32,1792]{2,1,0:T(8,128)(2,1)}, bf16[4,32,1792]{2,1,0:T(8,128)(2,1)S(1)}, u32[]{:S(2)}, u32[]{:S(2)}) collective-permute-start(bf16[4,32,1792]{2,1,0:T(8,128)(2,1)} %collective-permute-done.8.refs_2_), channel_id=1, source_target_pairs={{0,128},{8,136},{16,144},{24,152},{32,160},{40,168},{48,176},{56,1... | collective-permute-start | bytes 1376264 | tf_op jit(solution)/shard_map/ppermute | solution.py:55
  75.5 13.3 %collective-permute-start.14 = (bf16[4,32,1792]{2,1,0:T(8,128)(2,1)}, bf16[4,32,1792]{2,1,0:T(8,128)(2,1)}, u32[]{:S(2)}, u32[]{:S(2)}) collective-permute-start(bf16[4,32,1792]{2,1,0:T(8,128)(2,1)} %collective-permute-done.9.refs_3_), channel_id=1, source_target_pairs={{0,6},{8,14},{16,22},{24,30},{32,38},{40,46},{48,54},{56,62},{64,7... | collective-permute-start | bytes 1376264 | tf_op jit(solution)/shard_map/ppermute | solution.py:32
  87.0 32.7 %copy-start.5 = (bf16[4,32,1792]{2,1,0:T(8,128)(2,1)}, bf16[4,32,1792]{2,1,0:T(8,128)(2,1)S(1)}, u32[]{:S(2)}) copy-start(bf16[4,32,1792]{2,1,0:T(8,128)(2,1)S(1)} %collective-permute-done.12.refs_2_) | copy-start | bytes 1376260
  87.0 3.7 %collective-permute-start.18 = (bf16[4,32,1792]{2,1,0:T(8,128)(2,1)}, bf16[4,32,1792]{2,1,0:T(8,128)(2,1)}, u32[]{:S(2)}, u32[]{:S(2)}) collective-permute-start(bf16[4,32,1792]{2,1,0:T(8,128)(2,1)} %collective-permute-done.8.refs_2_), channel_id=1, source_target_pairs={{0,8},{8,0},{16,24},{24,16},{32,40},{40,32},{48,56},{56,48},{64,72... | collective-permute-start | bytes 1376264 | tf_op jit(solution)/shard_map/ppermute | solution.py:32
  88.8 4.6 %collective-permute-start.19 = (bf16[4,32,1792]{2,1,0:T(8,128)(2,1)}, bf16[4,32,1792]{2,1,0:T(8,128)(2,1)}, u32[]{:S(2)}, u32[]{:S(2)}) collective-permute-start(bf16[4,32,1792]{2,1,0:T(8,128)(2,1)} %collective-permute-done.9.refs_3_), channel_id=1, source_target_pairs={{0,8},{8,0},{16,24},{24,16},{32,40},{40,32},{48,56},{56,48},{64,72... | collective-permute-start | bytes 1376264 | tf_op jit(solution)/shard_map/ppermute | solution.py:32
  88.9 30.8 %copy-start.2 = (bf16[8,32,1792]{2,1,0:T(8,128)(2,1)}, bf16[8,32,1792]{2,1,0:T(8,128)(2,1)S(1)}, u32[]{:S(2)}) copy-start(bf16[8,32,1792]{2,1,0:T(8,128)(2,1)S(1)} %collective-permute-done.11.refs_0_) | copy-start | bytes 2752516
  88.9 1.4 copy-start.17
  89.0 1.0 copy-start.3
  89.9 4.6 %collective-permute-start.20 = (bf16[4,32,1792]{2,1,0:T(8,128)(2,1)}, bf16[4,32,1792]{2,1,0:T(8,128)(2,1)}, u32[]{:S(2)}, u32[]{:S(2)}) collective-permute-start(bf16[4,32,1792]{2,1,0:T(8,128)(2,1)} %collective-permute-done.13.refs_4_), channel_id=1, source_target_pairs={{0,8},{8,0},{16,24},{24,16},{32,40},{40,32},{48,56},{56,48},{64,72... | collective-permute-start | bytes 1376264 | tf_op jit(solution)/shard_map/ppermute | solution.py:32
  90.4 4.2 %collective-permute-start.21 = (bf16[4,32,1792]{2,1,0:T(8,128)(2,1)}, bf16[4,32,1792]{2,1,0:T(8,128)(2,1)}, u32[]{:S(2)}, u32[]{:S(2)}) collective-permute-start(bf16[4,32,1792]{2,1,0:T(8,128)(2,1)} %collective-permute-done.14.refs_5_), channel_id=1, source_target_pairs={{0,8},{8,0},{16,24},{24,16},{32,40},{40,32},{48,56},{56,48},{64,72... | collective-permute-start | bytes 1376264 | tf_op jit(solution)/shard_map/ppermute | solution.py:32
  90.6 20.6 %collective-permute-start.22 = (bf16[4,32,1792]{2,1,0:T(8,128)(2,1)}, bf16[4,32,1792]{2,1,0:T(8,128)(2,1)S(1)}, u32[]{:S(2)}, u32[]{:S(2)}) collective-permute-start(bf16[4,32,1792]{2,1,0:T(8,128)(2,1)} %collective-permute-done.9.refs_3_), channel_id=1, source_target_pairs={{0,128},{8,136},{16,144},{24,152},{32,160},{40,168},{48,176},{56,1... | collective-permute-start | bytes 1376264 | tf_op jit(solution)/shard_map/ppermute | solution.py:55
  90.8 20.4 %collective-permute-start.23 = (bf16[4,32,1792]{2,1,0:T(8,128)(2,1)}, bf16[4,32,1792]{2,1,0:T(8,128)(2,1)S(1)}, u32[]{:S(2)}, u32[]{:S(2)}) collective-permute-start(bf16[4,32,1792]{2,1,0:T(8,128)(2,1)} %collective-permute-done.13.refs_4_), channel_id=1, source_target_pairs={{0,129},{8,137},{16,145},{24,153},{32,161},{40,169},{48,177},{56,1... | collective-permute-start | bytes 1376264 | tf_op jit(solution)/shard_map/ppermute | solution.py:55
  93.4 20.2 %collective-permute-start.24 = (bf16[4,32,1792]{2,1,0:T(8,128)(2,1)}, bf16[4,32,1792]{2,1,0:T(8,128)(2,1)S(1)}, u32[]{:S(2)}, u32[]{:S(2)}) collective-permute-start(bf16[4,32,1792]{2,1,0:T(8,128)(2,1)} %collective-permute-done.14.refs_5_), channel_id=1, source_target_pairs={{0,129},{8,137},{16,145},{24,153},{32,161},{40,169},{48,177},{56,1... | collective-permute-start | bytes 1376264 | tf_op jit(solution)/shard_map/ppermute | solution.py:55
  111.2 8.5 %copy-start.6 = (bf16[4,32,1792]{2,1,0:T(8,128)(2,1)}, bf16[4,32,1792]{2,1,0:T(8,128)(2,1)S(1)}, u32[]{:S(2)}) copy-start(bf16[4,32,1792]{2,1,0:T(8,128)(2,1)S(1)} %collective-permute-done.22.refs_3_) | copy-start | bytes 1376260
  111.2 8.5 %copy-start.7 = (bf16[4,32,1792]{2,1,0:T(8,128)(2,1)}, bf16[4,32,1792]{2,1,0:T(8,128)(2,1)S(1)}, u32[]{:S(2)}) copy-start(bf16[4,32,1792]{2,1,0:T(8,128)(2,1)S(1)} %collective-permute-done.23.refs_4_) | copy-start | bytes 1376260
  113.6 6.1 %copy-start.8 = (bf16[4,32,1792]{2,1,0:T(8,128)(2,1)}, bf16[4,32,1792]{2,1,0:T(8,128)(2,1)S(1)}, u32[]{:S(2)}) copy-start(bf16[4,32,1792]{2,1,0:T(8,128)(2,1)S(1)} %collective-permute-done.24.refs_5_) | copy-start | bytes 1376260
  113.6 46.8 %copy-start.14 = (s32[4096]{0:T(1024)S(1)}, s32[4096]{0:T(1024)}, u32[]{:S(2)}) copy-start(s32[4096]{0:T(1024)} %param.8) | copy-start | bytes 49156
  113.6 6.1 %collective-permute-start.25 = (bf16[8,32,1792]{2,1,0:T(8,128)(2,1)S(1)}, bf16[8,32,1792]{2,1,0:T(8,128)(2,1)S(1)}, u32[]{:S(2)}, u32[]{:S(2)}) collective-permute-start(bf16[8,32,1792]{2,1,0:T(8,128)(2,1)S(1)} %collective-permute-done.11.refs_0_), channel_id=1, source_target_pairs={{0,8},{8,0},{16,24},{24,16},{32,40},{40,32},{48,56},{56,48},{64,72... | collective-permute-start | bytes 2752520 | tf_op jit(solution)/shard_map/ppermute | solution.py:32
  115.0 2.8 %collective-permute-start.26 = (bf16[4,32,1792]{2,1,0:T(8,128)(2,1)S(1)}, bf16[4,32,1792]{2,1,0:T(8,128)(2,1)S(1)}, u32[]{:S(2)}, u32[]{:S(2)}) collective-permute-start(bf16[4,32,1792]{2,1,0:T(8,128)(2,1)S(1)} %collective-permute-done.12.refs_2_), channel_id=1, source_target_pairs={{0,8},{8,0},{16,24},{24,16},{32,40},{40,32},{48,56},{56,48},{64,72... | collective-permute-start | bytes 1376264 | tf_op jit(solution)/shard_map/ppermute | solution.py:32
  115.1 3.3 %collective-permute-start.27 = (bf16[4,32,1792]{2,1,0:T(8,128)(2,1)S(1)}, bf16[4,32,1792]{2,1,0:T(8,128)(2,1)S(1)}, u32[]{:S(2)}, u32[]{:S(2)}) collective-permute-start(bf16[4,32,1792]{2,1,0:T(8,128)(2,1)S(1)} %collective-permute-done.22.refs_3_), channel_id=1, source_target_pairs={{0,8},{8,0},{16,24},{24,16},{32,40},{40,32},{48,56},{56,48},{64,72... | collective-permute-start | bytes 1376264 | tf_op jit(solution)/shard_map/ppermute | solution.py:32
  115.5 3.6 %collective-permute-start.28 = (bf16[4,32,1792]{2,1,0:T(8,128)(2,1)S(1)}, bf16[4,32,1792]{2,1,0:T(8,128)(2,1)S(1)}, u32[]{:S(2)}, u32[]{:S(2)}) collective-permute-start(bf16[4,32,1792]{2,1,0:T(8,128)(2,1)S(1)} %collective-permute-done.23.refs_4_), channel_id=1, source_target_pairs={{0,8},{8,0},{16,24},{24,16},{32,40},{40,32},{48,56},{56,48},{64,72... | collective-permute-start | bytes 1376264 | tf_op jit(solution)/shard_map/ppermute | solution.py:32
  115.6 4.1 %collective-permute-start.29 = (bf16[4,32,1792]{2,1,0:T(8,128)(2,1)S(1)}, bf16[4,32,1792]{2,1,0:T(8,128)(2,1)S(1)}, u32[]{:S(2)}, u32[]{:S(2)}) collective-permute-start(bf16[4,32,1792]{2,1,0:T(8,128)(2,1)S(1)} %collective-permute-done.24.refs_5_), channel_id=1, source_target_pairs={{0,8},{8,0},{16,24},{24,16},{32,40},{40,32},{48,56},{56,48},{64,72... | collective-permute-start | bytes 1376264 | tf_op jit(solution)/shard_map/ppermute | solution.py:32
  117.7 2.0 copy-start.9
  118.4 1.4 copy-start.10
  119.1 0.8 copy-start.11
  119.7 0.8 copy-start.12
  120.5 0.9 copy-start.4
  134.8 1.3 collective-permute-start.30
  136.4 3.1 %collective-permute-start.31 = (f32[2,4096]{1,0:T(2,128)S(1)}, f32[2,4096]{1,0:T(2,128)S(1)}, u32[]{:S(2)}, u32[]{:S(2)}) collective-permute-start(f32[2,4096]{1,0:T(2,128)S(1)} %get-tuple-element.92), channel_id=1, source_target_pairs={{0,128},{8,136},{16,144},{24,152},{32,160},{40,168},{48,176},{56,1... | collective-permute-start | bytes 98312 | tf_op jit(solution)/shard_map/ppermute | solution.py:55
  139.7 4.4 %collective-permute-start.32 = (f32[2,4096]{1,0:T(2,128)S(1)}, f32[2,4096]{1,0:T(2,128)S(1)}, u32[]{:S(2)}, u32[]{:S(2)}) collective-permute-start(f32[2,4096]{1,0:T(2,128)S(1)} %get-tuple-element.90), channel_id=1, source_target_pairs={{0,1},{8,9},{16,17},{24,25},{32,33},{40,41},{48,49},{56,57},{64,65... | collective-permute-start | bytes 98312 | tf_op jit(solution)/shard_map/ppermute | solution.py:32
  144.3 2.9 %collective-permute-start.33 = (f32[2,4096]{1,0:T(2,128)S(1)}, f32[2,4096]{1,0:T(2,128)S(1)}, u32[]{:S(2)}, u32[]{:S(2)}) collective-permute-start(f32[2,4096]{1,0:T(2,128)S(1)} %get-tuple-element.88), channel_id=1, source_target_pairs={{0,2},{8,10},{16,18},{24,26},{32,34},{40,42},{48,50},{56,58},{64,6... | collective-permute-start | bytes 98312 | tf_op jit(solution)/shard_map/ppermute | solution.py:298
  147.4 4.5 %collective-permute-start.34 = (f32[2,4096]{1,0:T(2,128)S(1)}, f32[2,4096]{1,0:T(2,128)S(1)}, u32[]{:S(2)}, u32[]{:S(2)}) collective-permute-start(f32[2,4096]{1,0:T(2,128)S(1)} %pad_maximum_fusion.9), channel_id=1, source_target_pairs={{0,4},{8,12},{16,20},{24,28},{32,36},{40,44},{48,52},{56,60},{64,6... | collective-permute-start | bytes 98312 | tf_op jit(solution)/shard_map/ppermute | solution.py:32
  152.9 21.7 %all-to-all-start.1 = ((f32[8,2,4096]{2,1,0:T(2,128)}), f32[8,2,4096]{2,1,0:T(2,128)S(1)}, u32[]{:S(2)}, u32[]{:S(2)}) async-start(f32[8,2,4096]{2,1,0:T(2,128)} %broadcast_in_dim.9), calls=%async_computation.1 | async-start | bytes 524288 | tf_op jit(solution)/shard_map/all_to_all | solution.py:268
  174.5 23.6 %copy-start.15 = (s32[32]{0:T(128)S(1)}, s32[32]{0:T(128)}, u32[]{:S(2)}) copy-start(s32[32]{0:T(128)} %param.9) | copy-start | bytes 388
  184.4 6.2 %collective-permute-start.35 = (f32[4096]{0:T(1024)S(1)}, f32[4096]{0:T(1024)S(1)}, u32[]{:S(2)}, u32[]{:S(2)}) collective-permute-start(f32[4096]{0:T(1024)S(1)} %bitcast.179), channel_id=1, source_target_pairs={{0,8},{8,0},{16,24},{24,16},{32,40},{40,32},{48,56},{56,48},{64,72... | collective-permute-start | bytes 49160 | tf_op jit(solution)/shard_map/ppermute | solution.py:32
  191.2 14.8 %all-to-all-start.2 = ((f32[8,1,4096]{2,1,0:T(1,128)}), f32[8,1,4096]{2,1,0:T(1,128)S(1)}, u32[]{:S(2)}, u32[]{:S(2)}) async-start(f32[8,1,4096]{2,1,0:T(1,128)} %broadcast_in_dim.10), calls=%async_computation.2 | async-start | bytes 262144 | tf_op jit(solution)/shard_map/all_to_all | solution.py:268
  207.1 13.5 %all-to-all-start.3 = ((f32[16,1,4096]{2,1,0:T(1,128)}), f32[16,1,4096]{2,1,0:T(1,128)S(1)}, u32[]{:S(2)}, u32[]{:S(2)}) async-start(f32[16,1,4096]{2,1,0:T(1,128)} %broadcast_in_dim.11), calls=%async_computation.3 | async-start | bytes 524288 | tf_op jit(solution)/shard_map/all_to_all | solution.py:268
where the time goes:
time: 239 us; the launch traced here: 237 us
  starting transfers between devices  78.7 us (33%)
  waiting for transfers between devices  76.2 us (32%)
  Pallas kernels  37.9 us (16%)
  local copies, waits for them, and re-layouts  16.2 us (7%)
  matrix products  15.5 us (6%)
  other arithmetic  11.2 us (5%)
    ppermute x28, waiting for transfers between devices, hop(): return lax.ppermute(array, AXES, pairs)  42.8 us
    ppermute x28, starting transfers between devices, hop(): return lax.ppermute(array, AXES, pairs)  38.2 us
    pallas_call x2, Pallas kernels, block_logits(): pl.pallas_call(functools.partial(logits_kernel, column), grid_spec=pltpu....  25.2 us
    all_to_all x3, starting transfers between devices, from_members(): lax.all_to_all(copies, AXES, split_axis=0, concat_axis=0, tiled=True, axi...  20.5 us
    ppermute x7, waiting for transfers between devices, cross(): return lax.ppermute(array, AXES, pairs)  18.2 us
    dot_general x1, matrix products, per_device(): lax.dot_general(gathered, dlogits, (((0,), (0,)), ((), ())), preferred_el...  15.5 us
    all_to_all x3, waiting for transfers between devices, from_members(): lax.all_to_all(copies, AXES, split_axis=0, concat_axis=0, tiled=True, axi...  13.4 us
    pallas_call x1, Pallas kernels, take_rows(): pl.pallas_call(rows_kernel, grid_spec=pltpu.PrefetchScalarGridSpec(num_sc...  12.7 us
  transfers between devices with their start and end apart: 40, of which 22 were waited for; matrix products, arithmetic and copies ran while one was open for 4% of the time, Pallas kernels for 16%

commit v1 on v0

--- a/solution.py
+++ b/solution.py
@@ -268,34 +268,9 @@
     return lax.all_to_all(copies, AXES, split_axis=0, concat_axis=0, tiled=True, axis_index_groups=groups)
 
 
-def merge_totals(peaks, totals):
-    peak = jnp.max(peaks, axis=0)
-    return jnp.stack([peak, jnp.sum(totals * jnp.exp(peaks - peak[None]), axis=0)])
-
-
-def merge_two(mine, theirs):
-    both = jnp.stack([mine, theirs])
-    return merge_totals(both[:, 0], both[:, 1])
-
-
-def merge_over_plane(stats, teacher):
-    stats = merge_two(stats, hop(stats, flip=1))
-    stats = merge_two(stats, cross(stats, near=True))
-    stats = merge_two(stats, hop(stats, dx=2))
-    stats = merge_two(stats, turn_pair(stats))
-    stats, teacher = tie(stats, teacher)
-    return merge_two(stats, hop(stats, dy=2)), teacher
-
-
-def turn_pair(array):
-    pairs = [
-        (linear(x, y, z, core), linear(x, y ^ 1, z, core))
-        for x in range(NX)
-        for y in range(NY)
-        for z in range(NZ)
-        for core in range(2)
-    ]
-    return lax.ppermute(array, AXES, pairs)
+def peak_and_total(logs):
+    peak = jnp.max(logs, axis=0)
+    return peak, jnp.sum(jnp.exp(logs - peak[None]), axis=0)
 
 
 def make_per_device(tok, voc):
@@ -308,14 +283,16 @@
         place = coords()
         gathered, logits, local_peak, local_total = gather_logits(place, here, head_weight)
         gathered = gathered.reshape(rows_all, -1)
-        along_z = members(lambda x_lo, z, core, voc: (x_lo, core, voc))
+        in_column = members(lambda x_lo, z, core, voc: (x_lo, voc))
         in_plane = members(lambda x_lo, z, core, voc: (z, core))
-        stats = jnp.stack([local_peak.reshape(-1), local_total.reshape(-1)])
-        stats, teacher = merge_over_plane(stats, teacher)
+        log_total = local_peak.reshape(-1) + jnp.log(local_total.reshape(-1))
+        log_total, teacher = tie(log_total, teacher)
         aligned = take_rows(teacher.reshape(rows_all, -1), to_local(teacher_row, place))
+        log_total = from_members(log_total, in_column)
+        log_total, aligned = tie(log_total, aligned)
         aligned = aligned.astype(jnp.float32)
-        stats = from_members(stats, along_z)
-        row_peak, row_total = merge_totals(stats[:, 0], stats[:, 1])
+        peak, total = peak_and_total(log_total)
+        row_peak, row_total = peak_and_total(from_members(peak + jnp.log(total), in_plane))
         row_peak, row_total = to_local(row_peak, place), to_local(row_total, place)
         log_student = logits - row_peak[:, None] - jnp.log(row_total)[:, None]
         student = jnp.exp(log_student)
@@ -323,8 +300,7 @@
         grad_prob = 0.5 * (log_student - log_mix)
         local_centre = jnp.sum(student * grad_prob, axis=1)
         centre = from_local(local_centre, place)
-        centre = centre + hop(centre, flip=1)
-        centre = jnp.sum(from_members(centre, along_z), axis=0)
+        centre = jnp.sum(from_members(centre, in_column), axis=0)
         centre = to_local(jnp.sum(from_members(centre, in_plane), axis=0), place)
         positions = jnp.arange(SEQ_LEN, dtype=jnp.int32)
         valid_mask = (positions[None, :] < lengths[:, None]).astype(jnp.float32).reshape(-1)

time: 239 us -> 234 us (0.979)
  blocking collectives: 0 us -> 13.5 us
  starting transfers between devices: 78.7 us -> 65.8 us
  waiting for transfers between devices: 76.2 us -> 72 us
    all_to_all x0 -> x1, blocking collectives: none -> 13.5 us  [from_members(): lax.all_to_all(copies, AXES, split_axis=0, concat_axis=0, tiled=True, axi...]
    ppermute x28 -> x24, starting transfers between devices: 38.2 us -> 27.3 us  [hop(): return lax.ppermute(array, AXES, pairs)]
    ppermute x28 -> x24, waiting for transfers between devices: 42.8 us -> 37.5 us  [hop(): return lax.ppermute(array, AXES, pairs)]
    all_to_all x3, waiting for transfers between devices: 13.4 us -> 18.4 us  [from_members(): lax.all_to_all(copies, AXES, split_axis=0, concat_axis=0, tiled=True, axi...]
    ppermute x7 -> x6, waiting for transfers between devices: 18.2 us -> 16.2 us  [cross(): return lax.ppermute(array, AXES, pairs)]
    ppermute x7 -> x6, starting transfers between devices: 7.7 us -> 6.67 us  [cross(): return lax.ppermute(array, AXES, pairs)]
  transfers between devices with their start and end apart: 40 -> 34, of which waited for: 22 -> 16; matrix products, arithmetic and copies ran while one was open for 4% -> 4% of each run, Pallas kernels for 16% -> 16%
where the time goes in v1:
time: 234 us; the launch traced here: 233 us
  waiting for transfers between devices  72 us (31%)
  starting transfers between devices  65.8 us (28%)
  Pallas kernels  37.9 us (16%)
  local copies, waits for them, and re-layouts  16.7 us (7%)
  matrix products  15.5 us (7%)
  blocking collectives  13.5 us (6%)
  other arithmetic  10.3 us (4%)
    ppermute x24, waiting for transfers between devices, hop(): return lax.ppermute(array, AXES, pairs)  37.5 us
    ppermute x24, starting transfers between devices, hop(): return lax.ppermute(array, AXES, pairs)  27.3 us
    pallas_call x2, Pallas kernels, block_logits(): pl.pallas_call(functools.partial(logits_kernel, column), grid_spec=pltpu....  25.2 us
    all_to_all x3, starting transfers between devices, from_members(): lax.all_to_all(copies, AXES, split_axis=0, concat_axis=0, tiled=True, axi...  20.6 us
    all_to_all x3, waiting for transfers between devices, from_members(): lax.all_to_all(copies, AXES, split_axis=0, concat_axis=0, tiled=True, axi...  18.4 us
    ppermute x6, waiting for transfers between devices, cross(): return lax.ppermute(array, AXES, pairs)  16.2 us
    dot_general x1, matrix products, per_device(): lax.dot_general(gathered, dlogits, (((0,), (0,)), ((), ())), preferred_el...  15.5 us
    all_to_all x1, blocking collectives, from_members(): lax.all_to_all(copies, AXES, split_axis=0, concat_axis=0, tiled=True, axi...  13.5 us
  transfers between devices with their start and end apart: 34, of which 16 were waited for; matrix products, arithmetic and copies ran while one was open for 4% of the time, Pallas kernels for 16%

profile of v1, /device:TPU:1, one launch (start us, length us, event | category | flops | bytes accessed | tf_op | source)
XLA Modules:
  0.0 232.9 jit_solution(2233343006683419989)
XLA Ops:
  0.0 0.9 bitcast_dynamic-update-slice_fusion.7
  0.9 2.5 %collective-permute-start = (bf16[32,1792]{1,0:T(8,128)(2,1)S(1)}, bf16[32,1792]{1,0:T(8,128)(2,1)S(1)}, u32[]{:S(2)}, u32[]{:S(2)}) collective-permute-start(bf16[32,1792]{1,0:T(8,128)(2,1)S(1)} %get-tuple-element.74), channel_id=1, source_target_pairs={{0,16},{8,24},{16,32},{24,40},{32,48},{40,56},{48,64},{56,72},{64,... | collective-permute-start | bytes 344072 | tf_op jit(solution)/shard_map/ppermute | solution.py:32
  3.5 4.0 %collective-permute-start.4 = (bf16[32,1792]{1,0:T(8,128)(2,1)S(1)}, bf16[32,1792]{1,0:T(8,128)(2,1)S(1)}, u32[]{:S(2)}, u32[]{:S(2)}) collective-permute-start(bf16[32,1792]{1,0:T(8,128)(2,1)S(1)} %get-tuple-element.74), channel_id=1, source_target_pairs={{0,112},{8,120},{16,0},{24,8},{32,16},{40,24},{48,32},{56,40},{64,... | collective-permute-start | bytes 344072 | tf_op jit(solution)/shard_map/ppermute | solution.py:32
  7.5 4.8 %copy.34 = bf16[16,32,8,512]{3,2,0,1:T(8,128)(2,1)} copy(bf16[16,32,8,512]{3,2,1,0:T(8,128)(2,1)} %bitcast.84) | data formatting | bytes 8388608 | tf_op jit(solution)/shard_map/reshape | solution.py:280
  12.3 2.7 %collective-permute-start.5 = (bf16[32,1792]{1,0:T(8,128)(2,1)S(1)}, bf16[32,1792]{1,0:T(8,128)(2,1)S(1)}, u32[]{:S(2)}, u32[]{:S(2)}) collective-permute-start(bf16[32,1792]{1,0:T(8,128)(2,1)S(1)} %collective-permute-done.4), channel_id=1, source_target_pairs={{0,112},{8,120},{16,0},{24,8},{32,16},{40,24},{48,32},{56,40},{64,... | collective-permute-start | bytes 344072 | tf_op jit(solution)/shard_map/ppermute | solution.py:32
  15.1 2.1 collective-permute-done.1
  17.2 2.7 %collective-permute-start.6 = (bf16[32,1792]{1,0:T(8,128)(2,1)S(1)}, bf16[32,1792]{1,0:T(8,128)(2,1)S(1)}, u32[]{:S(2)}, u32[]{:S(2)}) collective-permute-start(bf16[32,1792]{1,0:T(8,128)(2,1)S(1)} %collective-permute-done.5), channel_id=1, source_target_pairs={{0,112},{8,120},{16,0},{24,8},{32,16},{40,24},{48,32},{56,40},{64,... | collective-permute-start | bytes 344072 | tf_op jit(solution)/shard_map/ppermute | solution.py:32
  19.9 2.1 collective-permute-done.2
  22.0 4.8 %collective-permute-done.3 = bf16[32,1792]{1,0:T(8,128)(2,1)S(1)} collective-permute-done((bf16[32,1792]{1,0:T(8,128)(2,1)S(1)}, bf16[32,1792]{1,0:T(8,128)(2,1)S(1)}, u32[]{:S(2)}, u32[]{:S(2)}) %collective-permute-start.3) | collective-permute-done | bytes 114720 | tf_op jit(solution)/shard_map/ppermute | solution.py:32
  26.9 11.3 %all-to-all-start = ((bf16[32,128,512]{2,1,0:T(8,128)(2,1)}), bf16[32,128,512]{2,1,0:T(8,128)(2,1)}, u32[]{:S(2)}, u32[]{:S(2)}) async-start(bf16[32,128,512]{2,1,0:T(8,128)(2,1)} %bitcast.82), calls=%async_computation | async-start | bytes 8388608 | tf_op jit(solution)/shard_map/all_to_all | solution.py:282
  38.2 2.7 %collective-permute-start.10 = (bf16[8,32,1792]{2,1,0:T(8,128)(2,1)S(1)}, bf16[8,32,1792]{2,1,0:T(8,128)(2,1)S(1)}, u32[]{:S(2)}, u32[]{:S(2)}) collective-permute-start(bf16[8,32,1792]{2,1,0:T(8,128)(2,1)S(1)} %bitcast_dynamic-update-slice_fusion.refs_1_), channel_id=1, source_target_pairs={{0,129},{8,137},{16,145},{24,153},{32,161},{40,169},{48,177},{56,1... | collective-permute-start | bytes 2752520 | tf_op jit(solution)/shard_map/ppermute | solution.py:55
  41.0 1.3 collective-permute-start.7
  42.4 1.5 collective-permute-start.8
  43.9 1.5 collective-permute-start.9
  45.3 1.5 collective-permute-start.15
  46.8 6.8 %collective-permute-done.8.refs_2_ = bf16[4,32,1792]{2,1,0:T(8,128)(2,1)} collective-permute-done((bf16[4,32,1792]{2,1,0:T(8,128)(2,1)S(1)}, bf16[4,32,1792]{2,1,0:T(8,128)(2,1)}, u32[]{:S(2)}, u32[]{:S(2)}) %collective-permute-start.8) | collective-permute-done | bytes 458784 | tf_op jit(solution)/shard_map/ppermute | solution.py:32
  53.6 9.8 %collective-permute-done.9.refs_3_ = bf16[4,32,1792]{2,1,0:T(8,128)(2,1)} collective-permute-done((bf16[4,32,1792]{2,1,0:T(8,128)(2,1)S(1)}, bf16[4,32,1792]{2,1,0:T(8,128)(2,1)}, u32[]{:S(2)}, u32[]{:S(2)}) %collective-permute-start.9) | collective-permute-done | bytes 458784 | tf_op jit(solution)/shard_map/ppermute | solution.py:32
  63.7 1.2 collective-permute-start.13
  64.9 0.4 collective-permute-start.11
  65.3 2.1 collective-permute-start.16
  67.6 7.9 %collective-permute-done.13.refs_4_ = bf16[4,32,1792]{2,1,0:T(8,128)(2,1)} collective-permute-done((bf16[4,32,1792]{2,1,0:T(8,128)(2,1)S(1)}, bf16[4,32,1792]{2,1,0:T(8,128)(2,1)}, u32[]{:S(2)}, u32[]{:S(2)}) %collective-permute-start.13) | collective-permute-done | bytes 458784 | tf_op jit(solution)/shard_map/ppermute | solution.py:32
  75.5 1.2 collective-permute-start.14
  76.7 10.3 %collective-permute-done.12.refs_2_ = bf16[4,32,1792]{2,1,0:T(8,128)(2,1)S(1)} collective-permute-done((bf16[4,32,1792]{2,1,0:T(8,128)(2,1)}, bf16[4,32,1792]{2,1,0:T(8,128)(2,1)S(1)}, u32[]{:S(2)}, u32[]{:S(2)}) %collective-permute-start.12) | collective-permute-done | bytes 458784 | tf_op jit(solution)/shard_map/ppermute | solution.py:55
  87.0 1.8 collective-permute-start.18
  89.0 1.0 copy-done.3
  90.0 0.4 collective-permute-start.20
  90.8 2.6 %collective-permute-start.23 = (bf16[4,32,1792]{2,1,0:T(8,128)(2,1)}, bf16[4,32,1792]{2,1,0:T(8,128)(2,1)S(1)}, u32[]{:S(2)}, u32[]{:S(2)}) collective-permute-start(bf16[4,32,1792]{2,1,0:T(8,128)(2,1)} %collective-permute-done.13.refs_4_), channel_id=1, source_target_pairs={{0,129},{8,137},{16,145},{24,153},{32,161},{40,169},{48,177},{56,1... | collective-permute-start | bytes 1376264 | tf_op jit(solution)/shard_map/ppermute | solution.py:55
  93.4 0.6 collective-permute-start.24
  94.0 0.6 pad_add_fusion.place
  94.6 0.6 broadcast_in_dim.12.refs_13_.refs_14_
  95.2 12.6 %shard_map.55 = (bf16[4,4,256,1792]{3,2,1,0:T(8,128)(2,1)}, f32[4096,512]{1,0:T(8,128)}, f32[16,1,256]{2,1,0:T(1,128)}, f32[16,1,256]{2,1,0:T(1,128)}) custom-call(s32[4]{0:T(128)} %pad_add_fusion.place, bf16[8,32,1792]{2,1,0:T(8,128)(2,1)} %copy-done.13, bf16[8,32,1792]{2,1,0:T(8,128)(2,1)} %copy-done, bf16[4,32,1792]{2,1,0:T(8,128)(2,1)} %collective-permute-done.8.refs_2_, ...), custom_call_target="tpu_custom_call" | custom-call | flops 3758096384 | bytes 20709376 | tf_op jit(solution)/shard_map/pallas_call | solution.py:174
  107.7 3.5 %collective-permute-done.22.refs_3_ = bf16[4,32,1792]{2,1,0:T(8,128)(2,1)S(1)} collective-permute-done((bf16[4,32,1792]{2,1,0:T(8,128)(2,1)}, bf16[4,32,1792]{2,1,0:T(8,128)(2,1)S(1)}, u32[]{:S(2)}, u32[]{:S(2)}) %collective-permute-start.22) | collective-permute-done | bytes 458784 | tf_op jit(solution)/shard_map/ppermute | solution.py:55
  111.2 2.4 %collective-permute-done.24.refs_5_ = bf16[4,32,1792]{2,1,0:T(8,128)(2,1)S(1)} collective-permute-done((bf16[4,32,1792]{2,1,0:T(8,128)(2,1)}, bf16[4,32,1792]{2,1,0:T(8,128)(2,1)S(1)}, u32[]{:S(2)}, u32[]{:S(2)}) %collective-permute-start.24) | collective-permute-done | bytes 458784 | tf_op jit(solution)/shard_map/ppermute | solution.py:55
  113.5 1.4 collective-permute-start.25
  115.0 0.4 collective-permute-start.27
  115.6 0.4 collective-permute-start.29
  116.0 1.7 collective-permute-done.26.refs_8_
  117.7 0.7 collective-permute-done.27.refs_9_
  118.4 0.7 collective-permute-done.28.refs_10_
  119.0 0.7 collective-permute-done.29.refs_11_
  119.8 0.7 copy-done.12
  120.5 1.0 copy-done.4
  121.4 12.6 %shard_map.56 = (bf16[4,4,256,1792]{3,2,1,0:T(8,128)(2,1)}, f32[4096,512]{1,0:T(8,128)}, f32[16,1,256]{2,1,0:T(1,128)}, f32[16,1,256]{2,1,0:T(1,128)}) custom-call(s32[4]{0:T(128)} %pad_add_fusion.place, bf16[8,32,1792]{2,1,0:T(8,128)(2,1)} %copy-done.2, bf16[8,32,1792]{2,1,0:T(8,128)(2,1)} %copy-done.1, ...), custom_call_target="tpu_custom_call", output_to_operand_aliasing={{0}: (16, {}), {1}: (17, {})} | custom-call | flops 3758096384 | bytes 20709376 | tf_op jit(solution)/shard_map/pallas_call | solution.py:174
  134.1 0.7 log_add_fusion.1
  134.8 0.9 broadcast_in_dim.13
  135.7 8.4 %all-to-all-start.1 = ((f32[16,1,4096]{2,1,0:T(1,128)}), f32[16,1,4096]{2,1,0:T(1,128)S(1)}, u32[]{:S(2)}, u32[]{:S(2)}) async-start(f32[16,1,4096]{2,1,0:T(1,128)} %broadcast_in_dim.13), calls=%async_computation.1 | async-start | bytes 524288 | tf_op jit(solution)/shard_map/all_to_all | solution.py:268
  144.3 0.6 gather_fusion.1
  144.9 0.6 copy.23
  145.5 12.7 %shard_map.57 = bf16[4096,512]{1,0:T(8,128)(2,1)} custom-call(s32[4096]{0:T(1024)} %bitcast.91, bf16[4096,512]{1,0:T(8,128)(2,1)} %bitcast.33.teacher), custom_call_target="tpu_custom_call" | custom-call | bytes 41943040 | tf_op jit(solution)/shard_map/pallas_call | solution.py:239
  158.7 13.5 %all_to_all.35 = f32[16,1,4096]{2,1,0:T(1,128)S(1)} all-to-all(f32[16,1,4096]{2,1,0:T(1,128)S(1)} %broadcast_in_dim.14), channel_id=1, replica_groups={{0,1,2,3,4,5,6,7,128,129,130,131,132,133,134,135},{8,9,10,11,12,13,14,1..., dimensions={0} | all-to-all | bytes 524288 | tf_op jit(solution)/shard_map/all_to_all | solution.py:268
  172.4 0.6 gather_fusion.2
  173.2 0.6 gather_fusion.3
  173.8 7.5 %multiply_reduce_fusion = f32[4096]{0:T(1024)S(1)} fusion(f32[4096,512]{1,0:T(8,128)} %get-tuple-element.65, bf16[4096,512]{1,0:T(8,128)(2,1)} %shard_map.57, f32[4096]{0:T(1024)S(1)} %bitcast.89, f32[4096]{0:T(1024)S(1)} %bitcast.87), kind=kLoop, calls=%fused_computation.7 | loop fusion | flops 18870272 | bytes 12632064 | tf_op jit(solution)/shard_map/reduce_sum | solution.py:301
  181.4 0.6 gather_fusion.4
  182.0 0.9 broadcast_in_dim.16
  182.9 8.7 %all-to-all-start.3 = ((f32[16,1,4096]{2,1,0:T(1,128)}), f32[16,1,4096]{2,1,0:T(1,128)S(1)}, u32[]{:S(2)}, u32[]{:S(2)}) async-start(f32[16,1,4096]{2,1,0:T(1,128)} %broadcast_in_dim.16), calls=%async_computation.3 | async-start | bytes 524288 | tf_op jit(solution)/shard_map/all_to_all | solution.py:268
  191.7 11.6 %all-to-all-done.3 = f32[16,1,4096]{2,1,0:T(1,128)S(1)} async-done(((f32[16,1,4096]{2,1,0:T(1,128)}), f32[16,1,4096]{2,1,0:T(1,128)S(1)}, u32[]{:S(2)}, u32[]{:S(2)}) %all-to-all-start.3) | async-done | bytes 262176 | tf_op jit(solution)/shard_map/all_to_all | solution.py:268
  203.5 0.9 broadcast_in_dim.17
  204.4 3.5 %all-to-all-start.4 = ((f32[16,1,4096]{2,1,0:T(1,128)}), f32[16,1,4096]{2,1,0:T(1,128)S(1)}, u32[]{:S(2)}, u32[]{:S(2)}) async-start(f32[16,1,4096]{2,1,0:T(1,128)} %broadcast_in_dim.17), calls=%async_computation.4 | async-start | bytes 524288 | tf_op jit(solution)/shard_map/all_to_all | solution.py:268
  208.0 0.6 reduce_sum.54
  208.6 0.6 gather_fusion
  209.8 6.8 %all-to-all-done.4 = f32[16,1,4096]{2,1,0:T(1,128)S(1)} async-done(((f32[16,1,4096]{2,1,0:T(1,128)}), f32[16,1,4096]{2,1,0:T(1,128)S(1)}, u32[]{:S(2)}, u32[]{:S(2)}) %all-to-all-start.4) | async-done | bytes 262176 | tf_op jit(solution)/shard_map/all_to_all | solution.py:268
  216.8 0.6 gather_fusion.5
  217.4 15.5 %fusion.2 = bf16[1792,512]{1,0:T(8,128)(2,1)} fusion(bf16[4096,1792]{1,0:T(8,128)(2,1)} %bitcast.83, f32[4096,512]{1,0:T(8,128)} %get-tuple-element.65, bf16[4096,512]{1,0:T(8,128)(2,1)} %shard_map.57, f32[4096]{0:T(1024)S(1)} %bitcast.102, f32[4096]{0:T(1024)S(1)} %bitcast.90, f32[4096]{0:T(1024)S(1)} %bitcast.88, f32[4096]{0:T(1024)S(1)} %bitcast.101), kind=kOutput, calls=%fused_computation.13 | convolution fusion | flops 7540178944 | bytes 29163520 | tf_op jit(solution)/shard_map/dot_general | solution.py:313
  (99 shorter events, 3.0 us)
Async XLA Ops:
  0.9 11.4 %collective-permute-start = (bf16[32,1792]{1,0:T(8,128)(2,1)S(1)}, bf16[32,1792]{1,0:T(8,128)(2,1)S(1)}, u32[]{:S(2)}, u32[]{:S(2)}) collective-permute-start(bf16[32,1792]{1,0:T(8,128)(2,1)S(1)} %get-tuple-element.74), channel_id=1, source_target_pairs={{0,16},{8,24},{16,32},{24,40},{32,48},{40,56},{48,64},{56,72},{64,... | collective-permute-start | bytes 344072 | tf_op jit(solution)/shard_map/ppermute | solution.py:32
  3.5 8.8 %collective-permute-start.4 = (bf16[32,1792]{1,0:T(8,128)(2,1)S(1)}, bf16[32,1792]{1,0:T(8,128)(2,1)S(1)}, u32[]{:S(2)}, u32[]{:S(2)}) collective-permute-start(bf16[32,1792]{1,0:T(8,128)(2,1)S(1)} %get-tuple-element.74), channel_id=1, source_target_pairs={{0,112},{8,120},{16,0},{24,8},{32,16},{40,24},{48,32},{56,40},{64,... | collective-permute-start | bytes 344072 | tf_op jit(solution)/shard_map/ppermute | solution.py:32
  12.3 4.9 %collective-permute-start.1 = (bf16[32,1792]{1,0:T(8,128)(2,1)S(1)}, bf16[32,1792]{1,0:T(8,128)(2,1)S(1)}, u32[]{:S(2)}, u32[]{:S(2)}) collective-permute-start(bf16[32,1792]{1,0:T(8,128)(2,1)S(1)} %collective-permute-done), channel_id=1, source_target_pairs={{0,16},{8,24},{16,32},{24,40},{32,48},{40,56},{48,64},{56,72},{64,... | collective-permute-start | bytes 344072 | tf_op jit(solution)/shard_map/ppermute | solution.py:32
  12.3 4.8 %collective-permute-start.5 = (bf16[32,1792]{1,0:T(8,128)(2,1)S(1)}, bf16[32,1792]{1,0:T(8,128)(2,1)S(1)}, u32[]{:S(2)}, u32[]{:S(2)}) collective-permute-start(bf16[32,1792]{1,0:T(8,128)(2,1)S(1)} %collective-permute-done.4), channel_id=1, source_target_pairs={{0,112},{8,120},{16,0},{24,8},{32,16},{40,24},{48,32},{56,40},{64,... | collective-permute-start | bytes 344072 | tf_op jit(solution)/shard_map/ppermute | solution.py:32
  17.1 4.9 %collective-permute-start.2 = (bf16[32,1792]{1,0:T(8,128)(2,1)S(1)}, bf16[32,1792]{1,0:T(8,128)(2,1)S(1)}, u32[]{:S(2)}, u32[]{:S(2)}) collective-permute-start(bf16[32,1792]{1,0:T(8,128)(2,1)S(1)} %collective-permute-done.1), channel_id=1, source_target_pairs={{0,16},{8,24},{16,32},{24,40},{32,48},{40,56},{48,64},{56,72},{64,... | collective-permute-start | bytes 344072 | tf_op jit(solution)/shard_map/ppermute | solution.py:32
  17.2 9.7 %collective-permute-start.6 = (bf16[32,1792]{1,0:T(8,128)(2,1)S(1)}, bf16[32,1792]{1,0:T(8,128)(2,1)S(1)}, u32[]{:S(2)}, u32[]{:S(2)}) collective-permute-start(bf16[32,1792]{1,0:T(8,128)(2,1)S(1)} %collective-permute-done.5), channel_id=1, source_target_pairs={{0,112},{8,120},{16,0},{24,8},{32,16},{40,24},{48,32},{56,40},{64,... | collective-permute-start | bytes 344072 | tf_op jit(solution)/shard_map/ppermute | solution.py:32
  22.0 4.9 %collective-permute-start.3 = (bf16[32,1792]{1,0:T(8,128)(2,1)S(1)}, bf16[32,1792]{1,0:T(8,128)(2,1)S(1)}, u32[]{:S(2)}, u32[]{:S(2)}) collective-permute-start(bf16[32,1792]{1,0:T(8,128)(2,1)S(1)} %collective-permute-done.2), channel_id=1, source_target_pairs={{0,16},{8,24},{16,32},{24,40},{32,48},{40,56},{48,64},{56,72},{64,... | collective-permute-start | bytes 344072 | tf_op jit(solution)/shard_map/ppermute | solution.py:32
  26.9 68.2 %copy-start = (bf16[8,32,1792]{2,1,0:T(8,128)(2,1)}, bf16[8,32,1792]{2,1,0:T(8,128)(2,1)S(1)}, u32[]{:S(2)}) copy-start(bf16[8,32,1792]{2,1,0:T(8,128)(2,1)S(1)} %bitcast_dynamic-update-slice_fusion.refs_1_) | copy-start | bytes 2752516
  26.9 107.9 %all-to-all-start = ((bf16[32,128,512]{2,1,0:T(8,128)(2,1)}), bf16[32,128,512]{2,1,0:T(8,128)(2,1)}, u32[]{:S(2)}, u32[]{:S(2)}) async-start(bf16[32,128,512]{2,1,0:T(8,128)(2,1)} %bitcast.82), calls=%async_computation | async-start | bytes 8388608 | tf_op jit(solution)/shard_map/all_to_all | solution.py:282
  38.2 25.2 %collective-permute-start.10 = (bf16[8,32,1792]{2,1,0:T(8,128)(2,1)S(1)}, bf16[8,32,1792]{2,1,0:T(8,128)(2,1)S(1)}, u32[]{:S(2)}, u32[]{:S(2)}) collective-permute-start(bf16[8,32,1792]{2,1,0:T(8,128)(2,1)S(1)} %bitcast_dynamic-update-slice_fusion.refs_1_), channel_id=1, source_target_pairs={{0,129},{8,137},{16,145},{24,153},{32,161},{40,169},{48,177},{56,1... | collective-permute-start | bytes 2752520 | tf_op jit(solution)/shard_map/ppermute | solution.py:55
  41.0 22.7 %collective-permute-start.7 = (bf16[8,32,1792]{2,1,0:T(8,128)(2,1)S(1)}, bf16[8,32,1792]{2,1,0:T(8,128)(2,1)S(1)}, u32[]{:S(2)}, u32[]{:S(2)}) collective-permute-start(bf16[8,32,1792]{2,1,0:T(8,128)(2,1)S(1)} %bitcast_dynamic-update-slice_fusion.refs_1_), channel_id=1, source_target_pairs={{0,2},{8,10},{16,18},{24,26},{32,34},{40,42},{48,50},{56,58},{64,6... | collective-permute-start | bytes 2752520 | tf_op jit(solution)/shard_map/ppermute | solution.py:32
  42.4 11.3 %collective-permute-start.8 = (bf16[4,32,1792]{2,1,0:T(8,128)(2,1)S(1)}, bf16[4,32,1792]{2,1,0:T(8,128)(2,1)}, u32[]{:S(2)}, u32[]{:S(2)}) collective-permute-start(bf16[4,32,1792]{2,1,0:T(8,128)(2,1)S(1)} %get-tuple-element.76), channel_id=1, source_target_pairs={{0,6},{8,14},{16,22},{24,30},{32,38},{40,46},{48,54},{56,62},{64,7... | collective-permute-start | bytes 1376264 | tf_op jit(solution)/shard_map/ppermute | solution.py:32
  43.9 19.6 %collective-permute-start.9 = (bf16[4,32,1792]{2,1,0:T(8,128)(2,1)S(1)}, bf16[4,32,1792]{2,1,0:T(8,128)(2,1)}, u32[]{:S(2)}, u32[]{:S(2)}) collective-permute-start(bf16[4,32,1792]{2,1,0:T(8,128)(2,1)S(1)} %get-tuple-element.75), channel_id=1, source_target_pairs={{0,6},{8,14},{16,22},{24,30},{32,38},{40,46},{48,54},{56,62},{64,7... | collective-permute-start | bytes 1376264 | tf_op jit(solution)/shard_map/ppermute | solution.py:32
  45.3 22.1 %collective-permute-start.15 = (bf16[8,32,1792]{2,1,0:T(8,128)(2,1)S(1)}, bf16[8,32,1792]{2,1,0:T(8,128)(2,1)S(1)}, u32[]{:S(2)}, u32[]{:S(2)}) collective-permute-start(bf16[8,32,1792]{2,1,0:T(8,128)(2,1)S(1)} %bitcast_dynamic-update-slice_fusion.refs_1_), channel_id=1, source_target_pairs={{0,8},{8,0},{16,24},{24,16},{32,40},{40,32},{48,56},{56,48},{64,72... | collective-permute-start | bytes 2752520 | tf_op jit(solution)/shard_map/ppermute | solution.py:32
  63.5 56.2 %copy-start.1 = (bf16[8,32,1792]{2,1,0:T(8,128)(2,1)}, bf16[8,32,1792]{2,1,0:T(8,128)(2,1)S(1)}, u32[]{:S(2)}) copy-start(bf16[8,32,1792]{2,1,0:T(8,128)(2,1)S(1)} %collective-permute-done.10.refs_1_) | copy-start | bytes 2752516
  63.7 26.7 %copy-start.13 = (bf16[8,32,1792]{2,1,0:T(8,128)(2,1)}, bf16[8,32,1792]{2,1,0:T(8,128)(2,1)S(1)}, u32[]{:S(2)}) copy-start(bf16[8,32,1792]{2,1,0:T(8,128)(2,1)S(1)} %collective-permute-done.7.refs_0_) | copy-start | bytes 2752516
  63.7 11.8 %collective-permute-start.13 = (bf16[4,32,1792]{2,1,0:T(8,128)(2,1)S(1)}, bf16[4,32,1792]{2,1,0:T(8,128)(2,1)}, u32[]{:S(2)}, u32[]{:S(2)}) collective-permute-start(bf16[4,32,1792]{2,1,0:T(8,128)(2,1)S(1)} %slice.11), channel_id=1, source_target_pairs={{0,2},{8,10},{16,18},{24,26},{32,34},{40,42},{48,50},{56,58},{64,6... | collective-permute-start | bytes 1376264 | tf_op jit(solution)/shard_map/ppermute | solution.py:32
  64.9 24.0 %collective-permute-start.11 = (bf16[8,32,1792]{2,1,0:T(8,128)(2,1)S(1)}, bf16[8,32,1792]{2,1,0:T(8,128)(2,1)S(1)}, u32[]{:S(2)}, u32[]{:S(2)}) collective-permute-start(bf16[8,32,1792]{2,1,0:T(8,128)(2,1)S(1)} %collective-permute-done.7.refs_0_), channel_id=1, source_target_pairs={{0,129},{8,137},{16,145},{24,153},{32,161},{40,169},{48,177},{56,1... | collective-permute-start | bytes 2752520 | tf_op jit(solution)/shard_map/ppermute | solution.py:55
  65.3 23.6 %collective-permute-start.16 = (bf16[8,32,1792]{2,1,0:T(8,128)(2,1)S(1)}, bf16[8,32,1792]{2,1,0:T(8,128)(2,1)S(1)}, u32[]{:S(2)}, u32[]{:S(2)}) collective-permute-start(bf16[8,32,1792]{2,1,0:T(8,128)(2,1)S(1)} %collective-permute-done.7.refs_0_), channel_id=1, source_target_pairs={{0,8},{8,0},{16,24},{24,16},{32,40},{40,32},{48,56},{56,48},{64,72... | collective-permute-start | bytes 2752520 | tf_op jit(solution)/shard_map/ppermute | solution.py:32
  67.4 21.5 %collective-permute-start.17 = (bf16[8,32,1792]{2,1,0:T(8,128)(2,1)S(1)}, bf16[8,32,1792]{2,1,0:T(8,128)(2,1)S(1)}, u32[]{:S(2)}, u32[]{:S(2)}) collective-permute-start(bf16[8,32,1792]{2,1,0:T(8,128)(2,1)S(1)} %collective-permute-done.10.refs_1_), channel_id=1, source_target_pairs={{0,8},{8,0},{16,24},{24,16},{32,40},{40,32},{48,56},{56,48},{64,72... | collective-permute-start | bytes 2752520 | tf_op jit(solution)/shard_map/ppermute | solution.py:32
  67.4 23.0 %copy-start.16 = (bf16[8,32,1792]{2,1,0:T(8,128)(2,1)}, bf16[8,32,1792]{2,1,0:T(8,128)(2,1)S(1)}, u32[]{:S(2)}) copy-start(bf16[8,32,1792]{2,1,0:T(8,128)(2,1)S(1)} %collective-permute-done.15.refs_7_) | copy-start | bytes 2752516
  67.4 19.6 %collective-permute-start.12 = (bf16[4,32,1792]{2,1,0:T(8,128)(2,1)}, bf16[4,32,1792]{2,1,0:T(8,128)(2,1)S(1)}, u32[]{:S(2)}, u32[]{:S(2)}) collective-permute-start(bf16[4,32,1792]{2,1,0:T(8,128)(2,1)} %collective-permute-done.8.refs_2_), channel_id=1, source_target_pairs={{0,128},{8,136},{16,144},{24,152},{32,160},{40,168},{48,176},{56,1... | collective-permute-start | bytes 1376264 | tf_op jit(solution)/shard_map/ppermute | solution.py:55
  75.5 13.3 %collective-permute-start.14 = (bf16[4,32,1792]{2,1,0:T(8,128)(2,1)}, bf16[4,32,1792]{2,1,0:T(8,128)(2,1)}, u32[]{:S(2)}, u32[]{:S(2)}) collective-permute-start(bf16[4,32,1792]{2,1,0:T(8,128)(2,1)} %collective-permute-done.9.refs_3_), channel_id=1, source_target_pairs={{0,6},{8,14},{16,22},{24,30},{32,38},{40,46},{48,54},{56,62},{64,7... | collective-permute-start | bytes 1376264 | tf_op jit(solution)/shard_map/ppermute | solution.py:32
  87.0 32.7 %copy-start.5 = (bf16[4,32,1792]{2,1,0:T(8,128)(2,1)}, bf16[4,32,1792]{2,1,0:T(8,128)(2,1)S(1)}, u32[]{:S(2)}) copy-start(bf16[4,32,1792]{2,1,0:T(8,128)(2,1)S(1)} %collective-permute-done.12.refs_2_) | copy-start | bytes 1376260
  87.0 3.7 %collective-permute-start.18 = (bf16[4,32,1792]{2,1,0:T(8,128)(2,1)}, bf16[4,32,1792]{2,1,0:T(8,128)(2,1)}, u32[]{:S(2)}, u32[]{:S(2)}) collective-permute-start(bf16[4,32,1792]{2,1,0:T(8,128)(2,1)} %collective-permute-done.8.refs_2_), channel_id=1, source_target_pairs={{0,8},{8,0},{16,24},{24,16},{32,40},{40,32},{48,56},{56,48},{64,72... | collective-permute-start | bytes 1376264 | tf_op jit(solution)/shard_map/ppermute | solution.py:32
  88.8 4.6 %collective-permute-start.19 = (bf16[4,32,1792]{2,1,0:T(8,128)(2,1)}, bf16[4,32,1792]{2,1,0:T(8,128)(2,1)}, u32[]{:S(2)}, u32[]{:S(2)}) collective-permute-start(bf16[4,32,1792]{2,1,0:T(8,128)(2,1)} %collective-permute-done.9.refs_3_), channel_id=1, source_target_pairs={{0,8},{8,0},{16,24},{24,16},{32,40},{40,32},{48,56},{56,48},{64,72... | collective-permute-start | bytes 1376264 | tf_op jit(solution)/shard_map/ppermute | solution.py:32
  88.9 30.8 %copy-start.2 = (bf16[8,32,1792]{2,1,0:T(8,128)(2,1)}, bf16[8,32,1792]{2,1,0:T(8,128)(2,1)S(1)}, u32[]{:S(2)}) copy-start(bf16[8,32,1792]{2,1,0:T(8,128)(2,1)S(1)} %collective-permute-done.11.refs_0_) | copy-start | bytes 2752516
  88.9 1.5 copy-start.17
  88.9 1.0 copy-start.3
  90.0 4.6 %collective-permute-start.20 = (bf16[4,32,1792]{2,1,0:T(8,128)(2,1)}, bf16[4,32,1792]{2,1,0:T(8,128)(2,1)}, u32[]{:S(2)}, u32[]{:S(2)}) collective-permute-start(bf16[4,32,1792]{2,1,0:T(8,128)(2,1)} %collective-permute-done.13.refs_4_), channel_id=1, source_target_pairs={{0,8},{8,0},{16,24},{24,16},{32,40},{40,32},{48,56},{56,48},{64,72... | collective-permute-start | bytes 1376264 | tf_op jit(solution)/shard_map/ppermute | solution.py:32
  90.4 4.2 %collective-permute-start.21 = (bf16[4,32,1792]{2,1,0:T(8,128)(2,1)}, bf16[4,32,1792]{2,1,0:T(8,128)(2,1)}, u32[]{:S(2)}, u32[]{:S(2)}) collective-permute-start(bf16[4,32,1792]{2,1,0:T(8,128)(2,1)} %collective-permute-done.14.refs_5_), channel_id=1, source_target_pairs={{0,8},{8,0},{16,24},{24,16},{32,40},{40,32},{48,56},{56,48},{64,72... | collective-permute-start | bytes 1376264 | tf_op jit(solution)/shard_map/ppermute | solution.py:32
  90.6 20.6 %collective-permute-start.22 = (bf16[4,32,1792]{2,1,0:T(8,128)(2,1)}, bf16[4,32,1792]{2,1,0:T(8,128)(2,1)S(1)}, u32[]{:S(2)}, u32[]{:S(2)}) collective-permute-start(bf16[4,32,1792]{2,1,0:T(8,128)(2,1)} %collective-permute-done.9.refs_3_), channel_id=1, source_target_pairs={{0,128},{8,136},{16,144},{24,152},{32,160},{40,168},{48,176},{56,1... | collective-permute-start | bytes 1376264 | tf_op jit(solution)/shard_map/ppermute | solution.py:55
  90.8 20.4 %collective-permute-start.23 = (bf16[4,32,1792]{2,1,0:T(8,128)(2,1)}, bf16[4,32,1792]{2,1,0:T(8,128)(2,1)S(1)}, u32[]{:S(2)}, u32[]{:S(2)}) collective-permute-start(bf16[4,32,1792]{2,1,0:T(8,128)(2,1)} %collective-permute-done.13.refs_4_), channel_id=1, source_target_pairs={{0,129},{8,137},{16,145},{24,153},{32,161},{40,169},{48,177},{56,1... | collective-permute-start | bytes 1376264 | tf_op jit(solution)/shard_map/ppermute | solution.py:55
  93.4 20.1 %collective-permute-start.24 = (bf16[4,32,1792]{2,1,0:T(8,128)(2,1)}, bf16[4,32,1792]{2,1,0:T(8,128)(2,1)S(1)}, u32[]{:S(2)}, u32[]{:S(2)}) collective-permute-start(bf16[4,32,1792]{2,1,0:T(8,128)(2,1)} %collective-permute-done.14.refs_5_), channel_id=1, source_target_pairs={{0,129},{8,137},{16,145},{24,153},{32,161},{40,169},{48,177},{56,1... | collective-permute-start | bytes 1376264 | tf_op jit(solution)/shard_map/ppermute | solution.py:55
  111.2 8.5 %copy-start.6 = (bf16[4,32,1792]{2,1,0:T(8,128)(2,1)}, bf16[4,32,1792]{2,1,0:T(8,128)(2,1)S(1)}, u32[]{:S(2)}) copy-start(bf16[4,32,1792]{2,1,0:T(8,128)(2,1)S(1)} %collective-permute-done.22.refs_3_) | copy-start | bytes 1376260
  111.2 8.5 %copy-start.7 = (bf16[4,32,1792]{2,1,0:T(8,128)(2,1)}, bf16[4,32,1792]{2,1,0:T(8,128)(2,1)S(1)}, u32[]{:S(2)}) copy-start(bf16[4,32,1792]{2,1,0:T(8,128)(2,1)S(1)} %collective-permute-done.23.refs_4_) | copy-start | bytes 1376260
  113.5 6.2 %copy-start.8 = (bf16[4,32,1792]{2,1,0:T(8,128)(2,1)}, bf16[4,32,1792]{2,1,0:T(8,128)(2,1)S(1)}, u32[]{:S(2)}) copy-start(bf16[4,32,1792]{2,1,0:T(8,128)(2,1)S(1)} %collective-permute-done.24.refs_5_) | copy-start | bytes 1376260
  113.5 30.6 %copy-start.14 = (s32[4096]{0:T(1024)S(1)}, s32[4096]{0:T(1024)}, u32[]{:S(2)}) copy-start(s32[4096]{0:T(1024)} %param.8) | copy-start | bytes 49156
  113.5 6.1 %collective-permute-start.25 = (bf16[8,32,1792]{2,1,0:T(8,128)(2,1)S(1)}, bf16[8,32,1792]{2,1,0:T(8,128)(2,1)S(1)}, u32[]{:S(2)}, u32[]{:S(2)}) collective-permute-start(bf16[8,32,1792]{2,1,0:T(8,128)(2,1)S(1)} %collective-permute-done.11.refs_0_), channel_id=1, source_target_pairs={{0,8},{8,0},{16,24},{24,16},{32,40},{40,32},{48,56},{56,48},{64,72... | collective-permute-start | bytes 2752520 | tf_op jit(solution)/shard_map/ppermute | solution.py:32
  115.0 2.8 %collective-permute-start.26 = (bf16[4,32,1792]{2,1,0:T(8,128)(2,1)S(1)}, bf16[4,32,1792]{2,1,0:T(8,128)(2,1)S(1)}, u32[]{:S(2)}, u32[]{:S(2)}) collective-permute-start(bf16[4,32,1792]{2,1,0:T(8,128)(2,1)S(1)} %collective-permute-done.12.refs_2_), channel_id=1, source_target_pairs={{0,8},{8,0},{16,24},{24,16},{32,40},{40,32},{48,56},{56,48},{64,72... | collective-permute-start | bytes 1376264 | tf_op jit(solution)/shard_map/ppermute | solution.py:32
  115.0 3.3 %collective-permute-start.27 = (bf16[4,32,1792]{2,1,0:T(8,128)(2,1)S(1)}, bf16[4,32,1792]{2,1,0:T(8,128)(2,1)S(1)}, u32[]{:S(2)}, u32[]{:S(2)}) collective-permute-start(bf16[4,32,1792]{2,1,0:T(8,128)(2,1)S(1)} %collective-permute-done.22.refs_3_), channel_id=1, source_target_pairs={{0,8},{8,0},{16,24},{24,16},{32,40},{40,32},{48,56},{56,48},{64,72... | collective-permute-start | bytes 1376264 | tf_op jit(solution)/shard_map/ppermute | solution.py:32
  115.5 3.6 %collective-permute-start.28 = (bf16[4,32,1792]{2,1,0:T(8,128)(2,1)S(1)}, bf16[4,32,1792]{2,1,0:T(8,128)(2,1)S(1)}, u32[]{:S(2)}, u32[]{:S(2)}) collective-permute-start(bf16[4,32,1792]{2,1,0:T(8,128)(2,1)S(1)} %collective-permute-done.23.refs_4_), channel_id=1, source_target_pairs={{0,8},{8,0},{16,24},{24,16},{32,40},{40,32},{48,56},{56,48},{64,72... | collective-permute-start | bytes 1376264 | tf_op jit(solution)/shard_map/ppermute | solution.py:32
  115.6 4.1 %collective-permute-start.29 = (bf16[4,32,1792]{2,1,0:T(8,128)(2,1)S(1)}, bf16[4,32,1792]{2,1,0:T(8,128)(2,1)S(1)}, u32[]{:S(2)}, u32[]{:S(2)}) collective-permute-start(bf16[4,32,1792]{2,1,0:T(8,128)(2,1)S(1)} %collective-permute-done.24.refs_5_), channel_id=1, source_target_pairs={{0,8},{8,0},{16,24},{24,16},{32,40},{40,32},{48,56},{56,48},{64,72... | collective-permute-start | bytes 1376264 | tf_op jit(solution)/shard_map/ppermute | solution.py:32
  117.7 2.0 copy-start.9
  118.4 1.4 copy-start.10
  119.0 0.8 copy-start.11
  119.7 0.8 copy-start.12
  120.5 1.0 copy-start.4
  135.7 22.5 %all-to-all-start.1 = ((f32[16,1,4096]{2,1,0:T(1,128)}), f32[16,1,4096]{2,1,0:T(1,128)S(1)}, u32[]{:S(2)}, u32[]{:S(2)}) async-start(f32[16,1,4096]{2,1,0:T(1,128)} %broadcast_in_dim.13), calls=%async_computation.1 | async-start | bytes 524288 | tf_op jit(solution)/shard_map/all_to_all | solution.py:268
  158.2 33.4 %copy-start.15 = (s32[32]{0:T(128)S(1)}, s32[32]{0:T(128)}, u32[]{:S(2)}) copy-start(s32[32]{0:T(128)} %param.9) | copy-start | bytes 388
  182.9 20.4 %all-to-all-start.3 = ((f32[16,1,4096]{2,1,0:T(1,128)}), f32[16,1,4096]{2,1,0:T(1,128)S(1)}, u32[]{:S(2)}, u32[]{:S(2)}) async-start(f32[16,1,4096]{2,1,0:T(1,128)} %broadcast_in_dim.16), calls=%async_computation.3 | async-start | bytes 524288 | tf_op jit(solution)/shard_map/all_to_all | solution.py:268
  204.4 12.2 %all-to-all-start.4 = ((f32[16,1,4096]{2,1,0:T(1,128)}), f32[16,1,4096]{2,1,0:T(1,128)S(1)}, u32[]{:S(2)}, u32[]{:S(2)}) async-start(f32[16,1,4096]{2,1,0:T(1,128)} %broadcast_in_dim.17), calls=%async_computation.4 | async-start | bytes 524288 | tf_op jit(solution)/shard_map/all_to_all | solution.py:268

commit v2 on v1

--- a/solution.py
+++ b/solution.py
@@ -63,11 +63,11 @@
     return tuple(hop(array, flip=1) for array in arrays)
 
 
-def gather_logits(place, here, weight):
+def gather_logits(place, here, weight, early):
     prev, cross_here = hop(here, dy=1), cross(here, near=False)
     next_a, next_b = hop(here[:4], dy=-1), hop(here[4:], dy=-1)
 
-    prev, next_a, next_b, cross_here = tie(prev, next_a, next_b, cross_here)
+    prev, next_a, next_b, cross_here, early = tie(prev, next_a, next_b, cross_here, early)
     cross_prev, cross_next_a = cross(prev, near=False), cross(next_a, near=True)
     far_a, far_b = hop(prev[:4], dy=1), hop(next_b, dy=-1)
     here_flip, prev_flip, cross_here_flip = flip_all((here, prev, cross_here))
@@ -85,7 +85,7 @@
     rest_flip = flip_all(rest)
     crossed = (rest[0], cross_here) + rest[1:]
     crossed_flip = (rest_flip[0], cross_here_flip) + rest_flip[1:]
-    return block_logits(place, crossed, crossed_flip, weight, 1, done)
+    return block_logits(place, crossed, crossed_flip, weight, 1, done), early
 
 
 def coords():
@@ -192,13 +192,13 @@
             ],
         ),
         out_shape=[
-            jax.ShapeDtypeStruct((4, 4, block, depth), jnp.bfloat16),
-            jax.ShapeDtypeStruct((blocks * block, width), jnp.float32),
+            pltpu.HBM((4, 4, block, depth), jnp.bfloat16),
+            pltpu.HBM((blocks * block, width), jnp.float32),
             stat,
             stat,
         ],
         input_output_aliases=aliases,
-        compiler_params=pltpu.CompilerParams(vmem_limit_bytes=56 * 1024 * 1024),
+        compiler_params=pltpu.CompilerParams(vmem_limit_bytes=28 * 1024 * 1024),
         cost_estimate=pl.CostEstimate(
             flops=blocks * block * depth * width,
             transcendentals=blocks * block * width // 2,
@@ -249,8 +249,8 @@
                 pltpu.SemaphoreType.DMA((8,)),
             ],
         ),
-        out_shape=jax.ShapeDtypeStruct((rows, width), jnp.bfloat16),
-        compiler_params=pltpu.CompilerParams(vmem_limit_bytes=56 * 1024 * 1024),
+        out_shape=pltpu.HBM((rows, width), jnp.bfloat16),
+        compiler_params=pltpu.CompilerParams(vmem_limit_bytes=20 * 1024 * 1024),
         cost_estimate=pl.CostEstimate(flops=0, transcendentals=0, bytes_accessed=10 * rows * width * 2),
     )(chosen, teacher)
 
@@ -278,16 +278,17 @@
         rows_all = hidden.shape[0] * tok
         here = spread_over_z(hidden)
         by_owner = teacher_probs.reshape(teacher_probs.shape[0], tok, -1).transpose(1, 0, 2)
+        place = coords()
+        chosen = to_local(teacher_row, place)
         here, by_owner = tie(here, by_owner)
         teacher = lax.all_to_all(by_owner, "tok", split_axis=0, concat_axis=0, tiled=True)
-        place = coords()
-        gathered, logits, local_peak, local_total = gather_logits(place, here, head_weight)
+        (gathered, logits, local_peak, local_total), chosen = gather_logits(place, here, head_weight, chosen)
         gathered = gathered.reshape(rows_all, -1)
         in_column = members(lambda x_lo, z, core, voc: (x_lo, voc))
         in_plane = members(lambda x_lo, z, core, voc: (z, core))
         log_total = local_peak.reshape(-1) + jnp.log(local_total.reshape(-1))
         log_total, teacher = tie(log_total, teacher)
-        aligned = take_rows(teacher.reshape(rows_all, -1), to_local(teacher_row, place))
+        aligned = take_rows(teacher.reshape(rows_all, -1), chosen)
         log_total = from_members(log_total, in_column)
         log_total, aligned = tie(log_total, aligned)
         aligned = aligned.astype(jnp.float32)
@@ -296,8 +297,7 @@
         row_peak, row_total = to_local(row_peak, place), to_local(row_total, place)
         log_student = logits - row_peak[:, None] - jnp.log(row_total)[:, None]
         student = jnp.exp(log_student)
-        log_mix = jnp.log(0.5 * aligned + 0.5 * student)
-        grad_prob = 0.5 * (log_student - log_mix)
+        grad_prob = 0.5 * (log_student - jnp.log(aligned + student))
         local_centre = jnp.sum(student * grad_prob, axis=1)
         centre = from_local(local_centre, place)
         centre = jnp.sum(from_members(centre, in_column), axis=0)

time: 234 us -> 231 us (0.987)
  waiting for transfers between devices: 72 us -> 77.1 us
  Pallas kernels: 37.9 us -> 33.6 us
    pallas_call x2, Pallas kernels: 25.2 us -> 21 us  [block_logits(): pl.pallas_call(functools.partial(logits_kernel, column), grid_spec=pltpu....]
    ppermute x6, waiting for transfers between devices: 16.2 us -> 20.1 us  [cross(): return lax.ppermute(array, AXES, pairs)]
    unnamed x51 -> x21, local copies, waits for them, and re-layouts: 4.52 us -> 1.21 us
  transfers between devices with their start and end apart: 34 -> 34, of which waited for: 16 -> 17; matrix products, arithmetic and copies ran while one was open for 4% -> 4% of each run, Pallas kernels for 16% -> 15%
where the time goes in v2:
time: 231 us; the launch traced here: 230 us
  waiting for transfers between devices  77.1 us (33%)
  starting transfers between devices  65.4 us (28%)
  Pallas kernels  33.6 us (15%)
  matrix products  15.3 us (7%)
  local copies, waits for them, and re-layouts  14.8 us (6%)
  blocking collectives  14 us (6%)
  other arithmetic  8.69 us (4%)
    ppermute x24, waiting for transfers between devices, hop(): return lax.ppermute(array, AXES, pairs)  38.2 us
    ppermute x24, starting transfers between devices, hop(): return lax.ppermute(array, AXES, pairs)  27 us
    all_to_all x3, starting transfers between devices, from_members(): lax.all_to_all(copies, AXES, split_axis=0, concat_axis=0, tiled=True, axi...  21.2 us
    pallas_call x2, Pallas kernels, block_logits(): pl.pallas_call(functools.partial(logits_kernel, column), grid_spec=pltpu....  21 us
    ppermute x6, waiting for transfers between devices, cross(): return lax.ppermute(array, AXES, pairs)  20.1 us
    all_to_all x3, waiting for transfers between devices, from_members(): lax.all_to_all(copies, AXES, split_axis=0, concat_axis=0, tiled=True, axi...  18.2 us
    dot_general x1, matrix products, per_device(): lax.dot_general(gathered, dlogits, (((0,), (0,)), ((), ())), preferred_el...  15.3 us
    all_to_all x1, blocking collectives, from_members(): lax.all_to_all(copies, AXES, split_axis=0, concat_axis=0, tiled=True, axi...  14 us
  transfers between devices with their start and end apart: 34, of which 17 were waited for; matrix products, arithmetic and copies ran while one was open for 4% of the time, Pallas kernels for 15%

profile of v2, /device:TPU:1, one launch (start us, length us, event | category | flops | bytes accessed | tf_op | source)
XLA Modules:
  0.0 230.0 jit_solution(7053105666478347132)
XLA Ops:
  0.0 0.9 bitcast_dynamic-update-slice_fusion.7
  0.9 2.5 %collective-permute-start = (bf16[32,1792]{1,0:T(8,128)(2,1)S(1)}, bf16[32,1792]{1,0:T(8,128)(2,1)S(1)}, u32[]{:S(2)}, u32[]{:S(2)}) collective-permute-start(bf16[32,1792]{1,0:T(8,128)(2,1)S(1)} %get-tuple-element.76), channel_id=1, source_target_pairs={{0,16},{8,24},{16,32},{24,40},{32,48},{40,56},{48,64},{56,72},{64,... | collective-permute-start | bytes 344072 | tf_op jit(solution)/shard_map/ppermute | solution.py:32
  3.5 4.0 %collective-permute-start.4 = (bf16[32,1792]{1,0:T(8,128)(2,1)S(1)}, bf16[32,1792]{1,0:T(8,128)(2,1)S(1)}, u32[]{:S(2)}, u32[]{:S(2)}) collective-permute-start(bf16[32,1792]{1,0:T(8,128)(2,1)S(1)} %get-tuple-element.76), channel_id=1, source_target_pairs={{0,112},{8,120},{16,0},{24,8},{32,16},{40,24},{48,32},{56,40},{64,... | collective-permute-start | bytes 344072 | tf_op jit(solution)/shard_map/ppermute | solution.py:32
  7.5 4.8 %copy.34 = bf16[16,32,8,512]{3,2,0,1:T(8,128)(2,1)} copy(bf16[16,32,8,512]{3,2,1,0:T(8,128)(2,1)} %bitcast.87) | data formatting | bytes 8388608 | tf_op jit(solution)/shard_map/reshape | solution.py:280
  12.4 2.7 %collective-permute-start.5 = (bf16[32,1792]{1,0:T(8,128)(2,1)S(1)}, bf16[32,1792]{1,0:T(8,128)(2,1)S(1)}, u32[]{:S(2)}, u32[]{:S(2)}) collective-permute-start(bf16[32,1792]{1,0:T(8,128)(2,1)S(1)} %collective-permute-done.4), channel_id=1, source_target_pairs={{0,112},{8,120},{16,0},{24,8},{32,16},{40,24},{48,32},{56,40},{64,... | collective-permute-start | bytes 344072 | tf_op jit(solution)/shard_map/ppermute | solution.py:32
  15.1 2.1 collective-permute-done.1
  17.2 2.7 %collective-permute-start.6 = (bf16[32,1792]{1,0:T(8,128)(2,1)S(1)}, bf16[32,1792]{1,0:T(8,128)(2,1)S(1)}, u32[]{:S(2)}, u32[]{:S(2)}) collective-permute-start(bf16[32,1792]{1,0:T(8,128)(2,1)S(1)} %collective-permute-done.5), channel_id=1, source_target_pairs={{0,112},{8,120},{16,0},{24,8},{32,16},{40,24},{48,32},{56,40},{64,... | collective-permute-start | bytes 344072 | tf_op jit(solution)/shard_map/ppermute | solution.py:32
  20.0 2.1 collective-permute-done.2
  22.1 4.8 %collective-permute-done.3 = bf16[32,1792]{1,0:T(8,128)(2,1)S(1)} collective-permute-done((bf16[32,1792]{1,0:T(8,128)(2,1)S(1)}, bf16[32,1792]{1,0:T(8,128)(2,1)S(1)}, u32[]{:S(2)}, u32[]{:S(2)}) %collective-permute-start.3) | collective-permute-done | bytes 114720 | tf_op jit(solution)/shard_map/ppermute | solution.py:32
  27.0 11.3 %all-to-all-start = ((bf16[32,128,512]{2,1,0:T(8,128)(2,1)}), bf16[32,128,512]{2,1,0:T(8,128)(2,1)}, u32[]{:S(2)}, u32[]{:S(2)}) async-start(bf16[32,128,512]{2,1,0:T(8,128)(2,1)} %bitcast.85), calls=%async_computation | async-start | bytes 8388608 | tf_op jit(solution)/shard_map/all_to_all | solution.py:284
  38.3 2.7 %collective-permute-start.10 = (bf16[8,32,1792]{2,1,0:T(8,128)(2,1)S(1)}, bf16[8,32,1792]{2,1,0:T(8,128)(2,1)}, u32[]{:S(2)}, u32[]{:S(2)}) collective-permute-start(bf16[8,32,1792]{2,1,0:T(8,128)(2,1)S(1)} %bitcast_dynamic-update-slice_fusion.refs_1_), channel_id=1, source_target_pairs={{0,129},{8,137},{16,145},{24,153},{32,161},{40,169},{48,177},{56,1... | collective-permute-start | bytes 2752520 | tf_op jit(solution)/shard_map/ppermute | solution.py:55
  41.0 1.3 collective-permute-start.7
  42.3 1.0 fusion.8
  43.3 1.4 collective-permute-start.8
  44.8 1.5 collective-permute-start.9
  46.2 1.5 collective-permute-start.15
  47.9 0.6 gather_fusion
  48.5 6.3 %collective-permute-done.8.refs_2_ = bf16[4,32,1792]{2,1,0:T(8,128)(2,1)} collective-permute-done((bf16[4,32,1792]{2,1,0:T(8,128)(2,1)}, bf16[4,32,1792]{2,1,0:T(8,128)(2,1)}, u32[]{:S(2)}, u32[]{:S(2)}) %collective-permute-start.8) | collective-permute-done | bytes 458784 | tf_op jit(solution)/shard_map/ppermute | solution.py:32
  54.7 9.8 %collective-permute-done.9.refs_3_ = bf16[4,32,1792]{2,1,0:T(8,128)(2,1)S(1)} collective-permute-done((bf16[4,32,1792]{2,1,0:T(8,128)(2,1)}, bf16[4,32,1792]{2,1,0:T(8,128)(2,1)S(1)}, u32[]{:S(2)}, u32[]{:S(2)}) %collective-permute-start.9) | collective-permute-done | bytes 458784 | tf_op jit(solution)/shard_map/ppermute | solution.py:32
  64.6 1.1 slice.11
  65.6 1.4 collective-permute-start.13
  67.0 0.2 collective-permute-start.11
  67.2 2.1 collective-permute-start.16
  69.5 7.9 %collective-permute-done.13.refs_4_ = bf16[4,32,1792]{2,1,0:T(8,128)(2,1)S(1)} collective-permute-done((bf16[4,32,1792]{2,1,0:T(8,128)(2,1)S(1)}, bf16[4,32,1792]{2,1,0:T(8,128)(2,1)S(1)}, u32[]{:S(2)}, u32[]{:S(2)}) %collective-permute-start.13) | collective-permute-done | bytes 458784 | tf_op jit(solution)/shard_map/ppermute | solution.py:32
  77.4 1.5 collective-permute-start.14
  78.9 10.7 %collective-permute-done.12.refs_2_ = bf16[4,32,1792]{2,1,0:T(8,128)(2,1)S(1)} collective-permute-done((bf16[4,32,1792]{2,1,0:T(8,128)(2,1)}, bf16[4,32,1792]{2,1,0:T(8,128)(2,1)S(1)}, u32[]{:S(2)}, u32[]{:S(2)}) %collective-permute-start.12) | collective-permute-done | bytes 458784 | tf_op jit(solution)/shard_map/ppermute | solution.py:55
  89.5 1.4 collective-permute-start.18
  90.9 0.6 collective-permute-start.20
  91.7 1.5 collective-permute-done.18.refs_8_
  93.1 2.7 %collective-permute-start.23 = (bf16[4,32,1792]{2,1,0:T(8,128)(2,1)S(1)}, bf16[4,32,1792]{2,1,0:T(8,128)(2,1)S(1)}, u32[]{:S(2)}, u32[]{:S(2)}) collective-permute-start(bf16[4,32,1792]{2,1,0:T(8,128)(2,1)S(1)} %collective-permute-done.13.refs_4_), channel_id=1, source_target_pairs={{0,129},{8,137},{16,145},{24,153},{32,161},{40,169},{48,177},{56,1... | collective-permute-start | bytes 1376264 | tf_op jit(solution)/shard_map/ppermute | solution.py:55
  96.0 10.5 %shard_map.55 = (bf16[4,4,256,1792]{3,2,1,0:T(8,128)(2,1)}, f32[4096,512]{1,0:T(8,128)}, f32[16,1,256]{2,1,0:T(1,128)S(1)}, f32[16,1,256]{2,1,0:T(1,128)S(1)}) custom-call(s32[4]{0:T(128)S(1)} %pad_add_fusion.place, bf16[8,32,1792]{2,1,0:T(8,128)(2,1)} %collective-permute-done.7.refs_0_, bf16[8,32,1792]{2,1,0:T(8,128)(2,1)S(1)} %bitcast_dynamic-update-slice_fusion.refs_1_, ...), custom_call_target="tpu_custom_call" | custom-call | flops 3758096384 | bytes 20709376 | tf_op jit(solution)/shard_map/pallas_call | solution.py:174
  106.5 4.7 %collective-permute-done.22.refs_3_ = bf16[4,32,1792]{2,1,0:T(8,128)(2,1)S(1)} collective-permute-done((bf16[4,32,1792]{2,1,0:T(8,128)(2,1)S(1)}, bf16[4,32,1792]{2,1,0:T(8,128)(2,1)S(1)}, u32[]{:S(2)}, u32[]{:S(2)}) %collective-permute-start.22) | collective-permute-done | bytes 458784 | tf_op jit(solution)/shard_map/ppermute | solution.py:55
  111.3 4.7 %collective-permute-done.24.refs_5_ = bf16[4,32,1792]{2,1,0:T(8,128)(2,1)S(1)} collective-permute-done((bf16[4,32,1792]{2,1,0:T(8,128)(2,1)S(1)}, bf16[4,32,1792]{2,1,0:T(8,128)(2,1)S(1)}, u32[]{:S(2)}, u32[]{:S(2)}) %collective-permute-start.24) | collective-permute-done | bytes 458784 | tf_op jit(solution)/shard_map/ppermute | solution.py:55
  116.0 1.2 collective-permute-start.25
  117.2 0.5 collective-permute-start.27
  117.7 0.5 collective-permute-start.29
  118.2 1.7 collective-permute-done.26.refs_8_
  119.9 0.7 collective-permute-done.27.refs_9_
  120.6 0.7 collective-permute-done.28.refs_10_
  121.2 0.7 collective-permute-done.29.refs_11_
  121.9 10.5 %shard_map.56 = (bf16[4,4,256,1792]{3,2,1,0:T(8,128)(2,1)}, f32[4096,512]{1,0:T(8,128)}, f32[16,1,256]{2,1,0:T(1,128)S(1)}, f32[16,1,256]{2,1,0:T(1,128)S(1)}) custom-call(s32[4]{0:T(128)S(1)} %pad_add_fusion.place, bf16[8,32,1792]{2,1,0:T(8,128)(2,1)S(1)} %collective-permute-done.11.refs_0_, ...), custom_call_target="tpu_custom_call", output_to_operand_aliasing={{0}: (16, {}), {1}: (17, {})} | custom-call | flops 3758096384 | bytes 20709376 | tf_op jit(solution)/shard_map/pallas_call | solution.py:174
  132.4 0.5 all-to-all-done
  132.9 0.9 broadcast_in_dim.13
  133.8 9.0 %all-to-all-start.1 = ((f32[16,1,4096]{2,1,0:T(1,128)}), f32[16,1,4096]{2,1,0:T(1,128)S(1)}, u32[]{:S(2)}, u32[]{:S(2)}) async-start(f32[16,1,4096]{2,1,0:T(1,128)} %broadcast_in_dim.13), calls=%async_computation.1 | async-start | bytes 524288 | tf_op jit(solution)/shard_map/all_to_all | solution.py:268
  142.9 12.6 %shard_map.57 = bf16[4096,512]{1,0:T(8,128)(2,1)} custom-call(s32[4096]{0:T(1024)S(1)} %bitcast.82, bf16[4096,512]{1,0:T(8,128)(2,1)} %bitcast.33.teacher), custom_call_target="tpu_custom_call" | custom-call | bytes 41943040 | tf_op jit(solution)/shard_map/pallas_call | solution.py:239
  155.8 0.2 broadcast_in_dim.14
  156.0 14.0 %all_to_all.35 = f32[16,1,4096]{2,1,0:T(1,128)S(1)} all-to-all(f32[16,1,4096]{2,1,0:T(1,128)S(1)} %broadcast_in_dim.14), channel_id=1, replica_groups={{0,1,2,3,4,5,6,7,128,129,130,131,132,133,134,135},{8,9,10,11,12,13,14,1..., dimensions={0} | all-to-all | bytes 524288 | tf_op jit(solution)/shard_map/all_to_all | solution.py:268
  170.0 0.2 reduce_max.19
  170.2 0.6 gather_fusion.2
  170.8 0.2 fusion.4
  171.0 0.6 gather_fusion.3
  171.6 7.0 %multiply_reduce_fusion = f32[4096]{0:T(1024)S(1)} fusion(f32[4096,512]{1,0:T(8,128)} %get-tuple-element.66, bf16[4096,512]{1,0:T(8,128)(2,1)} %shard_map.57, f32[4096]{0:T(1024)S(1)} %bitcast.92, f32[4096]{0:T(1024)S(1)} %bitcast.90), kind=kLoop, calls=%fused_computation.7 | loop fusion | flops 16773120 | bytes 12632064 | tf_op jit(solution)/shard_map/reduce_sum | solution.py:301
  178.7 0.6 gather_fusion.4
  179.3 0.9 broadcast_in_dim.16
  180.2 8.7 %all-to-all-start.3 = ((f32[16,1,4096]{2,1,0:T(1,128)}), f32[16,1,4096]{2,1,0:T(1,128)S(1)}, u32[]{:S(2)}, u32[]{:S(2)}) async-start(f32[16,1,4096]{2,1,0:T(1,128)} %broadcast_in_dim.16), calls=%async_computation.3 | async-start | bytes 524288 | tf_op jit(solution)/shard_map/all_to_all | solution.py:268
  189.0 11.6 %all-to-all-done.3 = f32[16,1,4096]{2,1,0:T(1,128)S(1)} async-done(((f32[16,1,4096]{2,1,0:T(1,128)}), f32[16,1,4096]{2,1,0:T(1,128)S(1)}, u32[]{:S(2)}, u32[]{:S(2)}) %all-to-all-start.3) | async-done | bytes 262176 | tf_op jit(solution)/shard_map/all_to_all | solution.py:268
  200.6 0.2 reduce_sum.58
  200.8 0.9 broadcast_in_dim.17
  201.7 3.5 %all-to-all-start.4 = ((f32[16,1,4096]{2,1,0:T(1,128)}), f32[16,1,4096]{2,1,0:T(1,128)S(1)}, u32[]{:S(2)}, u32[]{:S(2)}) async-start(f32[16,1,4096]{2,1,0:T(1,128)} %broadcast_in_dim.17), calls=%async_computation.4 | async-start | bytes 524288 | tf_op jit(solution)/shard_map/all_to_all | solution.py:268
  205.3 0.7 reduce_sum.54
  206.0 0.6 gather_fusion.1
  207.3 6.6 %all-to-all-done.4 = f32[16,1,4096]{2,1,0:T(1,128)S(1)} async-done(((f32[16,1,4096]{2,1,0:T(1,128)}), f32[16,1,4096]{2,1,0:T(1,128)S(1)}, u32[]{:S(2)}, u32[]{:S(2)}) %all-to-all-start.4) | async-done | bytes 262176 | tf_op jit(solution)/shard_map/all_to_all | solution.py:268
  214.1 0.6 gather_fusion.5
  214.7 15.3 %fusion.2 = bf16[1792,512]{1,0:T(8,128)(2,1)} fusion(bf16[4096,1792]{1,0:T(8,128)(2,1)} %bitcast.86, f32[4096,512]{1,0:T(8,128)} %get-tuple-element.66, bf16[4096,512]{1,0:T(8,128)(2,1)} %shard_map.57, f32[4096]{0:T(1024)S(1)} %bitcast.102, f32[4096]{0:T(1024)S(1)} %bitcast.93, f32[4096]{0:T(1024)S(1)} %bitcast.91, f32[4096]{0:T(1024)S(1)} %bitcast.101), kind=kOutput, calls=%fused_computation.13 | convolution fusion | flops 7538081792 | bytes 29163520 | tf_op jit(solution)/shard_map/dot_general | solution.py:313
  (69 shorter events, 1.4 us)
Async XLA Ops:
  0.9 11.4 %collective-permute-start = (bf16[32,1792]{1,0:T(8,128)(2,1)S(1)}, bf16[32,1792]{1,0:T(8,128)(2,1)S(1)}, u32[]{:S(2)}, u32[]{:S(2)}) collective-permute-start(bf16[32,1792]{1,0:T(8,128)(2,1)S(1)} %get-tuple-element.76), channel_id=1, source_target_pairs={{0,16},{8,24},{16,32},{24,40},{32,48},{40,56},{48,64},{56,72},{64,... | collective-permute-start | bytes 344072 | tf_op jit(solution)/shard_map/ppermute | solution.py:32
  3.5 8.9 %collective-permute-start.4 = (bf16[32,1792]{1,0:T(8,128)(2,1)S(1)}, bf16[32,1792]{1,0:T(8,128)(2,1)S(1)}, u32[]{:S(2)}, u32[]{:S(2)}) collective-permute-start(bf16[32,1792]{1,0:T(8,128)(2,1)S(1)} %get-tuple-element.76), channel_id=1, source_target_pairs={{0,112},{8,120},{16,0},{24,8},{32,16},{40,24},{48,32},{56,40},{64,... | collective-permute-start | bytes 344072 | tf_op jit(solution)/shard_map/ppermute | solution.py:32
  7.5 40.2 %copy-start.1 = (s32[4096]{0:T(1024)S(1)}, s32[4096]{0:T(1024)}, u32[]{:S(2)}) copy-start(s32[4096]{0:T(1024)} %param.8) | copy-start | bytes 49156
  12.3 83.7 %copy-start = (bf16[1792,512]{1,0:T(8,128)(2,1)S(1)}, bf16[1792,512]{1,0:T(8,128)(2,1)}, u32[]{:S(2)}) copy-start(bf16[1792,512]{1,0:T(8,128)(2,1)} %refs_12_.3) | copy-start | bytes 5505028
  12.3 4.9 %collective-permute-start.1 = (bf16[32,1792]{1,0:T(8,128)(2,1)S(1)}, bf16[32,1792]{1,0:T(8,128)(2,1)S(1)}, u32[]{:S(2)}, u32[]{:S(2)}) collective-permute-start(bf16[32,1792]{1,0:T(8,128)(2,1)S(1)} %collective-permute-done), channel_id=1, source_target_pairs={{0,16},{8,24},{16,32},{24,40},{32,48},{40,56},{48,64},{56,72},{64,... | collective-permute-start | bytes 344072 | tf_op jit(solution)/shard_map/ppermute | solution.py:32
  12.4 4.8 %collective-permute-start.5 = (bf16[32,1792]{1,0:T(8,128)(2,1)S(1)}, bf16[32,1792]{1,0:T(8,128)(2,1)S(1)}, u32[]{:S(2)}, u32[]{:S(2)}) collective-permute-start(bf16[32,1792]{1,0:T(8,128)(2,1)S(1)} %collective-permute-done.4), channel_id=1, source_target_pairs={{0,112},{8,120},{16,0},{24,8},{32,16},{40,24},{48,32},{56,40},{64,... | collective-permute-start | bytes 344072 | tf_op jit(solution)/shard_map/ppermute | solution.py:32
  17.2 4.9 %collective-permute-start.2 = (bf16[32,1792]{1,0:T(8,128)(2,1)S(1)}, bf16[32,1792]{1,0:T(8,128)(2,1)S(1)}, u32[]{:S(2)}, u32[]{:S(2)}) collective-permute-start(bf16[32,1792]{1,0:T(8,128)(2,1)S(1)} %collective-permute-done.1), channel_id=1, source_target_pairs={{0,16},{8,24},{16,32},{24,40},{32,48},{40,56},{48,64},{56,72},{64,... | collective-permute-start | bytes 344072 | tf_op jit(solution)/shard_map/ppermute | solution.py:32
  17.2 9.7 %collective-permute-start.6 = (bf16[32,1792]{1,0:T(8,128)(2,1)S(1)}, bf16[32,1792]{1,0:T(8,128)(2,1)S(1)}, u32[]{:S(2)}, u32[]{:S(2)}) collective-permute-start(bf16[32,1792]{1,0:T(8,128)(2,1)S(1)} %collective-permute-done.5), channel_id=1, source_target_pairs={{0,112},{8,120},{16,0},{24,8},{32,16},{40,24},{48,32},{56,40},{64,... | collective-permute-start | bytes 344072 | tf_op jit(solution)/shard_map/ppermute | solution.py:32
  22.0 4.9 %collective-permute-start.3 = (bf16[32,1792]{1,0:T(8,128)(2,1)S(1)}, bf16[32,1792]{1,0:T(8,128)(2,1)S(1)}, u32[]{:S(2)}, u32[]{:S(2)}) collective-permute-start(bf16[32,1792]{1,0:T(8,128)(2,1)S(1)} %collective-permute-done.2), channel_id=1, source_target_pairs={{0,16},{8,24},{16,32},{24,40},{32,48},{40,56},{48,64},{56,72},{64,... | collective-permute-start | bytes 344072 | tf_op jit(solution)/shard_map/ppermute | solution.py:32
  27.0 106.0 %all-to-all-start = ((bf16[32,128,512]{2,1,0:T(8,128)(2,1)}), bf16[32,128,512]{2,1,0:T(8,128)(2,1)}, u32[]{:S(2)}, u32[]{:S(2)}) async-start(bf16[32,128,512]{2,1,0:T(8,128)(2,1)} %bitcast.85), calls=%async_computation | async-start | bytes 8388608 | tf_op jit(solution)/shard_map/all_to_all | solution.py:284
  38.3 26.3 %collective-permute-start.10 = (bf16[8,32,1792]{2,1,0:T(8,128)(2,1)S(1)}, bf16[8,32,1792]{2,1,0:T(8,128)(2,1)}, u32[]{:S(2)}, u32[]{:S(2)}) collective-permute-start(bf16[8,32,1792]{2,1,0:T(8,128)(2,1)S(1)} %bitcast_dynamic-update-slice_fusion.refs_1_), channel_id=1, source_target_pairs={{0,129},{8,137},{16,145},{24,153},{32,161},{40,169},{48,177},{56,1... | collective-permute-start | bytes 2752520 | tf_op jit(solution)/shard_map/ppermute | solution.py:55
  41.0 23.5 %collective-permute-start.7 = (bf16[8,32,1792]{2,1,0:T(8,128)(2,1)S(1)}, bf16[8,32,1792]{2,1,0:T(8,128)(2,1)}, u32[]{:S(2)}, u32[]{:S(2)}) collective-permute-start(bf16[8,32,1792]{2,1,0:T(8,128)(2,1)S(1)} %bitcast_dynamic-update-slice_fusion.refs_1_), channel_id=1, source_target_pairs={{0,2},{8,10},{16,18},{24,26},{32,34},{40,42},{48,50},{56,58},{64,6... | collective-permute-start | bytes 2752520 | tf_op jit(solution)/shard_map/ppermute | solution.py:32
  43.3 11.4 %collective-permute-start.8 = (bf16[4,32,1792]{2,1,0:T(8,128)(2,1)}, bf16[4,32,1792]{2,1,0:T(8,128)(2,1)}, u32[]{:S(2)}, u32[]{:S(2)}) collective-permute-start(bf16[4,32,1792]{2,1,0:T(8,128)(2,1)} %get-tuple-element.78), channel_id=1, source_target_pairs={{0,6},{8,14},{16,22},{24,30},{32,38},{40,46},{48,54},{56,62},{64,7... | collective-permute-start | bytes 1376264 | tf_op jit(solution)/shard_map/ppermute | solution.py:32
  44.8 19.8 %collective-permute-start.9 = (bf16[4,32,1792]{2,1,0:T(8,128)(2,1)}, bf16[4,32,1792]{2,1,0:T(8,128)(2,1)S(1)}, u32[]{:S(2)}, u32[]{:S(2)}) collective-permute-start(bf16[4,32,1792]{2,1,0:T(8,128)(2,1)} %get-tuple-element.77), channel_id=1, source_target_pairs={{0,6},{8,14},{16,22},{24,30},{32,38},{40,46},{48,54},{56,62},{64,7... | collective-permute-start | bytes 1376264 | tf_op jit(solution)/shard_map/ppermute | solution.py:32
  46.2 23.2 %collective-permute-start.15 = (bf16[8,32,1792]{2,1,0:T(8,128)(2,1)S(1)}, bf16[8,32,1792]{2,1,0:T(8,128)(2,1)}, u32[]{:S(2)}, u32[]{:S(2)}) collective-permute-start(bf16[8,32,1792]{2,1,0:T(8,128)(2,1)S(1)} %bitcast_dynamic-update-slice_fusion.refs_1_), channel_id=1, source_target_pairs={{0,8},{8,0},{16,24},{24,16},{32,40},{40,32},{48,56},{56,48},{64,72... | collective-permute-start | bytes 2752520 | tf_op jit(solution)/shard_map/ppermute | solution.py:32
  65.6 11.8 %collective-permute-start.13 = (bf16[4,32,1792]{2,1,0:T(8,128)(2,1)S(1)}, bf16[4,32,1792]{2,1,0:T(8,128)(2,1)S(1)}, u32[]{:S(2)}, u32[]{:S(2)}) collective-permute-start(bf16[4,32,1792]{2,1,0:T(8,128)(2,1)S(1)} %slice.11), channel_id=1, source_target_pairs={{0,2},{8,10},{16,18},{24,26},{32,34},{40,42},{48,50},{56,58},{64,6... | collective-permute-start | bytes 1376264 | tf_op jit(solution)/shard_map/ppermute | solution.py:32
  67.0 23.9 %collective-permute-start.11 = (bf16[8,32,1792]{2,1,0:T(8,128)(2,1)}, bf16[8,32,1792]{2,1,0:T(8,128)(2,1)S(1)}, u32[]{:S(2)}, u32[]{:S(2)}) collective-permute-start(bf16[8,32,1792]{2,1,0:T(8,128)(2,1)} %collective-permute-done.7.refs_0_), channel_id=1, source_target_pairs={{0,129},{8,137},{16,145},{24,153},{32,161},{40,169},{48,177},{56,1... | collective-permute-start | bytes 2752520 | tf_op jit(solution)/shard_map/ppermute | solution.py:55
  67.2 23.7 %collective-permute-start.16 = (bf16[8,32,1792]{2,1,0:T(8,128)(2,1)}, bf16[8,32,1792]{2,1,0:T(8,128)(2,1)S(1)}, u32[]{:S(2)}, u32[]{:S(2)}) collective-permute-start(bf16[8,32,1792]{2,1,0:T(8,128)(2,1)} %collective-permute-done.7.refs_0_), channel_id=1, source_target_pairs={{0,8},{8,0},{16,24},{24,16},{32,40},{40,32},{48,56},{56,48},{64,72... | collective-permute-start | bytes 2752520 | tf_op jit(solution)/shard_map/ppermute | solution.py:32
  69.4 21.6 %collective-permute-start.17 = (bf16[8,32,1792]{2,1,0:T(8,128)(2,1)}, bf16[8,32,1792]{2,1,0:T(8,128)(2,1)S(1)}, u32[]{:S(2)}, u32[]{:S(2)}) collective-permute-start(bf16[8,32,1792]{2,1,0:T(8,128)(2,1)} %collective-permute-done.10.refs_1_), channel_id=1, source_target_pairs={{0,8},{8,0},{16,24},{24,16},{32,40},{40,32},{48,56},{56,48},{64,72... | collective-permute-start | bytes 2752520 | tf_op jit(solution)/shard_map/ppermute | solution.py:32
  69.4 20.2 %collective-permute-start.12 = (bf16[4,32,1792]{2,1,0:T(8,128)(2,1)}, bf16[4,32,1792]{2,1,0:T(8,128)(2,1)S(1)}, u32[]{:S(2)}, u32[]{:S(2)}) collective-permute-start(bf16[4,32,1792]{2,1,0:T(8,128)(2,1)} %collective-permute-done.8.refs_2_), channel_id=1, source_target_pairs={{0,128},{8,136},{16,144},{24,152},{32,160},{40,168},{48,176},{56,1... | collective-permute-start | bytes 1376264 | tf_op jit(solution)/shard_map/ppermute | solution.py:55
  77.4 13.5 %collective-permute-start.14 = (bf16[4,32,1792]{2,1,0:T(8,128)(2,1)S(1)}, bf16[4,32,1792]{2,1,0:T(8,128)(2,1)S(1)}, u32[]{:S(2)}, u32[]{:S(2)}) collective-permute-start(bf16[4,32,1792]{2,1,0:T(8,128)(2,1)S(1)} %collective-permute-done.9.refs_3_), channel_id=1, source_target_pairs={{0,6},{8,14},{16,22},{24,30},{32,38},{40,46},{48,54},{56,62},{64,7... | collective-permute-start | bytes 1376264 | tf_op jit(solution)/shard_map/ppermute | solution.py:32
  89.5 3.6 %collective-permute-start.18 = (bf16[4,32,1792]{2,1,0:T(8,128)(2,1)}, bf16[4,32,1792]{2,1,0:T(8,128)(2,1)S(1)}, u32[]{:S(2)}, u32[]{:S(2)}) collective-permute-start(bf16[4,32,1792]{2,1,0:T(8,128)(2,1)} %collective-permute-done.8.refs_2_), channel_id=1, source_target_pairs={{0,8},{8,0},{16,24},{24,16},{32,40},{40,32},{48,56},{56,48},{64,72... | collective-permute-start | bytes 1376264 | tf_op jit(solution)/shard_map/ppermute | solution.py:32
  90.9 4.9 %collective-permute-start.19 = (bf16[4,32,1792]{2,1,0:T(8,128)(2,1)S(1)}, bf16[4,32,1792]{2,1,0:T(8,128)(2,1)S(1)}, u32[]{:S(2)}, u32[]{:S(2)}) collective-permute-start(bf16[4,32,1792]{2,1,0:T(8,128)(2,1)S(1)} %collective-permute-done.9.refs_3_), channel_id=1, source_target_pairs={{0,8},{8,0},{16,24},{24,16},{32,40},{40,32},{48,56},{56,48},{64,72... | collective-permute-start | bytes 1376264 | tf_op jit(solution)/shard_map/ppermute | solution.py:32
  90.9 5.0 %collective-permute-start.20 = (bf16[4,32,1792]{2,1,0:T(8,128)(2,1)S(1)}, bf16[4,32,1792]{2,1,0:T(8,128)(2,1)S(1)}, u32[]{:S(2)}, u32[]{:S(2)}) collective-permute-start(bf16[4,32,1792]{2,1,0:T(8,128)(2,1)S(1)} %collective-permute-done.13.refs_4_), channel_id=1, source_target_pairs={{0,8},{8,0},{16,24},{24,16},{32,40},{40,32},{48,56},{56,48},{64,72... | collective-permute-start | bytes 1376264 | tf_op jit(solution)/shard_map/ppermute | solution.py:32
  91.5 4.4 %collective-permute-start.21 = (bf16[4,32,1792]{2,1,0:T(8,128)(2,1)S(1)}, bf16[4,32,1792]{2,1,0:T(8,128)(2,1)S(1)}, u32[]{:S(2)}, u32[]{:S(2)}) collective-permute-start(bf16[4,32,1792]{2,1,0:T(8,128)(2,1)S(1)} %collective-permute-done.14.refs_5_), channel_id=1, source_target_pairs={{0,8},{8,0},{16,24},{24,16},{32,40},{40,32},{48,56},{56,48},{64,72... | collective-permute-start | bytes 1376264 | tf_op jit(solution)/shard_map/ppermute | solution.py:32
  91.6 19.6 %collective-permute-start.22 = (bf16[4,32,1792]{2,1,0:T(8,128)(2,1)S(1)}, bf16[4,32,1792]{2,1,0:T(8,128)(2,1)S(1)}, u32[]{:S(2)}, u32[]{:S(2)}) collective-permute-start(bf16[4,32,1792]{2,1,0:T(8,128)(2,1)S(1)} %collective-permute-done.9.refs_3_), channel_id=1, source_target_pairs={{0,128},{8,136},{16,144},{24,152},{32,160},{40,168},{48,176},{56,1... | collective-permute-start | bytes 1376264 | tf_op jit(solution)/shard_map/ppermute | solution.py:55
  93.1 18.1 %collective-permute-start.23 = (bf16[4,32,1792]{2,1,0:T(8,128)(2,1)S(1)}, bf16[4,32,1792]{2,1,0:T(8,128)(2,1)S(1)}, u32[]{:S(2)}, u32[]{:S(2)}) collective-permute-start(bf16[4,32,1792]{2,1,0:T(8,128)(2,1)S(1)} %collective-permute-done.13.refs_4_), channel_id=1, source_target_pairs={{0,129},{8,137},{16,145},{24,153},{32,161},{40,169},{48,177},{56,1... | collective-permute-start | bytes 1376264 | tf_op jit(solution)/shard_map/ppermute | solution.py:55
  95.9 20.1 %collective-permute-start.24 = (bf16[4,32,1792]{2,1,0:T(8,128)(2,1)S(1)}, bf16[4,32,1792]{2,1,0:T(8,128)(2,1)S(1)}, u32[]{:S(2)}, u32[]{:S(2)}) collective-permute-start(bf16[4,32,1792]{2,1,0:T(8,128)(2,1)S(1)} %collective-permute-done.14.refs_5_), channel_id=1, source_target_pairs={{0,129},{8,137},{16,145},{24,153},{32,161},{40,169},{48,177},{56,1... | collective-permute-start | bytes 1376264 | tf_op jit(solution)/shard_map/ppermute | solution.py:55
  116.0 5.9 %collective-permute-start.25 = (bf16[8,32,1792]{2,1,0:T(8,128)(2,1)S(1)}, bf16[8,32,1792]{2,1,0:T(8,128)(2,1)S(1)}, u32[]{:S(2)}, u32[]{:S(2)}) collective-permute-start(bf16[8,32,1792]{2,1,0:T(8,128)(2,1)S(1)} %collective-permute-done.11.refs_0_), channel_id=1, source_target_pairs={{0,8},{8,0},{16,24},{24,16},{32,40},{40,32},{48,56},{56,48},{64,72... | collective-permute-start | bytes 2752520 | tf_op jit(solution)/shard_map/ppermute | solution.py:32
  117.2 2.8 %collective-permute-start.26 = (bf16[4,32,1792]{2,1,0:T(8,128)(2,1)S(1)}, bf16[4,32,1792]{2,1,0:T(8,128)(2,1)S(1)}, u32[]{:S(2)}, u32[]{:S(2)}) collective-permute-start(bf16[4,32,1792]{2,1,0:T(8,128)(2,1)S(1)} %collective-permute-done.12.refs_2_), channel_id=1, source_target_pairs={{0,8},{8,0},{16,24},{24,16},{32,40},{40,32},{48,56},{56,48},{64,72... | collective-permute-start | bytes 1376264 | tf_op jit(solution)/shard_map/ppermute | solution.py:32
  117.2 3.4 %collective-permute-start.27 = (bf16[4,32,1792]{2,1,0:T(8,128)(2,1)S(1)}, bf16[4,32,1792]{2,1,0:T(8,128)(2,1)S(1)}, u32[]{:S(2)}, u32[]{:S(2)}) collective-permute-start(bf16[4,32,1792]{2,1,0:T(8,128)(2,1)S(1)} %collective-permute-done.22.refs_3_), channel_id=1, source_target_pairs={{0,8},{8,0},{16,24},{24,16},{32,40},{40,32},{48,56},{56,48},{64,72... | collective-permute-start | bytes 1376264 | tf_op jit(solution)/shard_map/ppermute | solution.py:32
  117.7 3.6 %collective-permute-start.28 = (bf16[4,32,1792]{2,1,0:T(8,128)(2,1)S(1)}, bf16[4,32,1792]{2,1,0:T(8,128)(2,1)S(1)}, u32[]{:S(2)}, u32[]{:S(2)}) collective-permute-start(bf16[4,32,1792]{2,1,0:T(8,128)(2,1)S(1)} %collective-permute-done.23.refs_4_), channel_id=1, source_target_pairs={{0,8},{8,0},{16,24},{24,16},{32,40},{40,32},{48,56},{56,48},{64,72... | collective-permute-start | bytes 1376264 | tf_op jit(solution)/shard_map/ppermute | solution.py:32
  117.7 4.2 %collective-permute-start.29 = (bf16[4,32,1792]{2,1,0:T(8,128)(2,1)S(1)}, bf16[4,32,1792]{2,1,0:T(8,128)(2,1)S(1)}, u32[]{:S(2)}, u32[]{:S(2)}) collective-permute-start(bf16[4,32,1792]{2,1,0:T(8,128)(2,1)S(1)} %collective-permute-done.24.refs_5_), channel_id=1, source_target_pairs={{0,8},{8,0},{16,24},{24,16},{32,40},{40,32},{48,56},{56,48},{64,72... | collective-permute-start | bytes 1376264 | tf_op jit(solution)/shard_map/ppermute | solution.py:32
  133.8 21.7 %all-to-all-start.1 = ((f32[16,1,4096]{2,1,0:T(1,128)}), f32[16,1,4096]{2,1,0:T(1,128)S(1)}, u32[]{:S(2)}, u32[]{:S(2)}) async-start(f32[16,1,4096]{2,1,0:T(1,128)} %broadcast_in_dim.13), calls=%async_computation.1 | async-start | bytes 524288 | tf_op jit(solution)/shard_map/all_to_all | solution.py:268
  155.5 33.4 %copy-start.2 = (s32[32]{0:T(128)S(1)}, s32[32]{0:T(128)}, u32[]{:S(2)}) copy-start(s32[32]{0:T(128)} %param.9) | copy-start | bytes 388
  180.2 20.4 %all-to-all-start.3 = ((f32[16,1,4096]{2,1,0:T(1,128)}), f32[16,1,4096]{2,1,0:T(1,128)S(1)}, u32[]{:S(2)}, u32[]{:S(2)}) async-start(f32[16,1,4096]{2,1,0:T(1,128)} %broadcast_in_dim.16), calls=%async_computation.3 | async-start | bytes 524288 | tf_op jit(solution)/shard_map/all_to_all | solution.py:268
  201.7 12.2 %all-to-all-start.4 = ((f32[16,1,4096]{2,1,0:T(1,128)}), f32[16,1,4096]{2,1,0:T(1,128)S(1)}, u32[]{:S(2)}, u32[]{:S(2)}) async-start(f32[16,1,4096]{2,1,0:T(1,128)} %broadcast_in_dim.17), calls=%async_computation.4 | async-start | bytes 524288 | tf_op jit(solution)/shard_map/all_to_all | solution.py:268

commit v3 on v2

--- a/solution.py
+++ b/solution.py
@@ -100,7 +100,8 @@
 
 def to_local(values, place):
     order = jnp.stack([token_block(place, column, k) for column in range(2) for k in range(NZ)])
-    return values.reshape(2 * NZ, -1)[order].reshape(-1)
+    blocks = values.reshape(*values.shape[:-1], 2 * NZ, -1)
+    return jnp.take(blocks, order, axis=-2, mode="clip").reshape(values.shape)
 
 
 def from_local(values, place):
@@ -207,9 +208,10 @@
     )(place, *pieces, weight, *extra)
 
 
-def rows_kernel(chosen, teacher, aligned, narrow, wide, sem):
+def rows_kernel(chosen, teacher, aligned, narrow, wide, picked, sem):
     step = pl.program_id(0)
-    count = aligned.shape[0]
+    count, width = aligned.shape
+    lines = width // 128
     parts = sem.shape[0]
     part = narrow.shape[0] // parts
 
@@ -223,14 +225,21 @@
             load(i).start()
         for i in range(parts):
             load(i).wait()
-            wide[pl.ds(i * part, part), :] = narrow[pl.ds(i * part, part), :].astype(jnp.float32)
+            for line in range(lines):
+                values = narrow[pl.ds(i * part, part), pl.ds(line * 128, 128)].astype(jnp.float32)
+                wide[pl.ds(i * part * lines + line, part, stride=lines), :] = values
 
     @pl.loop(0, count // 16, unroll=4)
     def _(group):
         first = step * count + group * 16
-        picked = [wide[pl.ds(chosen[first + i], 1), :] for i in range(16)]
-        rows = jnp.concatenate(picked, axis=0).astype(jnp.bfloat16)
-        aligned[pl.ds(pl.multiple_of(group * 16, 16), 16), :] = rows
+        to = group * 16 * lines
+        for i in range(16):
+            row = pl.multiple_of(chosen[first + i] * lines, lines)
+            picked[pl.ds(pl.multiple_of(to + i * lines, lines), lines), :] = wide[pl.ds(row, lines), :]
+
+    for line in range(lines):
+        values = picked[pl.ds(line, count, stride=lines), :]
+        aligned[:, pl.ds(line * 128, 128)] = values.astype(jnp.bfloat16)
 
 
 def take_rows(teacher, chosen):
@@ -245,12 +254,13 @@
             out_specs=pl.BlockSpec((count, width), lambda step, chosen: (step, 0)),
             scratch_shapes=[
                 pltpu.VMEM((rows, width), jnp.bfloat16),
-                pltpu.VMEM((rows, width), jnp.float32),
+                pltpu.VMEM((rows * (width // 128), 128), jnp.float32),
+                pltpu.VMEM((count * (width // 128), 128), jnp.float32),
                 pltpu.SemaphoreType.DMA((8,)),
             ],
         ),
         out_shape=pltpu.HBM((rows, width), jnp.bfloat16),
-        compiler_params=pltpu.CompilerParams(vmem_limit_bytes=20 * 1024 * 1024),
+        compiler_params=pltpu.CompilerParams(vmem_limit_bytes=24 * 1024 * 1024),
         cost_estimate=pl.CostEstimate(flops=0, transcendentals=0, bytes_accessed=10 * rows * width * 2),
     )(chosen, teacher)
 
@@ -294,7 +304,7 @@
         aligned = aligned.astype(jnp.float32)
         peak, total = peak_and_total(log_total)
         row_peak, row_total = peak_and_total(from_members(peak + jnp.log(total), in_plane))
-        row_peak, row_total = to_local(row_peak, place), to_local(row_total, place)
+        row_peak, row_total = to_local(jnp.stack([row_peak, row_total]), place)
         log_student = logits - row_peak[:, None] - jnp.log(row_total)[:, None]
         student = jnp.exp(log_student)
         grad_prob = 0.5 * (log_student - jnp.log(aligned + student))

time: 231 us -> 227 us (0.983)
  Pallas kernels: 33.6 us -> 30.9 us
    pallas_call x1, Pallas kernels: 12.6 us -> 9.87 us  [take_rows(): pl.pallas_call(rows_kernel, grid_spec=pltpu.PrefetchScalarGridSpec(num_sc...]
  transfers between devices with their start and end apart: 34 -> 34, of which waited for: 17 -> 18; matrix products, arithmetic and copies ran while one was open for 4% -> 4% of each run, Pallas kernels for 15% -> 14%
where the time goes in v3:
time: 227 us
  waiting for transfers between devices  79 us (35%)
  starting transfers between devices  63.1 us (28%)
  Pallas kernels  30.9 us (14%)
  matrix products  15.3 us (7%)
  blocking collectives  14.4 us (6%)
  local copies, waits for them, and re-layouts  14.3 us (6%)
  other arithmetic  8.64 us (4%)
    ppermute x24, waiting for transfers between devices, hop(): return lax.ppermute(array, AXES, pairs)  38.1 us
    ppermute x24, starting transfers between devices, hop(): return lax.ppermute(array, AXES, pairs)  27 us
    pallas_call x2, Pallas kernels, block_logits(): pl.pallas_call(functools.partial(logits_kernel, column), grid_spec=pltpu....  21 us
    all_to_all x3, waiting for transfers between devices, from_members(): lax.all_to_all(copies, AXES, split_axis=0, concat_axis=0, tiled=True, axi...  20.2 us
    ppermute x6, waiting for transfers between devices, cross(): return lax.ppermute(array, AXES, pairs)  20.1 us
    all_to_all x3, starting transfers between devices, from_members(): lax.all_to_all(copies, AXES, split_axis=0, concat_axis=0, tiled=True, axi...  19 us
    dot_general x1, matrix products, per_device(): lax.dot_general(gathered, dlogits, (((0,), (0,)), ((), ())), preferred_el...  15.3 us
    all_to_all x1, blocking collectives, from_members(): lax.all_to_all(copies, AXES, split_axis=0, concat_axis=0, tiled=True, axi...  14.4 us
  transfers between devices with their start and end apart: 34, of which 18 were waited for; matrix products, arithmetic and copies ran while one was open for 4% of the time, Pallas kernels for 14%

profile of v3, /device:TPU:1, one launch (start us, length us, event | category | flops | bytes accessed | tf_op | source)
XLA Modules:
  0.0 226.7 jit_solution(15957975348504506391)
XLA Ops:
  0.0 0.9 bitcast_dynamic-update-slice_fusion.7
  0.9 2.5 %collective-permute-start = (bf16[32,1792]{1,0:T(8,128)(2,1)S(1)}, bf16[32,1792]{1,0:T(8,128)(2,1)S(1)}, u32[]{:S(2)}, u32[]{:S(2)}) collective-permute-start(bf16[32,1792]{1,0:T(8,128)(2,1)S(1)} %get-tuple-element.76), channel_id=1, source_target_pairs={{0,16},{8,24},{16,32},{24,40},{32,48},{40,56},{48,64},{56,72},{64,... | collective-permute-start | bytes 344072 | tf_op jit(solution)/shard_map/ppermute | solution.py:32
  3.5 4.0 %collective-permute-start.4 = (bf16[32,1792]{1,0:T(8,128)(2,1)S(1)}, bf16[32,1792]{1,0:T(8,128)(2,1)S(1)}, u32[]{:S(2)}, u32[]{:S(2)}) collective-permute-start(bf16[32,1792]{1,0:T(8,128)(2,1)S(1)} %get-tuple-element.76), channel_id=1, source_target_pairs={{0,112},{8,120},{16,0},{24,8},{32,16},{40,24},{48,32},{56,40},{64,... | collective-permute-start | bytes 344072 | tf_op jit(solution)/shard_map/ppermute | solution.py:32
  7.5 4.8 %copy.32 = bf16[16,32,8,512]{3,2,0,1:T(8,128)(2,1)} copy(bf16[16,32,8,512]{3,2,1,0:T(8,128)(2,1)} %bitcast.103) | data formatting | bytes 8388608 | tf_op jit(solution)/shard_map/reshape | solution.py:290
  12.4 2.7 %collective-permute-start.5 = (bf16[32,1792]{1,0:T(8,128)(2,1)S(1)}, bf16[32,1792]{1,0:T(8,128)(2,1)S(1)}, u32[]{:S(2)}, u32[]{:S(2)}) collective-permute-start(bf16[32,1792]{1,0:T(8,128)(2,1)S(1)} %collective-permute-done.4), channel_id=1, source_target_pairs={{0,112},{8,120},{16,0},{24,8},{32,16},{40,24},{48,32},{56,40},{64,... | collective-permute-start | bytes 344072 | tf_op jit(solution)/shard_map/ppermute | solution.py:32
  15.1 2.1 collective-permute-done.1
  17.2 2.7 %collective-permute-start.6 = (bf16[32,1792]{1,0:T(8,128)(2,1)S(1)}, bf16[32,1792]{1,0:T(8,128)(2,1)S(1)}, u32[]{:S(2)}, u32[]{:S(2)}) collective-permute-start(bf16[32,1792]{1,0:T(8,128)(2,1)S(1)} %collective-permute-done.5), channel_id=1, source_target_pairs={{0,112},{8,120},{16,0},{24,8},{32,16},{40,24},{48,32},{56,40},{64,... | collective-permute-start | bytes 344072 | tf_op jit(solution)/shard_map/ppermute | solution.py:32
  20.0 2.1 collective-permute-done.2
  22.1 4.8 %collective-permute-done.3 = bf16[32,1792]{1,0:T(8,128)(2,1)S(1)} collective-permute-done((bf16[32,1792]{1,0:T(8,128)(2,1)S(1)}, bf16[32,1792]{1,0:T(8,128)(2,1)S(1)}, u32[]{:S(2)}, u32[]{:S(2)}) %collective-permute-start.3) | collective-permute-done | bytes 114720 | tf_op jit(solution)/shard_map/ppermute | solution.py:32
  27.0 11.3 %all-to-all-start = ((bf16[32,128,512]{2,1,0:T(8,128)(2,1)}), bf16[32,128,512]{2,1,0:T(8,128)(2,1)}, u32[]{:S(2)}, u32[]{:S(2)}) async-start(bf16[32,128,512]{2,1,0:T(8,128)(2,1)} %bitcast.101), calls=%async_computation | async-start | bytes 8388608 | tf_op jit(solution)/shard_map/all_to_all | solution.py:294
  38.3 2.7 %collective-permute-start.10 = (bf16[8,32,1792]{2,1,0:T(8,128)(2,1)S(1)}, bf16[8,32,1792]{2,1,0:T(8,128)(2,1)}, u32[]{:S(2)}, u32[]{:S(2)}) collective-permute-start(bf16[8,32,1792]{2,1,0:T(8,128)(2,1)S(1)} %bitcast_dynamic-update-slice_fusion.refs_1_), channel_id=1, source_target_pairs={{0,129},{8,137},{16,145},{24,153},{32,161},{40,169},{48,177},{56,1... | collective-permute-start | bytes 2752520 | tf_op jit(solution)/shard_map/ppermute | solution.py:55
  41.0 1.3 collective-permute-start.7
  42.3 1.0 fusion.8
  43.3 1.4 collective-permute-start.8
  44.8 1.5 collective-permute-start.9
  46.2 1.5 collective-permute-start.15
  48.0 0.6 gather_fusion
  48.6 6.2 %collective-permute-done.8.refs_2_ = bf16[4,32,1792]{2,1,0:T(8,128)(2,1)} collective-permute-done((bf16[4,32,1792]{2,1,0:T(8,128)(2,1)}, bf16[4,32,1792]{2,1,0:T(8,128)(2,1)}, u32[]{:S(2)}, u32[]{:S(2)}) %collective-permute-start.8) | collective-permute-done | bytes 458784 | tf_op jit(solution)/shard_map/ppermute | solution.py:32
  54.7 9.8 %collective-permute-done.9.refs_3_ = bf16[4,32,1792]{2,1,0:T(8,128)(2,1)S(1)} collective-permute-done((bf16[4,32,1792]{2,1,0:T(8,128)(2,1)}, bf16[4,32,1792]{2,1,0:T(8,128)(2,1)S(1)}, u32[]{:S(2)}, u32[]{:S(2)}) %collective-permute-start.9) | collective-permute-done | bytes 458784 | tf_op jit(solution)/shard_map/ppermute | solution.py:32
  64.6 1.1 slice.13
  65.6 1.4 collective-permute-start.13
  67.0 0.2 collective-permute-start.11
  67.2 2.1 collective-permute-start.16
  69.5 7.9 %collective-permute-done.13.refs_4_ = bf16[4,32,1792]{2,1,0:T(8,128)(2,1)S(1)} collective-permute-done((bf16[4,32,1792]{2,1,0:T(8,128)(2,1)S(1)}, bf16[4,32,1792]{2,1,0:T(8,128)(2,1)S(1)}, u32[]{:S(2)}, u32[]{:S(2)}) %collective-permute-start.13) | collective-permute-done | bytes 458784 | tf_op jit(solution)/shard_map/ppermute | solution.py:32
  77.4 1.5 collective-permute-start.14
  78.9 10.7 %collective-permute-done.12.refs_2_ = bf16[4,32,1792]{2,1,0:T(8,128)(2,1)S(1)} collective-permute-done((bf16[4,32,1792]{2,1,0:T(8,128)(2,1)}, bf16[4,32,1792]{2,1,0:T(8,128)(2,1)S(1)}, u32[]{:S(2)}, u32[]{:S(2)}) %collective-permute-start.12) | collective-permute-done | bytes 458784 | tf_op jit(solution)/shard_map/ppermute | solution.py:55
  89.5 1.4 collective-permute-start.18
  91.0 0.6 collective-permute-start.20
  91.7 1.5 collective-permute-done.18.refs_8_
  93.2 2.7 %collective-permute-start.23 = (bf16[4,32,1792]{2,1,0:T(8,128)(2,1)S(1)}, bf16[4,32,1792]{2,1,0:T(8,128)(2,1)S(1)}, u32[]{:S(2)}, u32[]{:S(2)}) collective-permute-start(bf16[4,32,1792]{2,1,0:T(8,128)(2,1)S(1)} %collective-permute-done.13.refs_4_), channel_id=1, source_target_pairs={{0,129},{8,137},{16,145},{24,153},{32,161},{40,169},{48,177},{56,1... | collective-permute-start | bytes 1376264 | tf_op jit(solution)/shard_map/ppermute | solution.py:55
  96.0 10.5 %shard_map.55 = (bf16[4,4,256,1792]{3,2,1,0:T(8,128)(2,1)}, f32[4096,512]{1,0:T(8,128)}, f32[16,1,256]{2,1,0:T(1,128)S(1)}, f32[16,1,256]{2,1,0:T(1,128)S(1)}) custom-call(s32[4]{0:T(128)S(1)} %pad_add_fusion.place, bf16[8,32,1792]{2,1,0:T(8,128)(2,1)} %collective-permute-done.7.refs_0_, bf16[8,32,1792]{2,1,0:T(8,128)(2,1)S(1)} %bitcast_dynamic-update-slice_fusion.refs_1_, ...), custom_call_target="tpu_custom_call" | custom-call | flops 3758096384 | bytes 20709376 | tf_op jit(solution)/shard_map/pallas_call | solution.py:175
  106.5 4.7 %collective-permute-done.22.refs_3_ = bf16[4,32,1792]{2,1,0:T(8,128)(2,1)S(1)} collective-permute-done((bf16[4,32,1792]{2,1,0:T(8,128)(2,1)S(1)}, bf16[4,32,1792]{2,1,0:T(8,128)(2,1)S(1)}, u32[]{:S(2)}, u32[]{:S(2)}) %collective-permute-start.22) | collective-permute-done | bytes 458784 | tf_op jit(solution)/shard_map/ppermute | solution.py:55
  111.3 4.7 %collective-permute-done.24.refs_5_ = bf16[4,32,1792]{2,1,0:T(8,128)(2,1)S(1)} collective-permute-done((bf16[4,32,1792]{2,1,0:T(8,128)(2,1)S(1)}, bf16[4,32,1792]{2,1,0:T(8,128)(2,1)S(1)}, u32[]{:S(2)}, u32[]{:S(2)}) %collective-permute-start.24) | collective-permute-done | bytes 458784 | tf_op jit(solution)/shard_map/ppermute | solution.py:55
  116.0 1.2 collective-permute-start.25
  117.2 0.5 collective-permute-start.27
  117.7 0.5 collective-permute-start.29
  118.2 1.7 collective-permute-done.26.refs_8_
  119.9 0.7 collective-permute-done.27.refs_9_
  120.6 0.7 collective-permute-done.28.refs_10_
  121.2 0.7 collective-permute-done.29.refs_11_
  121.9 10.5 %shard_map.56 = (bf16[4,4,256,1792]{3,2,1,0:T(8,128)(2,1)}, f32[4096,512]{1,0:T(8,128)}, f32[16,1,256]{2,1,0:T(1,128)S(1)}, f32[16,1,256]{2,1,0:T(1,128)S(1)}) custom-call(s32[4]{0:T(128)S(1)} %pad_add_fusion.place, bf16[8,32,1792]{2,1,0:T(8,128)(2,1)S(1)} %collective-permute-done.11.refs_0_, ...), custom_call_target="tpu_custom_call", output_to_operand_aliasing={{0}: (16, {}), {1}: (17, {})} | custom-call | flops 3758096384 | bytes 20709376 | tf_op jit(solution)/shard_map/pallas_call | solution.py:175
  132.4 0.5 all-to-all-done
  132.9 0.9 broadcast_in_dim.22
  133.8 9.0 %all-to-all-start.1 = ((f32[16,1,4096]{2,1,0:T(1,128)}), f32[16,1,4096]{2,1,0:T(1,128)S(1)}, u32[]{:S(2)}, u32[]{:S(2)}) async-start(f32[16,1,4096]{2,1,0:T(1,128)} %broadcast_in_dim.22), calls=%async_computation.1 | async-start | bytes 524288 | tf_op jit(solution)/shard_map/all_to_all | solution.py:278
  142.9 9.9 %shard_map.57 = bf16[4096,512]{1,0:T(8,128)(2,1)} custom-call(s32[4096]{0:T(1024)S(1)} %bitcast.98, bf16[4096,512]{1,0:T(8,128)(2,1)} %bitcast.32.teacher), custom_call_target="tpu_custom_call" | custom-call | bytes 41943040 | tf_op jit(solution)/shard_map/pallas_call | solution.py:248
  152.8 1.8 all-to-all-done.1
  154.9 0.2 broadcast_in_dim.23
  155.1 14.4 %all_to_all.35 = f32[16,1,4096]{2,1,0:T(1,128)S(1)} all-to-all(f32[16,1,4096]{2,1,0:T(1,128)S(1)} %broadcast_in_dim.23), channel_id=1, replica_groups={{0,1,2,3,4,5,6,7,128,129,130,131,132,133,134,135},{8,9,10,11,12,13,14,1..., dimensions={0} | all-to-all | bytes 524288 | tf_op jit(solution)/shard_map/all_to_all | solution.py:278
  169.5 0.2 reduce_max.19
  169.7 0.2 fusion.4
  169.9 0.6 gather_fusion.2
  170.6 7.0 %multiply_reduce_fusion = f32[4096]{0:T(1024)S(1)} fusion(f32[4096,512]{1,0:T(8,128)} %get-tuple-element.66, bf16[4096,512]{1,0:T(8,128)(2,1)} %shard_map.57, f32[4096]{0:T(1024)S(1)} %bitcast.110, f32[4096]{0:T(1024)S(1)} %bitcast.108), kind=kLoop, calls=%fused_computation.6 | loop fusion | flops 16773120 | bytes 12632064 | tf_op jit(solution)/shard_map/reduce_sum | solution.py:311
  177.6 0.6 gather_fusion.3
  178.2 0.9 broadcast_in_dim.26
  179.1 6.4 %all-to-all-start.3 = ((f32[16,1,4096]{2,1,0:T(1,128)}), f32[16,1,4096]{2,1,0:T(1,128)S(1)}, u32[]{:S(2)}, u32[]{:S(2)}) async-start(f32[16,1,4096]{2,1,0:T(1,128)} %broadcast_in_dim.26), calls=%async_computation.3 | async-start | bytes 524288 | tf_op jit(solution)/shard_map/all_to_all | solution.py:278
  185.7 11.6 %all-to-all-done.3 = f32[16,1,4096]{2,1,0:T(1,128)S(1)} async-done(((f32[16,1,4096]{2,1,0:T(1,128)}), f32[16,1,4096]{2,1,0:T(1,128)S(1)}, u32[]{:S(2)}, u32[]{:S(2)}) %all-to-all-start.3) | async-done | bytes 262176 | tf_op jit(solution)/shard_map/all_to_all | solution.py:278
  197.3 0.2 reduce_sum.58
  197.4 0.9 broadcast_in_dim.27
  198.4 3.5 %all-to-all-start.4 = ((f32[16,1,4096]{2,1,0:T(1,128)}), f32[16,1,4096]{2,1,0:T(1,128)S(1)}, u32[]{:S(2)}, u32[]{:S(2)}) async-start(f32[16,1,4096]{2,1,0:T(1,128)} %broadcast_in_dim.27), calls=%async_computation.4 | async-start | bytes 524288 | tf_op jit(solution)/shard_map/all_to_all | solution.py:278
  202.0 0.6 reduce_sum.54
  202.6 0.6 gather_fusion.1
  203.8 6.8 %all-to-all-done.4 = f32[16,1,4096]{2,1,0:T(1,128)S(1)} async-done(((f32[16,1,4096]{2,1,0:T(1,128)}), f32[16,1,4096]{2,1,0:T(1,128)S(1)}, u32[]{:S(2)}, u32[]{:S(2)}) %all-to-all-start.4) | async-done | bytes 262176 | tf_op jit(solution)/shard_map/all_to_all | solution.py:278
  210.8 0.6 gather_fusion.4
  211.4 15.3 %fusion.2 = bf16[1792,512]{1,0:T(8,128)(2,1)} fusion(bf16[4096,1792]{1,0:T(8,128)(2,1)} %bitcast.102, f32[4096,512]{1,0:T(8,128)} %get-tuple-element.66, bf16[4096,512]{1,0:T(8,128)(2,1)} %shard_map.57, f32[4096]{0:T(1024)S(1)} %bitcast.120, f32[4096]{0:T(1024)S(1)} %bitcast.111, f32[4096]{0:T(1024)S(1)} %bitcast.109, f32[4096]{0:T(1024)S(1)} %bitcast.119), kind=kOutput, calls=%fused_computation.12 | convolution fusion | flops 7538081792 | bytes 29163520 | tf_op jit(solution)/shard_map/dot_general | solution.py:323
  (66 shorter events, 1.5 us)
Async XLA Ops:
  0.9 11.4 %collective-permute-start = (bf16[32,1792]{1,0:T(8,128)(2,1)S(1)}, bf16[32,1792]{1,0:T(8,128)(2,1)S(1)}, u32[]{:S(2)}, u32[]{:S(2)}) collective-permute-start(bf16[32,1792]{1,0:T(8,128)(2,1)S(1)} %get-tuple-element.76), channel_id=1, source_target_pairs={{0,16},{8,24},{16,32},{24,40},{32,48},{40,56},{48,64},{56,72},{64,... | collective-permute-start | bytes 344072 | tf_op jit(solution)/shard_map/ppermute | solution.py:32
  3.5 8.9 %collective-permute-start.4 = (bf16[32,1792]{1,0:T(8,128)(2,1)S(1)}, bf16[32,1792]{1,0:T(8,128)(2,1)S(1)}, u32[]{:S(2)}, u32[]{:S(2)}) collective-permute-start(bf16[32,1792]{1,0:T(8,128)(2,1)S(1)} %get-tuple-element.76), channel_id=1, source_target_pairs={{0,112},{8,120},{16,0},{24,8},{32,16},{40,24},{48,32},{56,40},{64,... | collective-permute-start | bytes 344072 | tf_op jit(solution)/shard_map/ppermute | solution.py:32
  7.5 40.2 %copy-start.1 = (s32[4096]{0:T(1024)S(1)}, s32[4096]{0:T(1024)}, u32[]{:S(2)}) copy-start(s32[4096]{0:T(1024)} %param.8) | copy-start | bytes 49156
  12.3 83.7 %copy-start = (bf16[1792,512]{1,0:T(8,128)(2,1)S(1)}, bf16[1792,512]{1,0:T(8,128)(2,1)}, u32[]{:S(2)}) copy-start(bf16[1792,512]{1,0:T(8,128)(2,1)} %refs_12_.3) | copy-start | bytes 5505028
  12.3 4.9 %collective-permute-start.1 = (bf16[32,1792]{1,0:T(8,128)(2,1)S(1)}, bf16[32,1792]{1,0:T(8,128)(2,1)S(1)}, u32[]{:S(2)}, u32[]{:S(2)}) collective-permute-start(bf16[32,1792]{1,0:T(8,128)(2,1)S(1)} %collective-permute-done), channel_id=1, source_target_pairs={{0,16},{8,24},{16,32},{24,40},{32,48},{40,56},{48,64},{56,72},{64,... | collective-permute-start | bytes 344072 | tf_op jit(solution)/shard_map/ppermute | solution.py:32
  12.4 4.8 %collective-permute-start.5 = (bf16[32,1792]{1,0:T(8,128)(2,1)S(1)}, bf16[32,1792]{1,0:T(8,128)(2,1)S(1)}, u32[]{:S(2)}, u32[]{:S(2)}) collective-permute-start(bf16[32,1792]{1,0:T(8,128)(2,1)S(1)} %collective-permute-done.4), channel_id=1, source_target_pairs={{0,112},{8,120},{16,0},{24,8},{32,16},{40,24},{48,32},{56,40},{64,... | collective-permute-start | bytes 344072 | tf_op jit(solution)/shard_map/ppermute | solution.py:32
  17.2 4.9 %collective-permute-start.2 = (bf16[32,1792]{1,0:T(8,128)(2,1)S(1)}, bf16[32,1792]{1,0:T(8,128)(2,1)S(1)}, u32[]{:S(2)}, u32[]{:S(2)}) collective-permute-start(bf16[32,1792]{1,0:T(8,128)(2,1)S(1)} %collective-permute-done.1), channel_id=1, source_target_pairs={{0,16},{8,24},{16,32},{24,40},{32,48},{40,56},{48,64},{56,72},{64,... | collective-permute-start | bytes 344072 | tf_op jit(solution)/shard_map/ppermute | solution.py:32
  17.2 9.7 %collective-permute-start.6 = (bf16[32,1792]{1,0:T(8,128)(2,1)S(1)}, bf16[32,1792]{1,0:T(8,128)(2,1)S(1)}, u32[]{:S(2)}, u32[]{:S(2)}) collective-permute-start(bf16[32,1792]{1,0:T(8,128)(2,1)S(1)} %collective-permute-done.5), channel_id=1, source_target_pairs={{0,112},{8,120},{16,0},{24,8},{32,16},{40,24},{48,32},{56,40},{64,... | collective-permute-start | bytes 344072 | tf_op jit(solution)/shard_map/ppermute | solution.py:32
  22.0 4.9 %collective-permute-start.3 = (bf16[32,1792]{1,0:T(8,128)(2,1)S(1)}, bf16[32,1792]{1,0:T(8,128)(2,1)S(1)}, u32[]{:S(2)}, u32[]{:S(2)}) collective-permute-start(bf16[32,1792]{1,0:T(8,128)(2,1)S(1)} %collective-permute-done.2), channel_id=1, source_target_pairs={{0,16},{8,24},{16,32},{24,40},{32,48},{40,56},{48,64},{56,72},{64,... | collective-permute-start | bytes 344072 | tf_op jit(solution)/shard_map/ppermute | solution.py:32
  27.0 106.0 %all-to-all-start = ((bf16[32,128,512]{2,1,0:T(8,128)(2,1)}), bf16[32,128,512]{2,1,0:T(8,128)(2,1)}, u32[]{:S(2)}, u32[]{:S(2)}) async-start(bf16[32,128,512]{2,1,0:T(8,128)(2,1)} %bitcast.101), calls=%async_computation | async-start | bytes 8388608 | tf_op jit(solution)/shard_map/all_to_all | solution.py:294
  38.3 26.3 %collective-permute-start.10 = (bf16[8,32,1792]{2,1,0:T(8,128)(2,1)S(1)}, bf16[8,32,1792]{2,1,0:T(8,128)(2,1)}, u32[]{:S(2)}, u32[]{:S(2)}) collective-permute-start(bf16[8,32,1792]{2,1,0:T(8,128)(2,1)S(1)} %bitcast_dynamic-update-slice_fusion.refs_1_), channel_id=1, source_target_pairs={{0,129},{8,137},{16,145},{24,153},{32,161},{40,169},{48,177},{56,1... | collective-permute-start | bytes 2752520 | tf_op jit(solution)/shard_map/ppermute | solution.py:55
  41.0 23.5 %collective-permute-start.7 = (bf16[8,32,1792]{2,1,0:T(8,128)(2,1)S(1)}, bf16[8,32,1792]{2,1,0:T(8,128)(2,1)}, u32[]{:S(2)}, u32[]{:S(2)}) collective-permute-start(bf16[8,32,1792]{2,1,0:T(8,128)(2,1)S(1)} %bitcast_dynamic-update-slice_fusion.refs_1_), channel_id=1, source_target_pairs={{0,2},{8,10},{16,18},{24,26},{32,34},{40,42},{48,50},{56,58},{64,6... | collective-permute-start | bytes 2752520 | tf_op jit(solution)/shard_map/ppermute | solution.py:32
  43.3 11.4 %collective-permute-start.8 = (bf16[4,32,1792]{2,1,0:T(8,128)(2,1)}, bf16[4,32,1792]{2,1,0:T(8,128)(2,1)}, u32[]{:S(2)}, u32[]{:S(2)}) collective-permute-start(bf16[4,32,1792]{2,1,0:T(8,128)(2,1)} %get-tuple-element.78), channel_id=1, source_target_pairs={{0,6},{8,14},{16,22},{24,30},{32,38},{40,46},{48,54},{56,62},{64,7... | collective-permute-start | bytes 1376264 | tf_op jit(solution)/shard_map/ppermute | solution.py:32
  44.8 19.8 %collective-permute-start.9 = (bf16[4,32,1792]{2,1,0:T(8,128)(2,1)}, bf16[4,32,1792]{2,1,0:T(8,128)(2,1)S(1)}, u32[]{:S(2)}, u32[]{:S(2)}) collective-permute-start(bf16[4,32,1792]{2,1,0:T(8,128)(2,1)} %get-tuple-element.77), channel_id=1, source_target_pairs={{0,6},{8,14},{16,22},{24,30},{32,38},{40,46},{48,54},{56,62},{64,7... | collective-permute-start | bytes 1376264 | tf_op jit(solution)/shard_map/ppermute | solution.py:32
  46.2 23.2 %collective-permute-start.15 = (bf16[8,32,1792]{2,1,0:T(8,128)(2,1)S(1)}, bf16[8,32,1792]{2,1,0:T(8,128)(2,1)}, u32[]{:S(2)}, u32[]{:S(2)}) collective-permute-start(bf16[8,32,1792]{2,1,0:T(8,128)(2,1)S(1)} %bitcast_dynamic-update-slice_fusion.refs_1_), channel_id=1, source_target_pairs={{0,8},{8,0},{16,24},{24,16},{32,40},{40,32},{48,56},{56,48},{64,72... | collective-permute-start | bytes 2752520 | tf_op jit(solution)/shard_map/ppermute | solution.py:32
  65.6 11.8 %collective-permute-start.13 = (bf16[4,32,1792]{2,1,0:T(8,128)(2,1)S(1)}, bf16[4,32,1792]{2,1,0:T(8,128)(2,1)S(1)}, u32[]{:S(2)}, u32[]{:S(2)}) collective-permute-start(bf16[4,32,1792]{2,1,0:T(8,128)(2,1)S(1)} %slice.13), channel_id=1, source_target_pairs={{0,2},{8,10},{16,18},{24,26},{32,34},{40,42},{48,50},{56,58},{64,6... | collective-permute-start | bytes 1376264 | tf_op jit(solution)/shard_map/ppermute | solution.py:32
  67.0 23.9 %collective-permute-start.11 = (bf16[8,32,1792]{2,1,0:T(8,128)(2,1)}, bf16[8,32,1792]{2,1,0:T(8,128)(2,1)S(1)}, u32[]{:S(2)}, u32[]{:S(2)}) collective-permute-start(bf16[8,32,1792]{2,1,0:T(8,128)(2,1)} %collective-permute-done.7.refs_0_), channel_id=1, source_target_pairs={{0,129},{8,137},{16,145},{24,153},{32,161},{40,169},{48,177},{56,1... | collective-permute-start | bytes 2752520 | tf_op jit(solution)/shard_map/ppermute | solution.py:55
  67.2 23.7 %collective-permute-start.16 = (bf16[8,32,1792]{2,1,0:T(8,128)(2,1)}, bf16[8,32,1792]{2,1,0:T(8,128)(2,1)S(1)}, u32[]{:S(2)}, u32[]{:S(2)}) collective-permute-start(bf16[8,32,1792]{2,1,0:T(8,128)(2,1)} %collective-permute-done.7.refs_0_), channel_id=1, source_target_pairs={{0,8},{8,0},{16,24},{24,16},{32,40},{40,32},{48,56},{56,48},{64,72... | collective-permute-start | bytes 2752520 | tf_op jit(solution)/shard_map/ppermute | solution.py:32
  69.4 21.6 %collective-permute-start.17 = (bf16[8,32,1792]{2,1,0:T(8,128)(2,1)}, bf16[8,32,1792]{2,1,0:T(8,128)(2,1)S(1)}, u32[]{:S(2)}, u32[]{:S(2)}) collective-permute-start(bf16[8,32,1792]{2,1,0:T(8,128)(2,1)} %collective-permute-done.10.refs_1_), channel_id=1, source_target_pairs={{0,8},{8,0},{16,24},{24,16},{32,40},{40,32},{48,56},{56,48},{64,72... | collective-permute-start | bytes 2752520 | tf_op jit(solution)/shard_map/ppermute | solution.py:32
  69.4 20.2 %collective-permute-start.12 = (bf16[4,32,1792]{2,1,0:T(8,128)(2,1)}, bf16[4,32,1792]{2,1,0:T(8,128)(2,1)S(1)}, u32[]{:S(2)}, u32[]{:S(2)}) collective-permute-start(bf16[4,32,1792]{2,1,0:T(8,128)(2,1)} %collective-permute-done.8.refs_2_), channel_id=1, source_target_pairs={{0,128},{8,136},{16,144},{24,152},{32,160},{40,168},{48,176},{56,1... | collective-permute-start | bytes 1376264 | tf_op jit(solution)/shard_map/ppermute | solution.py:55
  77.4 13.5 %collective-permute-start.14 = (bf16[4,32,1792]{2,1,0:T(8,128)(2,1)S(1)}, bf16[4,32,1792]{2,1,0:T(8,128)(2,1)S(1)}, u32[]{:S(2)}, u32[]{:S(2)}) collective-permute-start(bf16[4,32,1792]{2,1,0:T(8,128)(2,1)S(1)} %collective-permute-done.9.refs_3_), channel_id=1, source_target_pairs={{0,6},{8,14},{16,22},{24,30},{32,38},{40,46},{48,54},{56,62},{64,7... | collective-permute-start | bytes 1376264 | tf_op jit(solution)/shard_map/ppermute | solution.py:32
  89.5 3.6 %collective-permute-start.18 = (bf16[4,32,1792]{2,1,0:T(8,128)(2,1)}, bf16[4,32,1792]{2,1,0:T(8,128)(2,1)S(1)}, u32[]{:S(2)}, u32[]{:S(2)}) collective-permute-start(bf16[4,32,1792]{2,1,0:T(8,128)(2,1)} %collective-permute-done.8.refs_2_), channel_id=1, source_target_pairs={{0,8},{8,0},{16,24},{24,16},{32,40},{40,32},{48,56},{56,48},{64,72... | collective-permute-start | bytes 1376264 | tf_op jit(solution)/shard_map/ppermute | solution.py:32
  90.9 4.9 %collective-permute-start.19 = (bf16[4,32,1792]{2,1,0:T(8,128)(2,1)S(1)}, bf16[4,32,1792]{2,1,0:T(8,128)(2,1)S(1)}, u32[]{:S(2)}, u32[]{:S(2)}) collective-permute-start(bf16[4,32,1792]{2,1,0:T(8,128)(2,1)S(1)} %collective-permute-done.9.refs_3_), channel_id=1, source_target_pairs={{0,8},{8,0},{16,24},{24,16},{32,40},{40,32},{48,56},{56,48},{64,72... | collective-permute-start | bytes 1376264 | tf_op jit(solution)/shard_map/ppermute | solution.py:32
  91.0 5.0 %collective-permute-start.20 = (bf16[4,32,1792]{2,1,0:T(8,128)(2,1)S(1)}, bf16[4,32,1792]{2,1,0:T(8,128)(2,1)S(1)}, u32[]{:S(2)}, u32[]{:S(2)}) collective-permute-start(bf16[4,32,1792]{2,1,0:T(8,128)(2,1)S(1)} %collective-permute-done.13.refs_4_), channel_id=1, source_target_pairs={{0,8},{8,0},{16,24},{24,16},{32,40},{40,32},{48,56},{56,48},{64,72... | collective-permute-start | bytes 1376264 | tf_op jit(solution)/shard_map/ppermute | solution.py:32
  91.5 4.4 %collective-permute-start.21 = (bf16[4,32,1792]{2,1,0:T(8,128)(2,1)S(1)}, bf16[4,32,1792]{2,1,0:T(8,128)(2,1)S(1)}, u32[]{:S(2)}, u32[]{:S(2)}) collective-permute-start(bf16[4,32,1792]{2,1,0:T(8,128)(2,1)S(1)} %collective-permute-done.14.refs_5_), channel_id=1, source_target_pairs={{0,8},{8,0},{16,24},{24,16},{32,40},{40,32},{48,56},{56,48},{64,72... | collective-permute-start | bytes 1376264 | tf_op jit(solution)/shard_map/ppermute | solution.py:32
  91.6 19.6 %collective-permute-start.22 = (bf16[4,32,1792]{2,1,0:T(8,128)(2,1)S(1)}, bf16[4,32,1792]{2,1,0:T(8,128)(2,1)S(1)}, u32[]{:S(2)}, u32[]{:S(2)}) collective-permute-start(bf16[4,32,1792]{2,1,0:T(8,128)(2,1)S(1)} %collective-permute-done.9.refs_3_), channel_id=1, source_target_pairs={{0,128},{8,136},{16,144},{24,152},{32,160},{40,168},{48,176},{56,1... | collective-permute-start | bytes 1376264 | tf_op jit(solution)/shard_map/ppermute | solution.py:55
  93.2 18.1 %collective-permute-start.23 = (bf16[4,32,1792]{2,1,0:T(8,128)(2,1)S(1)}, bf16[4,32,1792]{2,1,0:T(8,128)(2,1)S(1)}, u32[]{:S(2)}, u32[]{:S(2)}) collective-permute-start(bf16[4,32,1792]{2,1,0:T(8,128)(2,1)S(1)} %collective-permute-done.13.refs_4_), channel_id=1, source_target_pairs={{0,129},{8,137},{16,145},{24,153},{32,161},{40,169},{48,177},{56,1... | collective-permute-start | bytes 1376264 | tf_op jit(solution)/shard_map/ppermute | solution.py:55
  95.9 20.1 %collective-permute-start.24 = (bf16[4,32,1792]{2,1,0:T(8,128)(2,1)S(1)}, bf16[4,32,1792]{2,1,0:T(8,128)(2,1)S(1)}, u32[]{:S(2)}, u32[]{:S(2)}) collective-permute-start(bf16[4,32,1792]{2,1,0:T(8,128)(2,1)S(1)} %collective-permute-done.14.refs_5_), channel_id=1, source_target_pairs={{0,129},{8,137},{16,145},{24,153},{32,161},{40,169},{48,177},{56,1... | collective-permute-start | bytes 1376264 | tf_op jit(solution)/shard_map/ppermute | solution.py:55
  116.0 5.9 %collective-permute-start.25 = (bf16[8,32,1792]{2,1,0:T(8,128)(2,1)S(1)}, bf16[8,32,1792]{2,1,0:T(8,128)(2,1)S(1)}, u32[]{:S(2)}, u32[]{:S(2)}) collective-permute-start(bf16[8,32,1792]{2,1,0:T(8,128)(2,1)S(1)} %collective-permute-done.11.refs_0_), channel_id=1, source_target_pairs={{0,8},{8,0},{16,24},{24,16},{32,40},{40,32},{48,56},{56,48},{64,72... | collective-permute-start | bytes 2752520 | tf_op jit(solution)/shard_map/ppermute | solution.py:32
  117.2 2.8 %collective-permute-start.26 = (bf16[4,32,1792]{2,1,0:T(8,128)(2,1)S(1)}, bf16[4,32,1792]{2,1,0:T(8,128)(2,1)S(1)}, u32[]{:S(2)}, u32[]{:S(2)}) collective-permute-start(bf16[4,32,1792]{2,1,0:T(8,128)(2,1)S(1)} %collective-permute-done.12.refs_2_), channel_id=1, source_target_pairs={{0,8},{8,0},{16,24},{24,16},{32,40},{40,32},{48,56},{56,48},{64,72... | collective-permute-start | bytes 1376264 | tf_op jit(solution)/shard_map/ppermute | solution.py:32
  117.2 3.4 %collective-permute-start.27 = (bf16[4,32,1792]{2,1,0:T(8,128)(2,1)S(1)}, bf16[4,32,1792]{2,1,0:T(8,128)(2,1)S(1)}, u32[]{:S(2)}, u32[]{:S(2)}) collective-permute-start(bf16[4,32,1792]{2,1,0:T(8,128)(2,1)S(1)} %collective-permute-done.22.refs_3_), channel_id=1, source_target_pairs={{0,8},{8,0},{16,24},{24,16},{32,40},{40,32},{48,56},{56,48},{64,72... | collective-permute-start | bytes 1376264 | tf_op jit(solution)/shard_map/ppermute | solution.py:32
  117.7 3.6 %collective-permute-start.28 = (bf16[4,32,1792]{2,1,0:T(8,128)(2,1)S(1)}, bf16[4,32,1792]{2,1,0:T(8,128)(2,1)S(1)}, u32[]{:S(2)}, u32[]{:S(2)}) collective-permute-start(bf16[4,32,1792]{2,1,0:T(8,128)(2,1)S(1)} %collective-permute-done.23.refs_4_), channel_id=1, source_target_pairs={{0,8},{8,0},{16,24},{24,16},{32,40},{40,32},{48,56},{56,48},{64,72... | collective-permute-start | bytes 1376264 | tf_op jit(solution)/shard_map/ppermute | solution.py:32
  117.7 4.2 %collective-permute-start.29 = (bf16[4,32,1792]{2,1,0:T(8,128)(2,1)S(1)}, bf16[4,32,1792]{2,1,0:T(8,128)(2,1)S(1)}, u32[]{:S(2)}, u32[]{:S(2)}) collective-permute-start(bf16[4,32,1792]{2,1,0:T(8,128)(2,1)S(1)} %collective-permute-done.24.refs_5_), channel_id=1, source_target_pairs={{0,8},{8,0},{16,24},{24,16},{32,40},{40,32},{48,56},{56,48},{64,72... | collective-permute-start | bytes 1376264 | tf_op jit(solution)/shard_map/ppermute | solution.py:32
  133.8 20.7 %all-to-all-start.1 = ((f32[16,1,4096]{2,1,0:T(1,128)}), f32[16,1,4096]{2,1,0:T(1,128)S(1)}, u32[]{:S(2)}, u32[]{:S(2)}) async-start(f32[16,1,4096]{2,1,0:T(1,128)} %broadcast_in_dim.22), calls=%async_computation.1 | async-start | bytes 524288 | tf_op jit(solution)/shard_map/all_to_all | solution.py:278
  152.8 32.8 %copy-start.2 = (s32[32]{0:T(128)S(1)}, s32[32]{0:T(128)}, u32[]{:S(2)}) copy-start(s32[32]{0:T(128)} %param.9) | copy-start | bytes 388
  179.1 18.1 %all-to-all-start.3 = ((f32[16,1,4096]{2,1,0:T(1,128)}), f32[16,1,4096]{2,1,0:T(1,128)S(1)}, u32[]{:S(2)}, u32[]{:S(2)}) async-start(f32[16,1,4096]{2,1,0:T(1,128)} %broadcast_in_dim.26), calls=%async_computation.3 | async-start | bytes 524288 | tf_op jit(solution)/shard_map/all_to_all | solution.py:278
  198.4 12.2 %all-to-all-start.4 = ((f32[16,1,4096]{2,1,0:T(1,128)}), f32[16,1,4096]{2,1,0:T(1,128)S(1)}, u32[]{:S(2)}, u32[]{:S(2)}) async-start(f32[16,1,4096]{2,1,0:T(1,128)} %broadcast_in_dim.27), calls=%async_computation.4 | async-start | bytes 524288 | tf_op jit(solution)/shard_map/all_to_all | solution.py:278

commit v4 on v3

--- a/solution.py
+++ b/solution.py
@@ -40,8 +40,9 @@
     for step in range(1, 4):
         up.append(hop(up[-1], dz=1))
         down.append(hop(down[-1], dz=-1))
-    up.append(hop(up[-1], dz=1))
-    return jnp.stack([*up, down[3], down[2], down[1]])
+    half = rows // 2
+    opposite = jnp.concatenate([hop(up[2][:half], dz=2), hop(down[2][half:], dz=-2)])
+    return jnp.stack([*up, opposite, down[3], down[2], down[1]])
 
 
 def cross(array, near):

time: 227 us -> 226 us (level)
  waiting for transfers between devices: 79 us -> 74.8 us
  starting transfers between devices: 63.1 us -> 65.9 us
    ppermute x24 -> x25, waiting for transfers between devices: 38.1 us -> 34 us  [hop(): return lax.ppermute(array, AXES, pairs)]
    ppermute x24 -> x25, starting transfers between devices: 27 us -> 30.5 us  [hop(): return lax.ppermute(array, AXES, pairs)]
  transfers between devices with their start and end apart: 34 -> 35, of which waited for: 18 -> 18; matrix products, arithmetic and copies ran while one was open for 4% -> 4% of each run, Pallas kernels for 14% -> 14%
where the time goes in v4:
time: 226 us
  waiting for transfers between devices  74.8 us (33%)
  starting transfers between devices  65.9 us (29%)
  Pallas kernels  30.8 us (14%)
  matrix products  15.3 us (7%)
  blocking collectives  14.5 us (6%)
  local copies, waits for them, and re-layouts  14.3 us (6%)
  other arithmetic  8.73 us (4%)
    ppermute x25, waiting for transfers between devices, hop(): return lax.ppermute(array, AXES, pairs)  34 us
    ppermute x25, starting transfers between devices, hop(): return lax.ppermute(array, AXES, pairs)  30.5 us
    pallas_call x2, Pallas kernels, block_logits(): pl.pallas_call(functools.partial(logits_kernel, column), grid_spec=pltpu....  21 us
    ppermute x6, waiting for transfers between devices, cross(): return lax.ppermute(array, AXES, pairs)  20.4 us
    all_to_all x3, waiting for transfers between devices, from_members(): lax.all_to_all(copies, AXES, split_axis=0, concat_axis=0, tiled=True, axi...  20 us
    all_to_all x3, starting transfers between devices, from_members(): lax.all_to_all(copies, AXES, split_axis=0, concat_axis=0, tiled=True, axi...  19 us
    dot_general x1, matrix products, per_device(): lax.dot_general(gathered, dlogits, (((0,), (0,)), ((), ())), preferred_el...  15.3 us
    all_to_all x1, blocking collectives, from_members(): lax.all_to_all(copies, AXES, split_axis=0, concat_axis=0, tiled=True, axi...  14.5 us
  transfers between devices with their start and end apart: 35, of which 18 were waited for; matrix products, arithmetic and copies ran while one was open for 4% of the time, Pallas kernels for 14%

profile of v4, /device:TPU:1, one launch (start us, length us, event | category | flops | bytes accessed | tf_op | source)
XLA Modules:
  0.0 225.5 jit_solution(15222291884363829237)
XLA Ops:
  0.0 0.9 bitcast_dynamic-update-slice_fusion.6
  0.9 2.5 %collective-permute-start = (bf16[32,1792]{1,0:T(8,128)(2,1)S(1)}, bf16[32,1792]{1,0:T(8,128)(2,1)S(1)}, u32[]{:S(2)}, u32[]{:S(2)}) collective-permute-start(bf16[32,1792]{1,0:T(8,128)(2,1)S(1)} %get-tuple-element.76), channel_id=1, source_target_pairs={{0,16},{8,24},{16,32},{24,40},{32,48},{40,56},{48,64},{56,72},{64,... | collective-permute-start | bytes 344072 | tf_op jit(solution)/shard_map/ppermute | solution.py:32
  3.5 4.0 %collective-permute-start.4 = (bf16[32,1792]{1,0:T(8,128)(2,1)S(1)}, bf16[32,1792]{1,0:T(8,128)(2,1)S(1)}, u32[]{:S(2)}, u32[]{:S(2)}) collective-permute-start(bf16[32,1792]{1,0:T(8,128)(2,1)S(1)} %get-tuple-element.76), channel_id=1, source_target_pairs={{0,112},{8,120},{16,0},{24,8},{32,16},{40,24},{48,32},{56,40},{64,... | collective-permute-start | bytes 344072 | tf_op jit(solution)/shard_map/ppermute | solution.py:32
  7.5 4.8 %copy.32 = bf16[16,32,8,512]{3,2,0,1:T(8,128)(2,1)} copy(bf16[16,32,8,512]{3,2,1,0:T(8,128)(2,1)} %bitcast.105) | data formatting | bytes 8388608 | tf_op jit(solution)/shard_map/reshape | solution.py:291
  12.4 2.7 %collective-permute-start.5 = (bf16[32,1792]{1,0:T(8,128)(2,1)S(1)}, bf16[32,1792]{1,0:T(8,128)(2,1)S(1)}, u32[]{:S(2)}, u32[]{:S(2)}) collective-permute-start(bf16[32,1792]{1,0:T(8,128)(2,1)S(1)} %collective-permute-done.4), channel_id=1, source_target_pairs={{0,112},{8,120},{16,0},{24,8},{32,16},{40,24},{48,32},{56,40},{64,... | collective-permute-start | bytes 344072 | tf_op jit(solution)/shard_map/ppermute | solution.py:32
  15.0 2.2 collective-permute-done.1
  17.2 3.6 %collective-permute-start.6 = (bf16[16,1792]{1,0:T(8,128)(2,1)S(1)}, bf16[16,1792]{1,0:T(8,128)(2,1)S(1)}, u32[]{:S(2)}, u32[]{:S(2)}) collective-permute-start(bf16[16,1792]{1,0:T(8,128)(2,1)S(1)} %slice.33), channel_id=1, source_target_pairs={{0,96},{8,104},{16,112},{24,120},{32,0},{40,8},{48,16},{56,24},{64... | collective-permute-start | bytes 172040 | tf_op jit(solution)/shard_map/ppermute | solution.py:32
  20.9 0.2 collective-permute-start.2
  21.1 2.5 %collective-permute-start.7 = (bf16[32,1792]{1,0:T(8,128)(2,1)S(1)}, bf16[32,1792]{1,0:T(8,128)(2,1)S(1)}, u32[]{:S(2)}, u32[]{:S(2)}) collective-permute-start(bf16[32,1792]{1,0:T(8,128)(2,1)S(1)} %collective-permute-done.5), channel_id=1, source_target_pairs={{0,112},{8,120},{16,0},{24,8},{32,16},{40,24},{48,32},{56,40},{64,... | collective-permute-start | bytes 344072 | tf_op jit(solution)/shard_map/ppermute | solution.py:32
  23.6 2.7 %collective-permute-done.2 = bf16[32,1792]{1,0:T(8,128)(2,1)S(1)} collective-permute-done((bf16[32,1792]{1,0:T(8,128)(2,1)S(1)}, bf16[32,1792]{1,0:T(8,128)(2,1)S(1)}, u32[]{:S(2)}, u32[]{:S(2)}) %collective-permute-start.2) | collective-permute-done | bytes 114720 | tf_op jit(solution)/shard_map/ppermute | solution.py:32
  26.6 10.5 %all-to-all-start = ((bf16[32,128,512]{2,1,0:T(8,128)(2,1)}), bf16[32,128,512]{2,1,0:T(8,128)(2,1)}, u32[]{:S(2)}, u32[]{:S(2)}) async-start(bf16[32,128,512]{2,1,0:T(8,128)(2,1)} %bitcast.103), calls=%async_computation | async-start | bytes 8388608 | tf_op jit(solution)/shard_map/all_to_all | solution.py:295
  37.1 2.7 %collective-permute-start.11 = (bf16[8,32,1792]{2,1,0:T(8,128)(2,1)S(1)}, bf16[8,32,1792]{2,1,0:T(8,128)(2,1)}, u32[]{:S(2)}, u32[]{:S(2)}) collective-permute-start(bf16[8,32,1792]{2,1,0:T(8,128)(2,1)S(1)} %bitcast_dynamic-update-slice_fusion.refs_1_), channel_id=1, source_target_pairs={{0,129},{8,137},{16,145},{24,153},{32,161},{40,169},{48,177},{56,1... | collective-permute-start | bytes 2752520 | tf_op jit(solution)/shard_map/ppermute | solution.py:56
  39.8 1.3 collective-permute-start.8
  41.1 1.0 fusion.9
  42.1 1.4 collective-permute-start.10
  43.5 1.5 collective-permute-start.9
  45.0 1.5 collective-permute-start.16
  46.7 0.6 gather_fusion
  47.3 6.2 %collective-permute-done.10.refs_3_ = bf16[4,32,1792]{2,1,0:T(8,128)(2,1)S(1)} collective-permute-done((bf16[4,32,1792]{2,1,0:T(8,128)(2,1)}, bf16[4,32,1792]{2,1,0:T(8,128)(2,1)S(1)}, u32[]{:S(2)}, u32[]{:S(2)}) %collective-permute-start.10) | collective-permute-done | bytes 458784 | tf_op jit(solution)/shard_map/ppermute | solution.py:32
  53.5 9.8 %collective-permute-done.9.refs_2_ = bf16[4,32,1792]{2,1,0:T(8,128)(2,1)} collective-permute-done((bf16[4,32,1792]{2,1,0:T(8,128)(2,1)}, bf16[4,32,1792]{2,1,0:T(8,128)(2,1)}, u32[]{:S(2)}, u32[]{:S(2)}) %collective-permute-start.9) | collective-permute-done | bytes 458784 | tf_op jit(solution)/shard_map/ppermute | solution.py:32
  63.3 1.1 slice.21
  64.4 1.4 collective-permute-start.14
  65.8 0.2 collective-permute-start.12
  66.0 2.2 collective-permute-start.17
  68.4 7.7 %collective-permute-done.14.refs_4_ = bf16[4,32,1792]{2,1,0:T(8,128)(2,1)S(1)} collective-permute-done((bf16[4,32,1792]{2,1,0:T(8,128)(2,1)S(1)}, bf16[4,32,1792]{2,1,0:T(8,128)(2,1)S(1)}, u32[]{:S(2)}, u32[]{:S(2)}) %collective-permute-start.14) | collective-permute-done | bytes 458784 | tf_op jit(solution)/shard_map/ppermute | solution.py:32
  76.1 1.5 collective-permute-start.15
  77.5 10.9 %collective-permute-done.13.refs_2_ = bf16[4,32,1792]{2,1,0:T(8,128)(2,1)S(1)} collective-permute-done((bf16[4,32,1792]{2,1,0:T(8,128)(2,1)}, bf16[4,32,1792]{2,1,0:T(8,128)(2,1)S(1)}, u32[]{:S(2)}, u32[]{:S(2)}) %collective-permute-start.13) | collective-permute-done | bytes 458784 | tf_op jit(solution)/shard_map/ppermute | solution.py:56
  88.4 1.4 collective-permute-start.19
  89.8 0.6 collective-permute-start.21
  90.5 1.5 collective-permute-done.19.refs_8_
  92.0 2.8 %collective-permute-start.24 = (bf16[4,32,1792]{2,1,0:T(8,128)(2,1)S(1)}, bf16[4,32,1792]{2,1,0:T(8,128)(2,1)S(1)}, u32[]{:S(2)}, u32[]{:S(2)}) collective-permute-start(bf16[4,32,1792]{2,1,0:T(8,128)(2,1)S(1)} %collective-permute-done.14.refs_4_), channel_id=1, source_target_pairs={{0,129},{8,137},{16,145},{24,153},{32,161},{40,169},{48,177},{56,1... | collective-permute-start | bytes 1376264 | tf_op jit(solution)/shard_map/ppermute | solution.py:56
  94.9 10.5 %shard_map.55 = (bf16[4,4,256,1792]{3,2,1,0:T(8,128)(2,1)}, f32[4096,512]{1,0:T(8,128)}, f32[16,1,256]{2,1,0:T(1,128)S(1)}, f32[16,1,256]{2,1,0:T(1,128)S(1)}) custom-call(s32[4]{0:T(128)S(1)} %pad_add_fusion.place, bf16[8,32,1792]{2,1,0:T(8,128)(2,1)} %collective-permute-done.8.refs_0_, bf16[8,32,1792]{2,1,0:T(8,128)(2,1)S(1)} %bitcast_dynamic-update-slice_fusion.refs_1_, ...), custom_call_target="tpu_custom_call" | custom-call | flops 3758096384 | bytes 20709376 | tf_op jit(solution)/shard_map/pallas_call | solution.py:176
  105.5 4.6 %collective-permute-done.23.refs_3_ = bf16[4,32,1792]{2,1,0:T(8,128)(2,1)S(1)} collective-permute-done((bf16[4,32,1792]{2,1,0:T(8,128)(2,1)S(1)}, bf16[4,32,1792]{2,1,0:T(8,128)(2,1)S(1)}, u32[]{:S(2)}, u32[]{:S(2)}) %collective-permute-start.23) | collective-permute-done | bytes 458784 | tf_op jit(solution)/shard_map/ppermute | solution.py:56
  110.0 5.0 %collective-permute-done.25.refs_5_ = bf16[4,32,1792]{2,1,0:T(8,128)(2,1)S(1)} collective-permute-done((bf16[4,32,1792]{2,1,0:T(8,128)(2,1)S(1)}, bf16[4,32,1792]{2,1,0:T(8,128)(2,1)S(1)}, u32[]{:S(2)}, u32[]{:S(2)}) %collective-permute-start.25) | collective-permute-done | bytes 458784 | tf_op jit(solution)/shard_map/ppermute | solution.py:56
  115.0 1.1 collective-permute-start.26
  116.1 0.5 collective-permute-start.28
  116.6 0.5 collective-permute-start.30
  117.1 1.7 collective-permute-done.27.refs_8_
  118.8 0.7 collective-permute-done.28.refs_9_
  119.5 0.7 collective-permute-done.29.refs_10_
  120.2 0.7 collective-permute-done.30.refs_11_
  120.8 10.5 %shard_map.56 = (bf16[4,4,256,1792]{3,2,1,0:T(8,128)(2,1)}, f32[4096,512]{1,0:T(8,128)}, f32[16,1,256]{2,1,0:T(1,128)S(1)}, f32[16,1,256]{2,1,0:T(1,128)S(1)}) custom-call(s32[4]{0:T(128)S(1)} %pad_add_fusion.place, bf16[8,32,1792]{2,1,0:T(8,128)(2,1)S(1)} %collective-permute-done.12.refs_0_, ...), custom_call_target="tpu_custom_call", output_to_operand_aliasing={{0}: (16, {}), {1}: (17, {})} | custom-call | flops 3758096384 | bytes 20709376 | tf_op jit(solution)/shard_map/pallas_call | solution.py:176
  131.3 0.4 all-to-all-done
  131.7 0.9 broadcast_in_dim.22
  132.6 9.1 %all-to-all-start.1 = ((f32[16,1,4096]{2,1,0:T(1,128)}), f32[16,1,4096]{2,1,0:T(1,128)S(1)}, u32[]{:S(2)}, u32[]{:S(2)}) async-start(f32[16,1,4096]{2,1,0:T(1,128)} %broadcast_in_dim.22), calls=%async_computation.1 | async-start | bytes 524288 | tf_op jit(solution)/shard_map/all_to_all | solution.py:279
  141.7 9.9 %shard_map.57 = bf16[4096,512]{1,0:T(8,128)(2,1)} custom-call(s32[4096]{0:T(1024)S(1)} %bitcast.100, bf16[4096,512]{1,0:T(8,128)(2,1)} %bitcast.32.teacher), custom_call_target="tpu_custom_call" | custom-call | bytes 41943040 | tf_op jit(solution)/shard_map/pallas_call | solution.py:249
  151.6 1.8 all-to-all-done.1
  153.7 0.2 broadcast_in_dim.23
  153.9 14.5 %all_to_all.35 = f32[16,1,4096]{2,1,0:T(1,128)S(1)} all-to-all(f32[16,1,4096]{2,1,0:T(1,128)S(1)} %broadcast_in_dim.23), channel_id=1, replica_groups={{0,1,2,3,4,5,6,7,128,129,130,131,132,133,134,135},{8,9,10,11,12,13,14,1..., dimensions={0} | all-to-all | bytes 524288 | tf_op jit(solution)/shard_map/all_to_all | solution.py:279
  168.4 0.2 reduce_max.19
  168.5 0.2 fusion.4
  168.8 0.6 gather_fusion.2
  169.4 7.0 %multiply_reduce_fusion = f32[4096]{0:T(1024)S(1)} fusion(f32[4096,512]{1,0:T(8,128)} %get-tuple-element.66, bf16[4096,512]{1,0:T(8,128)(2,1)} %shard_map.57, f32[4096]{0:T(1024)S(1)} %bitcast.112, f32[4096]{0:T(1024)S(1)} %bitcast.110), kind=kLoop, calls=%fused_computation.6 | loop fusion | flops 16773120 | bytes 12632064 | tf_op jit(solution)/shard_map/reduce_sum | solution.py:312
  176.5 0.6 gather_fusion.3
  177.1 0.9 broadcast_in_dim.26
  178.0 6.4 %all-to-all-start.3 = ((f32[16,1,4096]{2,1,0:T(1,128)}), f32[16,1,4096]{2,1,0:T(1,128)S(1)}, u32[]{:S(2)}, u32[]{:S(2)}) async-start(f32[16,1,4096]{2,1,0:T(1,128)} %broadcast_in_dim.26), calls=%async_computation.3 | async-start | bytes 524288 | tf_op jit(solution)/shard_map/all_to_all | solution.py:279
  184.5 11.6 %all-to-all-done.3 = f32[16,1,4096]{2,1,0:T(1,128)S(1)} async-done(((f32[16,1,4096]{2,1,0:T(1,128)}), f32[16,1,4096]{2,1,0:T(1,128)S(1)}, u32[]{:S(2)}, u32[]{:S(2)}) %all-to-all-start.3) | async-done | bytes 262176 | tf_op jit(solution)/shard_map/all_to_all | solution.py:279
  196.3 0.9 broadcast_in_dim.27
  197.2 3.5 %all-to-all-start.4 = ((f32[16,1,4096]{2,1,0:T(1,128)}), f32[16,1,4096]{2,1,0:T(1,128)S(1)}, u32[]{:S(2)}, u32[]{:S(2)}) async-start(f32[16,1,4096]{2,1,0:T(1,128)} %broadcast_in_dim.27), calls=%async_computation.4 | async-start | bytes 524288 | tf_op jit(solution)/shard_map/all_to_all | solution.py:279
  200.8 0.7 reduce_sum.54
  201.5 0.6 gather_fusion.1
  202.8 6.6 %all-to-all-done.4 = f32[16,1,4096]{2,1,0:T(1,128)S(1)} async-done(((f32[16,1,4096]{2,1,0:T(1,128)}), f32[16,1,4096]{2,1,0:T(1,128)S(1)}, u32[]{:S(2)}, u32[]{:S(2)}) %all-to-all-start.4) | async-done | bytes 262176 | tf_op jit(solution)/shard_map/all_to_all | solution.py:279
  209.6 0.6 gather_fusion.4
  210.2 15.3 %fusion.2 = bf16[1792,512]{1,0:T(8,128)(2,1)} fusion(bf16[4096,1792]{1,0:T(8,128)(2,1)} %bitcast.104, f32[4096,512]{1,0:T(8,128)} %get-tuple-element.66, bf16[4096,512]{1,0:T(8,128)(2,1)} %shard_map.57, f32[4096]{0:T(1024)S(1)} %bitcast.122, f32[4096]{0:T(1024)S(1)} %bitcast.113, f32[4096]{0:T(1024)S(1)} %bitcast.111, f32[4096]{0:T(1024)S(1)} %bitcast.121), kind=kOutput, calls=%fused_computation.12 | convolution fusion | flops 7538081792 | bytes 29163520 | tf_op jit(solution)/shard_map/dot_general | solution.py:324
  (70 shorter events, 1.8 us)
Async XLA Ops:
  0.9 11.4 %collective-permute-start = (bf16[32,1792]{1,0:T(8,128)(2,1)S(1)}, bf16[32,1792]{1,0:T(8,128)(2,1)S(1)}, u32[]{:S(2)}, u32[]{:S(2)}) collective-permute-start(bf16[32,1792]{1,0:T(8,128)(2,1)S(1)} %get-tuple-element.76), channel_id=1, source_target_pairs={{0,16},{8,24},{16,32},{24,40},{32,48},{40,56},{48,64},{56,72},{64,... | collective-permute-start | bytes 344072 | tf_op jit(solution)/shard_map/ppermute | solution.py:32
  3.5 8.9 %collective-permute-start.4 = (bf16[32,1792]{1,0:T(8,128)(2,1)S(1)}, bf16[32,1792]{1,0:T(8,128)(2,1)S(1)}, u32[]{:S(2)}, u32[]{:S(2)}) collective-permute-start(bf16[32,1792]{1,0:T(8,128)(2,1)S(1)} %get-tuple-element.76), channel_id=1, source_target_pairs={{0,112},{8,120},{16,0},{24,8},{32,16},{40,24},{48,32},{56,40},{64,... | collective-permute-start | bytes 344072 | tf_op jit(solution)/shard_map/ppermute | solution.py:32
  7.5 39.0 %copy-start.1 = (s32[4096]{0:T(1024)S(1)}, s32[4096]{0:T(1024)}, u32[]{:S(2)}) copy-start(s32[4096]{0:T(1024)} %param.8) | copy-start | bytes 49156
  12.3 82.6 %copy-start = (bf16[1792,512]{1,0:T(8,128)(2,1)S(1)}, bf16[1792,512]{1,0:T(8,128)(2,1)}, u32[]{:S(2)}) copy-start(bf16[1792,512]{1,0:T(8,128)(2,1)} %refs_12_.3) | copy-start | bytes 5505028
  12.3 4.9 %collective-permute-start.1 = (bf16[32,1792]{1,0:T(8,128)(2,1)S(1)}, bf16[32,1792]{1,0:T(8,128)(2,1)S(1)}, u32[]{:S(2)}, u32[]{:S(2)}) collective-permute-start(bf16[32,1792]{1,0:T(8,128)(2,1)S(1)} %collective-permute-done), channel_id=1, source_target_pairs={{0,16},{8,24},{16,32},{24,40},{32,48},{40,56},{48,64},{56,72},{64,... | collective-permute-start | bytes 344072 | tf_op jit(solution)/shard_map/ppermute | solution.py:32
  12.4 4.9 %collective-permute-start.5 = (bf16[32,1792]{1,0:T(8,128)(2,1)S(1)}, bf16[32,1792]{1,0:T(8,128)(2,1)S(1)}, u32[]{:S(2)}, u32[]{:S(2)}) collective-permute-start(bf16[32,1792]{1,0:T(8,128)(2,1)S(1)} %collective-permute-done.4), channel_id=1, source_target_pairs={{0,112},{8,120},{16,0},{24,8},{32,16},{40,24},{48,32},{56,40},{64,... | collective-permute-start | bytes 344072 | tf_op jit(solution)/shard_map/ppermute | solution.py:32
  17.2 9.1 %collective-permute-start.3 = (bf16[16,1792]{1,0:T(8,128)(2,1)S(1)}, bf16[16,1792]{1,0:T(8,128)(2,1)S(1)}, u32[]{:S(2)}, u32[]{:S(2)}) collective-permute-start(bf16[16,1792]{1,0:T(8,128)(2,1)S(1)} %slice.32), channel_id=1, source_target_pairs={{0,32},{8,40},{16,48},{24,56},{32,64},{40,72},{48,80},{56,88},{64,... | collective-permute-start | bytes 172040 | tf_op jit(solution)/shard_map/ppermute | solution.py:32
  17.2 9.1 %collective-permute-start.6 = (bf16[16,1792]{1,0:T(8,128)(2,1)S(1)}, bf16[16,1792]{1,0:T(8,128)(2,1)S(1)}, u32[]{:S(2)}, u32[]{:S(2)}) collective-permute-start(bf16[16,1792]{1,0:T(8,128)(2,1)S(1)} %slice.33), channel_id=1, source_target_pairs={{0,96},{8,104},{16,112},{24,120},{32,0},{40,8},{48,16},{56,24},{64... | collective-permute-start | bytes 172040 | tf_op jit(solution)/shard_map/ppermute | solution.py:32
  20.9 5.4 %collective-permute-start.2 = (bf16[32,1792]{1,0:T(8,128)(2,1)S(1)}, bf16[32,1792]{1,0:T(8,128)(2,1)S(1)}, u32[]{:S(2)}, u32[]{:S(2)}) collective-permute-start(bf16[32,1792]{1,0:T(8,128)(2,1)S(1)} %collective-permute-done.1), channel_id=1, source_target_pairs={{0,16},{8,24},{16,32},{24,40},{32,48},{40,56},{48,64},{56,72},{64,... | collective-permute-start | bytes 344072 | tf_op jit(solution)/shard_map/ppermute | solution.py:32
  21.1 5.4 %collective-permute-start.7 = (bf16[32,1792]{1,0:T(8,128)(2,1)S(1)}, bf16[32,1792]{1,0:T(8,128)(2,1)S(1)}, u32[]{:S(2)}, u32[]{:S(2)}) collective-permute-start(bf16[32,1792]{1,0:T(8,128)(2,1)S(1)} %collective-permute-done.5), channel_id=1, source_target_pairs={{0,112},{8,120},{16,0},{24,8},{32,16},{40,24},{48,32},{56,40},{64,... | collective-permute-start | bytes 344072 | tf_op jit(solution)/shard_map/ppermute | solution.py:32
  26.6 105.1 %all-to-all-start = ((bf16[32,128,512]{2,1,0:T(8,128)(2,1)}), bf16[32,128,512]{2,1,0:T(8,128)(2,1)}, u32[]{:S(2)}, u32[]{:S(2)}) async-start(bf16[32,128,512]{2,1,0:T(8,128)(2,1)} %bitcast.103), calls=%async_computation | async-start | bytes 8388608 | tf_op jit(solution)/shard_map/all_to_all | solution.py:295
  37.1 26.3 %collective-permute-start.11 = (bf16[8,32,1792]{2,1,0:T(8,128)(2,1)S(1)}, bf16[8,32,1792]{2,1,0:T(8,128)(2,1)}, u32[]{:S(2)}, u32[]{:S(2)}) collective-permute-start(bf16[8,32,1792]{2,1,0:T(8,128)(2,1)S(1)} %bitcast_dynamic-update-slice_fusion.refs_1_), channel_id=1, source_target_pairs={{0,129},{8,137},{16,145},{24,153},{32,161},{40,169},{48,177},{56,1... | collective-permute-start | bytes 2752520 | tf_op jit(solution)/shard_map/ppermute | solution.py:56
  39.8 23.5 %collective-permute-start.8 = (bf16[8,32,1792]{2,1,0:T(8,128)(2,1)S(1)}, bf16[8,32,1792]{2,1,0:T(8,128)(2,1)}, u32[]{:S(2)}, u32[]{:S(2)}) collective-permute-start(bf16[8,32,1792]{2,1,0:T(8,128)(2,1)S(1)} %bitcast_dynamic-update-slice_fusion.refs_1_), channel_id=1, source_target_pairs={{0,2},{8,10},{16,18},{24,26},{32,34},{40,42},{48,50},{56,58},{64,6... | collective-permute-start | bytes 2752520 | tf_op jit(solution)/shard_map/ppermute | solution.py:32
  42.1 11.4 %collective-permute-start.10 = (bf16[4,32,1792]{2,1,0:T(8,128)(2,1)}, bf16[4,32,1792]{2,1,0:T(8,128)(2,1)S(1)}, u32[]{:S(2)}, u32[]{:S(2)}) collective-permute-start(bf16[4,32,1792]{2,1,0:T(8,128)(2,1)} %get-tuple-element.77), channel_id=1, source_target_pairs={{0,6},{8,14},{16,22},{24,30},{32,38},{40,46},{48,54},{56,62},{64,7... | collective-permute-start | bytes 1376264 | tf_op jit(solution)/shard_map/ppermute | solution.py:32
  43.5 19.8 %collective-permute-start.9 = (bf16[4,32,1792]{2,1,0:T(8,128)(2,1)}, bf16[4,32,1792]{2,1,0:T(8,128)(2,1)}, u32[]{:S(2)}, u32[]{:S(2)}) collective-permute-start(bf16[4,32,1792]{2,1,0:T(8,128)(2,1)} %get-tuple-element.78), channel_id=1, source_target_pairs={{0,6},{8,14},{16,22},{24,30},{32,38},{40,46},{48,54},{56,62},{64,7... | collective-permute-start | bytes 1376264 | tf_op jit(solution)/shard_map/ppermute | solution.py:32
  45.0 23.3 %collective-permute-start.16 = (bf16[8,32,1792]{2,1,0:T(8,128)(2,1)S(1)}, bf16[8,32,1792]{2,1,0:T(8,128)(2,1)}, u32[]{:S(2)}, u32[]{:S(2)}) collective-permute-start(bf16[8,32,1792]{2,1,0:T(8,128)(2,1)S(1)} %bitcast_dynamic-update-slice_fusion.refs_1_), channel_id=1, source_target_pairs={{0,8},{8,0},{16,24},{24,16},{32,40},{40,32},{48,56},{56,48},{64,72... | collective-permute-start | bytes 2752520 | tf_op jit(solution)/shard_map/ppermute | solution.py:32
  64.4 11.7 %collective-permute-start.14 = (bf16[4,32,1792]{2,1,0:T(8,128)(2,1)S(1)}, bf16[4,32,1792]{2,1,0:T(8,128)(2,1)S(1)}, u32[]{:S(2)}, u32[]{:S(2)}) collective-permute-start(bf16[4,32,1792]{2,1,0:T(8,128)(2,1)S(1)} %slice.21), channel_id=1, source_target_pairs={{0,2},{8,10},{16,18},{24,26},{32,34},{40,42},{48,50},{56,58},{64,6... | collective-permute-start | bytes 1376264 | tf_op jit(solution)/shard_map/ppermute | solution.py:32
  65.8 24.0 %collective-permute-start.12 = (bf16[8,32,1792]{2,1,0:T(8,128)(2,1)}, bf16[8,32,1792]{2,1,0:T(8,128)(2,1)S(1)}, u32[]{:S(2)}, u32[]{:S(2)}) collective-permute-start(bf16[8,32,1792]{2,1,0:T(8,128)(2,1)} %collective-permute-done.8.refs_0_), channel_id=1, source_target_pairs={{0,129},{8,137},{16,145},{24,153},{32,161},{40,169},{48,177},{56,1... | collective-permute-start | bytes 2752520 | tf_op jit(solution)/shard_map/ppermute | solution.py:56
  66.0 23.8 %collective-permute-start.17 = (bf16[8,32,1792]{2,1,0:T(8,128)(2,1)}, bf16[8,32,1792]{2,1,0:T(8,128)(2,1)S(1)}, u32[]{:S(2)}, u32[]{:S(2)}) collective-permute-start(bf16[8,32,1792]{2,1,0:T(8,128)(2,1)} %collective-permute-done.8.refs_0_), channel_id=1, source_target_pairs={{0,8},{8,0},{16,24},{24,16},{32,40},{40,32},{48,56},{56,48},{64,72... | collective-permute-start | bytes 2752520 | tf_op jit(solution)/shard_map/ppermute | solution.py:32
  68.2 21.6 %collective-permute-start.18 = (bf16[8,32,1792]{2,1,0:T(8,128)(2,1)}, bf16[8,32,1792]{2,1,0:T(8,128)(2,1)S(1)}, u32[]{:S(2)}, u32[]{:S(2)}) collective-permute-start(bf16[8,32,1792]{2,1,0:T(8,128)(2,1)} %collective-permute-done.11.refs_1_), channel_id=1, source_target_pairs={{0,8},{8,0},{16,24},{24,16},{32,40},{40,32},{48,56},{56,48},{64,72... | collective-permute-start | bytes 2752520 | tf_op jit(solution)/shard_map/ppermute | solution.py:32
  68.3 20.2 %collective-permute-start.13 = (bf16[4,32,1792]{2,1,0:T(8,128)(2,1)}, bf16[4,32,1792]{2,1,0:T(8,128)(2,1)S(1)}, u32[]{:S(2)}, u32[]{:S(2)}) collective-permute-start(bf16[4,32,1792]{2,1,0:T(8,128)(2,1)} %collective-permute-done.9.refs_2_), channel_id=1, source_target_pairs={{0,128},{8,136},{16,144},{24,152},{32,160},{40,168},{48,176},{56,1... | collective-permute-start | bytes 1376264 | tf_op jit(solution)/shard_map/ppermute | solution.py:56
  76.1 13.7 %collective-permute-start.15 = (bf16[4,32,1792]{2,1,0:T(8,128)(2,1)S(1)}, bf16[4,32,1792]{2,1,0:T(8,128)(2,1)S(1)}, u32[]{:S(2)}, u32[]{:S(2)}) collective-permute-start(bf16[4,32,1792]{2,1,0:T(8,128)(2,1)S(1)} %collective-permute-done.10.refs_3_), channel_id=1, source_target_pairs={{0,6},{8,14},{16,22},{24,30},{32,38},{40,46},{48,54},{56,62},{64,7... | collective-permute-start | bytes 1376264 | tf_op jit(solution)/shard_map/ppermute | solution.py:32
  88.4 3.6 %collective-permute-start.19 = (bf16[4,32,1792]{2,1,0:T(8,128)(2,1)}, bf16[4,32,1792]{2,1,0:T(8,128)(2,1)S(1)}, u32[]{:S(2)}, u32[]{:S(2)}) collective-permute-start(bf16[4,32,1792]{2,1,0:T(8,128)(2,1)} %collective-permute-done.9.refs_2_), channel_id=1, source_target_pairs={{0,8},{8,0},{16,24},{24,16},{32,40},{40,32},{48,56},{56,48},{64,72... | collective-permute-start | bytes 1376264 | tf_op jit(solution)/shard_map/ppermute | solution.py:32
  89.8 5.0 %collective-permute-start.20 = (bf16[4,32,1792]{2,1,0:T(8,128)(2,1)S(1)}, bf16[4,32,1792]{2,1,0:T(8,128)(2,1)S(1)}, u32[]{:S(2)}, u32[]{:S(2)}) collective-permute-start(bf16[4,32,1792]{2,1,0:T(8,128)(2,1)S(1)} %collective-permute-done.10.refs_3_), channel_id=1, source_target_pairs={{0,8},{8,0},{16,24},{24,16},{32,40},{40,32},{48,56},{56,48},{64,72... | collective-permute-start | bytes 1376264 | tf_op jit(solution)/shard_map/ppermute | solution.py:32
  89.8 5.1 %collective-permute-start.21 = (bf16[4,32,1792]{2,1,0:T(8,128)(2,1)S(1)}, bf16[4,32,1792]{2,1,0:T(8,128)(2,1)S(1)}, u32[]{:S(2)}, u32[]{:S(2)}) collective-permute-start(bf16[4,32,1792]{2,1,0:T(8,128)(2,1)S(1)} %collective-permute-done.14.refs_4_), channel_id=1, source_target_pairs={{0,8},{8,0},{16,24},{24,16},{32,40},{40,32},{48,56},{56,48},{64,72... | collective-permute-start | bytes 1376264 | tf_op jit(solution)/shard_map/ppermute | solution.py:32
  90.4 4.5 %collective-permute-start.22 = (bf16[4,32,1792]{2,1,0:T(8,128)(2,1)S(1)}, bf16[4,32,1792]{2,1,0:T(8,128)(2,1)S(1)}, u32[]{:S(2)}, u32[]{:S(2)}) collective-permute-start(bf16[4,32,1792]{2,1,0:T(8,128)(2,1)S(1)} %collective-permute-done.15.refs_5_), channel_id=1, source_target_pairs={{0,8},{8,0},{16,24},{24,16},{32,40},{40,32},{48,56},{56,48},{64,72... | collective-permute-start | bytes 1376264 | tf_op jit(solution)/shard_map/ppermute | solution.py:32
  90.5 19.5 %collective-permute-start.23 = (bf16[4,32,1792]{2,1,0:T(8,128)(2,1)S(1)}, bf16[4,32,1792]{2,1,0:T(8,128)(2,1)S(1)}, u32[]{:S(2)}, u32[]{:S(2)}) collective-permute-start(bf16[4,32,1792]{2,1,0:T(8,128)(2,1)S(1)} %collective-permute-done.10.refs_3_), channel_id=1, source_target_pairs={{0,128},{8,136},{16,144},{24,152},{32,160},{40,168},{48,176},{56,1... | collective-permute-start | bytes 1376264 | tf_op jit(solution)/shard_map/ppermute | solution.py:56
  92.0 18.0 %collective-permute-start.24 = (bf16[4,32,1792]{2,1,0:T(8,128)(2,1)S(1)}, bf16[4,32,1792]{2,1,0:T(8,128)(2,1)S(1)}, u32[]{:S(2)}, u32[]{:S(2)}) collective-permute-start(bf16[4,32,1792]{2,1,0:T(8,128)(2,1)S(1)} %collective-permute-done.14.refs_4_), channel_id=1, source_target_pairs={{0,129},{8,137},{16,145},{24,153},{32,161},{40,169},{48,177},{56,1... | collective-permute-start | bytes 1376264 | tf_op jit(solution)/shard_map/ppermute | solution.py:56
  94.8 20.2 %collective-permute-start.25 = (bf16[4,32,1792]{2,1,0:T(8,128)(2,1)S(1)}, bf16[4,32,1792]{2,1,0:T(8,128)(2,1)S(1)}, u32[]{:S(2)}, u32[]{:S(2)}) collective-permute-start(bf16[4,32,1792]{2,1,0:T(8,128)(2,1)S(1)} %collective-permute-done.15.refs_5_), channel_id=1, source_target_pairs={{0,129},{8,137},{16,145},{24,153},{32,161},{40,169},{48,177},{56,1... | collective-permute-start | bytes 1376264 | tf_op jit(solution)/shard_map/ppermute | solution.py:56
  115.0 5.8 %collective-permute-start.26 = (bf16[8,32,1792]{2,1,0:T(8,128)(2,1)S(1)}, bf16[8,32,1792]{2,1,0:T(8,128)(2,1)S(1)}, u32[]{:S(2)}, u32[]{:S(2)}) collective-permute-start(bf16[8,32,1792]{2,1,0:T(8,128)(2,1)S(1)} %collective-permute-done.12.refs_0_), channel_id=1, source_target_pairs={{0,8},{8,0},{16,24},{24,16},{32,40},{40,32},{48,56},{56,48},{64,72... | collective-permute-start | bytes 2752520 | tf_op jit(solution)/shard_map/ppermute | solution.py:32
  116.1 2.8 %collective-permute-start.27 = (bf16[4,32,1792]{2,1,0:T(8,128)(2,1)S(1)}, bf16[4,32,1792]{2,1,0:T(8,128)(2,1)S(1)}, u32[]{:S(2)}, u32[]{:S(2)}) collective-permute-start(bf16[4,32,1792]{2,1,0:T(8,128)(2,1)S(1)} %collective-permute-done.13.refs_2_), channel_id=1, source_target_pairs={{0,8},{8,0},{16,24},{24,16},{32,40},{40,32},{48,56},{56,48},{64,72... | collective-permute-start | bytes 1376264 | tf_op jit(solution)/shard_map/ppermute | solution.py:32
  116.1 3.4 %collective-permute-start.28 = (bf16[4,32,1792]{2,1,0:T(8,128)(2,1)S(1)}, bf16[4,32,1792]{2,1,0:T(8,128)(2,1)S(1)}, u32[]{:S(2)}, u32[]{:S(2)}) collective-permute-start(bf16[4,32,1792]{2,1,0:T(8,128)(2,1)S(1)} %collective-permute-done.23.refs_3_), channel_id=1, source_target_pairs={{0,8},{8,0},{16,24},{24,16},{32,40},{40,32},{48,56},{56,48},{64,72... | collective-permute-start | bytes 1376264 | tf_op jit(solution)/shard_map/ppermute | solution.py:32
  116.6 3.6 %collective-permute-start.29 = (bf16[4,32,1792]{2,1,0:T(8,128)(2,1)S(1)}, bf16[4,32,1792]{2,1,0:T(8,128)(2,1)S(1)}, u32[]{:S(2)}, u32[]{:S(2)}) collective-permute-start(bf16[4,32,1792]{2,1,0:T(8,128)(2,1)S(1)} %collective-permute-done.24.refs_4_), channel_id=1, source_target_pairs={{0,8},{8,0},{16,24},{24,16},{32,40},{40,32},{48,56},{56,48},{64,72... | collective-permute-start | bytes 1376264 | tf_op jit(solution)/shard_map/ppermute | solution.py:32
  116.6 4.2 %collective-permute-start.30 = (bf16[4,32,1792]{2,1,0:T(8,128)(2,1)S(1)}, bf16[4,32,1792]{2,1,0:T(8,128)(2,1)S(1)}, u32[]{:S(2)}, u32[]{:S(2)}) collective-permute-start(bf16[4,32,1792]{2,1,0:T(8,128)(2,1)S(1)} %collective-permute-done.25.refs_5_), channel_id=1, source_target_pairs={{0,8},{8,0},{16,24},{24,16},{32,40},{40,32},{48,56},{56,48},{64,72... | collective-permute-start | bytes 1376264 | tf_op jit(solution)/shard_map/ppermute | solution.py:32
  132.6 20.8 %all-to-all-start.1 = ((f32[16,1,4096]{2,1,0:T(1,128)}), f32[16,1,4096]{2,1,0:T(1,128)S(1)}, u32[]{:S(2)}, u32[]{:S(2)}) async-start(f32[16,1,4096]{2,1,0:T(1,128)} %broadcast_in_dim.22), calls=%async_computation.1 | async-start | bytes 524288 | tf_op jit(solution)/shard_map/all_to_all | solution.py:279
  151.6 32.8 %copy-start.2 = (s32[32]{0:T(128)S(1)}, s32[32]{0:T(128)}, u32[]{:S(2)}) copy-start(s32[32]{0:T(128)} %param.9) | copy-start | bytes 388
  178.0 18.1 %all-to-all-start.3 = ((f32[16,1,4096]{2,1,0:T(1,128)}), f32[16,1,4096]{2,1,0:T(1,128)S(1)}, u32[]{:S(2)}, u32[]{:S(2)}) async-start(f32[16,1,4096]{2,1,0:T(1,128)} %broadcast_in_dim.26), calls=%async_computation.3 | async-start | bytes 524288 | tf_op jit(solution)/shard_map/all_to_all | solution.py:279
  197.2 12.2 %all-to-all-start.4 = ((f32[16,1,4096]{2,1,0:T(1,128)}), f32[16,1,4096]{2,1,0:T(1,128)S(1)}, u32[]{:S(2)}, u32[]{:S(2)}) async-start(f32[16,1,4096]{2,1,0:T(1,128)} %broadcast_in_dim.27), calls=%async_computation.4 | async-start | bytes 524288 | tf_op jit(solution)/shard_map/all_to_all | solution.py:279
